TPU v7x, 32 devices: a whole 2x2x4 slice. The times are simulated.
32 devices in a mesh: section: 4 (over z), tensor: 8 (over y, x, core).
Axes of the slice: x: 2, y: 2, z: 4, core: 2. Of those that a mesh axis runs over, the one named last changes fastest.
Arguments:
- tokens: bfloat16 [192, 6144], P('tensor', 'section'), may hold values from -6 to 6
- combine: float32 [192, 2], replicated, may hold values from 0.1 to 1
- expert_ids: int32 [192, 2], replicated, may hold values from 0 to 3, as said below
- expert_counts: int32 [4], replicated, may hold values from 0 to 192, as said below
- w_gate: bfloat16 [4, 6144, 16384], P(None, 'section', 'tensor'), may hold values from -0.078125 to 0.078125
- w_up: bfloat16 [4, 6144, 16384], P(None, 'section', 'tensor'), may hold values from -0.078125 to 0.078125
- w_down: bfloat16 [4, 16384, 6144], P(None, 'tensor', 'section'), may hold values from -0.046875 to 0.046875
- cotangent: bfloat16 [192, 6144], P('tensor', 'section'), may hold values from -6 to 6
Outputs:
- layer_out: bfloat16 [192, 6144], P('tensor', 'section')
- d_tokens: bfloat16 [192, 6144], P('tensor', 'section')
- d_down: bfloat16 [4, 16384, 6144], P(None, 'tensor', 'section')
Inputs may be any that keep to these rules, and one draw needn't show every extreme that they name: `expert_ids`: each row names two different experts; one expert, drawn from the seed, is named by every row. expert_counts[e] is the number of entries of expert_ids equal to e.
All inputs are finite; a program needn't handle non-finite values.
Results may differ from a plain program's by a relative error of at most 0.0058.
Values may be sent and summed in bfloat16 or wider, within the bound.
No kernel may reach another device: no remote copies, remote signals or barrier semaphores. Data moves between devices by JAX's collectives and lax.ppermute only.
A program may use at most 320 MiB of HBM per device.

v0:
```python
import jax
import jax.numpy as jnp
from jax import lax
from jax.sharding import PartitionSpec as P

EXPERTS = 4
BLOCK = 128


def route_layout(expert_ids, expert_counts, tokens_total, capacity):
    flat_ids = expert_ids.reshape(-1)
    onehot = (flat_ids[:, None] == jnp.arange(EXPERTS, dtype=jnp.int32)[None, :]).astype(jnp.int32)
    within = jnp.sum((jnp.cumsum(onehot, 0) - onehot) * onehot, 1)
    padded = (expert_counts + BLOCK - 1) // BLOCK * BLOCK
    block_ends = jnp.cumsum(padded)
    block_starts = block_ends - padded
    slot_index = jnp.sum(onehot * block_starts[None, :], 1) + within
    entry_token = jnp.arange(flat_ids.shape[0], dtype=jnp.int32) // 2
    owner_token = jnp.full((capacity,), tokens_total, jnp.int32).at[slot_index].set(entry_token)
    first_rows = jnp.arange(capacity // BLOCK, dtype=jnp.int32) * BLOCK
    block_expert = jnp.minimum(
        jnp.sum((block_ends[None, :] <= first_rows[:, None]).astype(jnp.int32), 1), EXPERTS - 1
    )
    return (slot_index, owner_token, block_expert)


def blocked_product(rows, weights, block_expert, transpose):
    nblocks = block_expert.shape[0]
    blocks = rows.reshape(nblocks, rows.shape[0] // nblocks, rows.shape[1])

    def apply_block(operand):
        segment, expert = operand
        matrix = lax.dynamic_index_in_dim(weights, expert, 0, keepdims=False)
        if transpose:
            return lax.dot_general(
                segment, matrix, (((1,), (1,)), ((), ())), preferred_element_type=jnp.float32
            )
        return jnp.dot(segment, matrix, preferred_element_type=jnp.float32)

    result = lax.map(apply_block, (blocks, block_expert))
    return result.reshape(rows.shape[0], result.shape[2])


def gate_forward(gate, up):
    sigmoid = jax.nn.sigmoid(gate)
    return (gate * sigmoid * up).astype(jnp.bfloat16)


def gate_backward(d_hidden, gate, up):
    sigmoid = jax.nn.sigmoid(gate)
    d_gate = (d_hidden * up * sigmoid * (1.0 + gate * (1.0 - sigmoid))).astype(jnp.bfloat16)
    d_up = (d_hidden * gate * sigmoid).astype(jnp.bfloat16)
    return (d_gate, d_up)


def on_device(tokens, combine, expert_ids, expert_counts, w_gate, w_up, w_down, cotangent):
    tokens_total = combine.shape[0]
    capacity = 2 * tokens_total + EXPERTS * BLOCK
    slot_index, owner_token, block_expert = route_layout(
        expert_ids, expert_counts, tokens_total, capacity
    )
    slot_pairs = slot_index.reshape(tokens_total, 2)
    full_tokens = lax.all_gather(tokens, "tensor", axis=0, tiled=True)
    zero_row = jnp.zeros((1, full_tokens.shape[1]), full_tokens.dtype)
    rows = jnp.concatenate([full_tokens, zero_row], 0)[owner_token]
    gate_part = blocked_product(rows, w_gate, block_expert, False)
    up_part = blocked_product(rows, w_up, block_expert, False)
    gate, up = (
        lax.psum_scatter(gate_part, "section", scatter_dimension=1, tiled=True),
        lax.psum_scatter(up_part, "section", scatter_dimension=1, tiled=True),
    )
    hidden = lax.all_gather(gate_forward(gate, up), "section", axis=1, tiled=True)
    out_rows = blocked_product(hidden, w_down, block_expert, False)
    token_terms = jnp.sum(combine[:, :, None] * out_rows[slot_pairs], 1)
    layer_out = lax.psum_scatter(token_terms, "tensor", scatter_dimension=0, tiled=True).astype(
        jnp.bfloat16
    )
    full_cot = lax.all_gather(cotangent, "tensor", axis=0, tiled=True)
    combine_slot = jnp.zeros((capacity,), jnp.float32).at[slot_index].set(combine.reshape(-1))
    cot_rows = jnp.concatenate([full_cot, zero_row], 0)[owner_token]
    row_grad = (combine_slot[:, None] * cot_rows.astype(jnp.float32)).astype(jnp.bfloat16)
    hidden_part = blocked_product(row_grad, w_down, block_expert, True)
    d_hidden = lax.psum_scatter(hidden_part, "section", scatter_dimension=1, tiled=True)
    gate_share, up_share = gate_backward(d_hidden, gate, up)
    d_gate, d_up = (
        lax.all_gather(gate_share, "section", axis=1, tiled=True),
        lax.all_gather(up_share, "section", axis=1, tiled=True),
    )
    nblocks = block_expert.shape[0]
    hidden_blocks = hidden.reshape(nblocks, BLOCK, hidden.shape[1])
    grad_blocks = row_grad.reshape(nblocks, BLOCK, row_grad.shape[1])
    block_terms = lax.dot_general(
        hidden_blocks, grad_blocks, (((1,), (1,)), ((0,), (0,))), preferred_element_type=jnp.float32
    )
    block_owner = (block_expert[None, :] == jnp.arange(EXPERTS, dtype=jnp.int32)[:, None]).astype(
        jnp.float32
    )
    d_down = jnp.einsum(
        "eb,bfd->efd", block_owner, block_terms, precision=lax.Precision.HIGHEST
    ).astype(jnp.bfloat16)
    d_rows = blocked_product(d_gate, w_gate, block_expert, True) + blocked_product(
        d_up, w_up, block_expert, True
    )
    grad_terms = jnp.sum(d_rows[slot_pairs], 1)
    d_tokens = lax.psum_scatter(grad_terms, "tensor", scatter_dimension=0, tiled=True).astype(
        jnp.bfloat16
    )
    return (layer_out, d_tokens, d_down)


def solution(mesh):
    in_specs = (
        P("tensor", "section"),
        P(),
        P(),
        P(),
        P(None, "section", "tensor"),
        P(None, "section", "tensor"),
        P(None, "tensor", "section"),
        P("tensor", "section"),
    )
    out_specs = (P("tensor", "section"), P("tensor", "section"), P(None, "tensor", "section"))
    return jax.shard_map(
        on_device, mesh=mesh, in_specs=in_specs, out_specs=out_specs, check_vma=False
    )
```

profile of v0, /device:TPU:0, one launch (start us, length us, event | category | flops | bytes accessed | tf_op | source)
XLA Modules:
  0.0 974.9 jit_solution(12361082168523723385)
XLA Ops:
  14.7 11.8 %all_gather.15 = bf16[192,1536]{1,0:T(8,128)(2,1)S(1)} all-gather(bf16[24,1536]{1,0:T(8,128)(2,1)} %param.20), channel_id=1, replica_groups=mesh['section'=4,'tensor'=8] {'tensor'}, dimensions={0}, use_global_device_ids=true | all-gather | bytes 663552 | tf_op jit(solution)/shard_map/all_gather | solution.py:63
  34.4 51.1 %while.60 = (s32[]{:T(128)}, f32[7,128,2048]{2,1,0:T(8,128)}, bf16[7,128,1536]{2,1,0:T(8,128)(2,1)S(1)}, s32[7]{0:T(128)S(1)}, bf16[4,1536,2048]{2,1,0:T(8,128)(2,1)}, /*index=5*/s32[]{:T(128)}, s32[]{:T(128)}, s32[]{:T(128)}) while((s32[]{:T(128)}, f32[7,128,2048]{2,1,0:T(8,128)}, bf16[7,128,1536]{2,1,0:T(8,128)(2,1)S(1)}, s32[7]{0:T(128)S(1)}, ...), condition=%wide.region_8.9_spmd, body=%wide.region_7.8_spmd.sunk | while | flops 805306368 | bytes 7734923 | solution.py:40
  36.9 4.8 fusion.121
  44.2 4.8 fusion.121
  51.5 4.8 fusion.121
  58.8 4.8 fusion.121
  66.1 4.8 fusion.121
  73.4 4.8 fusion.121
  80.7 4.8 fusion.121
  86.5 9.6 all_gather.17
  96.2 4.4 gather_fusion.2
  109.8 58.8 %while.63 = (s32[]{:T(128)}, f32[7,128,2048]{2,1,0:T(8,128)}, bf16[7,128,1536]{2,1,0:T(8,128)(2,1)S(1)}, s32[7]{0:T(128)S(1)}, bf16[4,2048,1536]{2,1,0:T(8,128)(2,1)}, /*index=5*/s32[]{:T(128)}, s32[]{:T(128)}, s32[]{:T(128)}) while((s32[]{:T(128)}, f32[7,128,2048]{2,1,0:T(8,128)}, bf16[7,128,1536]{2,1,0:T(8,128)(2,1)S(1)}, ...), condition=%wide.region_19.20_spmd, body=%wide.region_18.19_spmd.sunk | while | flops 805306368 | bytes 7734923 | solution.py:40
  112.3 5.9 fusion.130
  120.7 5.9 fusion.130
  129.1 5.9 fusion.130
  137.5 5.9 fusion.130
  145.9 5.9 fusion.130
  154.3 5.9 fusion.130
  162.7 5.9 fusion.130
  172.6 52.6 %while.61 = (s32[]{:T(128)}, f32[7,128,2048]{2,1,0:T(8,128)}, bf16[7,128,1536]{2,1,0:T(8,128)(2,1)}, s32[7]{0:T(128)S(1)}, bf16[4,1536,2048]{2,1,0:T(8,128)(2,1)}, /*index=5*/s32[]{:T(128)}, s32[]{:T(128)}, s32[]{:T(128)}) while((s32[]{:T(128)}, f32[7,128,2048]{2,1,0:T(8,128)}, bf16[7,128,1536]{2,1,0:T(8,128)(2,1)}, s32[7]{0:T(128)S(1)}, ...), condition=%wide.region_11.12_spmd, body=%wide.region_10.11_spmd.sunk | while | flops 805306368 | bytes 7734923 | solution.py:40
  175.1 4.9 fusion.124
  182.6 5.2 fusion.124
  190.3 4.9 fusion.124
  197.7 4.9 fusion.124
  205.1 4.9 fusion.124
  212.6 5.1 fusion.124
  220.2 5.0 fusion.124
  225.5 119.4 %reduce-scatter.12.cloned.1.call-done = f32[896,512]{1,0:T(8,128)} async-done(((f32[896,2048]{1,0:T(8,128)}), f32[896,512]{1,0:T(8,128)}) %reduce-scatter.12.cloned.1.call-update) | async-done | bytes 1835024 | tf_op jit(solution)/shard_map/reduce_scatter | solution.py:83
  344.9 130.6 %reduce-scatter.8.cloned.1.call-done = f32[896,512]{1,0:T(8,128)} async-done(((f32[896,2048]{1,0:T(8,128)}), f32[896,512]{1,0:T(8,128)}) %reduce-scatter.8.cloned.1.call-update) | async-done | bytes 1835024 | tf_op jit(solution)/shard_map/reduce_scatter | solution.py:70
  475.5 5.6 multiply_convert_fusion
  482.7 71.2 %all-gather.8.cloned.1.call-done = bf16[896,2048]{1,0:T(8,128)(2,1)} async-done(((bf16[896,512]{1,0:T(8,128)(2,1)}), bf16[896,2048]{1,0:T(8,128)(2,1)}) %all-gather.8.cloned.1.call-update) | async-done | bytes 3670032 | tf_op jit(solution)/shard_map/all_gather | solution.py:87
  557.0 60.8 %while.65 = (s32[]{:T(128)}, f32[7,128,1536]{2,1,0:T(8,128)}, bf16[7,128,2048]{2,1,0:T(8,128)(2,1)}, s32[7]{0:T(128)S(1)}, bf16[4,1536,2048]{2,1,0:T(8,128)(2,1)}, /*index=5*/s32[]{:T(128)}, s32[]{:T(128)}, s32[]{:T(128)}) while((s32[]{:T(128)}, f32[7,128,1536]{2,1,0:T(8,128)}, bf16[7,128,2048]{2,1,0:T(8,128)(2,1)}, s32[7]{0:T(128)S(1)}, ...), condition=%wide.region_24.25_spmd, body=%wide.region_23.24_spmd.sunk | while | flops 805306368 | bytes 7603851 | solution.py:40
  559.5 6.6 fusion.136
  568.7 6.1 fusion.136
  577.3 6.1 fusion.136
  586.0 6.1 fusion.136
  594.6 6.1 fusion.136
  603.2 6.1 fusion.136
  611.8 6.1 fusion.136
  617.9 8.3 all-gather.6.cloned.1.call-done
  629.3 59.3 %while.64 = (s32[]{:T(128)}, f32[7,128,1536]{2,1,0:T(8,128)}, bf16[7,128,2048]{2,1,0:T(8,128)(2,1)}, s32[7]{0:T(128)S(1)}, bf16[4,1536,2048]{2,1,0:T(8,128)(2,1)}, /*index=5*/s32[]{:T(128)}, s32[]{:T(128)}, s32[]{:T(128)}) while((s32[]{:T(128)}, f32[7,128,1536]{2,1,0:T(8,128)}, bf16[7,128,2048]{2,1,0:T(8,128)(2,1)}, s32[7]{0:T(128)S(1)}, ...), condition=%wide.region_22.23_spmd, body=%wide.region_21.22_spmd.sunk | while | flops 805306368 | bytes 7603851 | solution.py:40
  631.6 6.6 fusion.133
  640.5 6.1 fusion.133
  648.9 6.1 fusion.133
  657.3 6.1 fusion.133
  665.7 6.1 fusion.133
  674.1 6.1 fusion.133
  682.5 6.1 fusion.133
  688.6 7.8 add.129
  696.4 6.9 gather_fusion.3
  707.1 5.5 reduce_sum.49
  713.1 33.1 %fusion.94 = f32[7,2048,1536]{2,1,0:T(8,128)} fusion(bf16[7,128,2048]{2,1,0:T(8,128)(2,1)} %bitcast.191, bf16[7,128,1536]{2,1,0:T(8,128)(2,1)S(1)} %get-tuple-element.600), kind=kOutput, calls=%fused_computation.103 | convolution fusion | flops 5637144576 | bytes 94502912 | tf_op jit(solution)/shard_map/dot_general | solution.py:92
  749.3 51.6 %while.62 = (s32[]{:T(128)}, f32[7,128,1536]{2,1,0:T(8,128)}, bf16[7,128,2048]{2,1,0:T(8,128)(2,1)}, s32[7]{0:T(128)S(1)}, bf16[4,2048,1536]{2,1,0:T(8,128)(2,1)}, /*index=5*/s32[]{:T(128)}, s32[]{:T(128)}, s32[]{:T(128)}) while((s32[]{:T(128)}, f32[7,128,1536]{2,1,0:T(8,128)}, bf16[7,128,2048]{2,1,0:T(8,128)(2,1)}, s32[7]{0:T(128)S(1)}, ...), condition=%wide.region_14.15_spmd, body=%wide.region_13.14_spmd.sunk | while | flops 805306368 | bytes 7603851 | solution.py:40
  751.9 4.9 fusion.127
  759.2 4.9 fusion.127
  766.6 4.9 fusion.127
  774.0 4.8 fusion.127
  781.4 4.9 fusion.127
  788.7 4.8 fusion.127
  796.1 4.8 fusion.127
  801.0 6.9 gather_fusion.1
  810.8 4.6 multiply_reduce_fusion
  815.4 125.2 %fusion.74 = bf16[4,2048,1536]{2,0,1:T(4,128)(2,1)} fusion(f32[7,2048,1536]{2,1,0:T(8,128)} %fusion.94, s32[7]{0:T(128)S(1)} %get-tuple-element.625), kind=kOutput, calls=%fused_computation.56 | convolution fusion | flops 1069547520 | bytes 113246240 | tf_op jit(solution)/shard_map/eb,bfd->efd/dot_general | solution.py:98
  940.7 24.0 %copy.31 = bf16[4,2048,1536]{2,1,0:T(8,128)(2,1)} copy(bf16[4,2048,1536]{2,0,1:T(4,128)(2,1)} %fusion.74) | data formatting | bytes 50331648
  (110 shorter events, 75.5 us)
Async XLA Ops:
  7.2 218.3 %reduce-scatter.6.cloned.1.call-start = ((), (), s32[]{:S(2)}) async-start(), calls=%async_computation.5 | async-start | bytes 9175040 | tf_op jit(solution)/shard_map/reduce_scatter | solution.py:69
  85.5 15.1 %copy-start = (bf16[7,128,1536]{2,1,0:T(8,128)(2,1)}, bf16[7,128,1536]{2,1,0:T(8,128)(2,1)S(1)}, u32[]{:S(2)}) copy-start(bf16[7,128,1536]{2,1,0:T(8,128)(2,1)S(1)} %get-tuple-element.601) | copy-start | bytes 8257540
  85.5 0.7 copy-start.2
  85.5 1.0 copy-start.1
  85.5 259.4 %reduce-scatter.12.cloned.1.call-start = ((), (), s32[]{:S(2)}) async-start(), calls=%async_computation.9 | async-start | bytes 9175040 | tf_op jit(solution)/shard_map/reduce_scatter | solution.py:83
  168.6 306.9 %reduce-scatter.8.cloned.1.call-start = ((), (), s32[]{:S(2)}) async-start(), calls=%async_computation.6 | async-start | bytes 9175040 | tf_op jit(solution)/shard_map/reduce_scatter | solution.py:70
  225.2 328.7 %all-gather.8.cloned.1.call-start = ((), (), s32[]{:S(2)}) async-start(), calls=%async_computation.11 | async-start | bytes 4587520 | tf_op jit(solution)/shard_map/all_gather | solution.py:87
  481.2 145.0 %all-gather.6.cloned.1.call-start = ((), (), s32[]{:S(2)}) async-start(), calls=%async_computation.10 | async-start | bytes 4587520 | tf_op jit(solution)/shard_map/all_gather | solution.py:86
  481.7 231.4 %all-gather.4.cloned.1.call-start = ((), (), s32[]{:S(2)}) async-start(), calls=%async_computation.7 | async-start | bytes 4587520 | tf_op jit(solution)/shard_map/all_gather | solution.py:72
  482.3 482.4 %reduce-scatter.14.cloned.1.call-start = ((), (), s32[]{:S(2)}) async-start(), calls=%async_computation.12 | async-start | bytes 1327104 | tf_op jit(solution)/shard_map/reduce_scatter | solution.py:105
  712.6 253.6 %reduce-scatter.10.cloned.1.call-start = ((), (), s32[]{:S(2)}) async-start(), calls=%async_computation.8 | async-start | bytes 1327104 | tf_op jit(solution)/shard_map/reduce_scatter | solution.py:75
Sparse Core Ops, SparseCore 0:
  85.7 128.0 reduce-scatter.5
  216.6 128.2 reduce-scatter.11
  347.2 128.2 reduce-scatter.7
  481.3 72.6 all-gather.7
  555.4 70.7 all-gather.5
  627.6 70.6 all-gather.3
  712.8 34.8 reduce-scatter.13
  815.6 34.9 reduce-scatter.9
where the time goes:
time: 986 us; the launch traced here: 975 us
  matrix products  388 us (39%)
  waiting for transfers between devices  331 us (34%)
  local copies, waits for them, and re-layouts  107 us (11%)
  loops' own time  80.1 us (8%)
  other arithmetic  32.1 us (3%)
  blocking collectives  21.4 us (2%)
  between operations  14.5 us (1%)
    reduce_scatter x1, waiting for transfers between devices, on_device(): lax.psum_scatter(up_part, 'section', scatter_dimension=1, tiled=True)  131 us
    dot_general x21, matrix products, apply_block(): lax.dot_general(segment, matrix, (((1,), (1,)), ((), ())), preferred_elem...  127 us
    dot_general x1, matrix products, on_device(): jnp.einsum('eb,bfd->efd', block_owner, block_terms, precision=lax.Precisi...  125 us
    reduce_scatter x1, waiting for transfers between devices, on_device(): lax.psum_scatter(hidden_part, 'section', scatter_dimension=1, tiled=True)  119 us
    dot_general x21, matrix products, apply_block(): return jnp.dot(segment, matrix, preferred_element_type=jnp.float32)  102 us
    another operation x6, loops' own time, blocked_product(): result = lax.map(apply_block, (blocks, block_expert))  80.1 us
    all_gather x1, waiting for transfers between devices, on_device(): lax.all_gather(up_share, 'section', axis=1, tiled=True)  71.2 us
    dot_general x1, matrix products, on_device(): lax.dot_general(hidden_blocks, grad_blocks, (((1,), (1,)), ((0,), (0,))),...  33.1 us
  transfers between devices with their start and end apart: 8, of which 4 were waited for; matrix products, arithmetic and copies ran while one was open for 48% of the time, Pallas kernels for 0%

commit v1 on v0

v1 whole, which is shorter than its diff:
```python
import functools

import jax
import jax.numpy as jnp
from jax import lax
from jax.experimental import pallas as pl
from jax.experimental.pallas import tpu as pltpu
from jax.sharding import PartitionSpec as P

SUB = 256
F32 = jnp.float32
BF16 = jnp.bfloat16
VMEM_LIMIT = 40 * 1024 * 1024


def dot(a, b, contract):
    return lax.dot_general(a, b, ((contract[0], contract[1]), ((), ())), preferred_element_type=F32)


def partial_kernel(masked, order, x, rg, other, wg, wu, wd, *rest):
    own, send = rest[-2:]
    step = pl.program_id(1)
    terms = (
        dot(x[...], wg[0], ((1,), (0,))),
        dot(x[...], wu[0], ((1,), (0,))),
        dot(rg[...], wd[0], ((1,), (1,))),
    )
    if not masked:
        for n, term in enumerate(terms):
            own[n] = term
            send[n] = term.astype(BF16)
        return
    chosen = other[...] == order[1 + step]
    last = pl.num_programs(1) - 1

    @pl.when(step == 0)
    def _():
        for n, term in enumerate(terms):
            own[n] = term

    @pl.when(step > 0)
    def _():
        for n, term in enumerate(terms):
            own[n] = jnp.where(chosen, term, own[n])

    @pl.when(step == last)
    def _():
        for n in range(3):
            send[n] = own[n].astype(BF16)


def partial_products(chunk, order, x, rg, other, w_gate, w_up, w_down, after):
    group, start, width = chunk
    experts, depth, _ = w_gate.shape
    rows = x.shape[0]
    sub = min(SUB, width)
    first, count = (0, 1) if group == 0 else (1, experts - 1)
    base = start // sub
    const = lambda j, e, order: (0, 0)
    column = lambda j, e, order: (order[first + e], 0, base + j)
    row = lambda j, e, order: (order[first + e], base + j, 0)
    out = lambda j, e, order: (0, 0, j)
    return pl.pallas_call(
        functools.partial(partial_kernel, group == 1),
        grid_spec=pltpu.PrefetchScalarGridSpec(
            num_scalar_prefetch=1,
            grid=(width // sub, count),
            in_specs=[
                pl.BlockSpec((rows, depth), const),
                pl.BlockSpec((rows, depth), const),
                pl.BlockSpec((rows, 1), const),
                pl.BlockSpec((1, depth, sub), column),
                pl.BlockSpec((1, depth, sub), column),
                pl.BlockSpec((1, sub, depth), row),
            ]
            + [pl.BlockSpec(memory_space=pl.ANY)] * len(after),
            out_specs=[
                pl.BlockSpec((3, rows, sub), out),
                pl.BlockSpec((3, rows, sub), out),
            ],
        ),
        out_shape=[
            jax.ShapeDtypeStruct((3, rows, width), F32),
            jax.ShapeDtypeStruct((3, rows, width), BF16),
        ],
        compiler_params=pltpu.CompilerParams(vmem_limit_bytes=VMEM_LIMIT),
        cost_estimate=pl.CostEstimate(
            flops=6 * rows * depth * width * count,
            bytes_accessed=6 * depth * width * count + 18 * rows * width,
            transcendentals=0,
        ),
        name="partial",
    )(order, x, rg, other, w_gate, w_up, w_down, *after)


def post_kernel(masked, opening, closing, order, mine, came, rg, weight, other, wg, wu, wd, *rest):
    picked, rest = rest[-1], rest[:-1]
    if not opening:
        sums_in, rest = rest[0], rest[2:]
    sums, d_down, pieces = rest[0], rest[1], rest[2:]
    j, step = pl.program_id(0), pl.program_id(1)

    @pl.when(jnp.logical_and(j == 0, step == 0))
    def _():
        sums[...] = jnp.zeros_like(sums) if opening else sums_in[...]

    edge = order[order.shape[0] - 1]

    @pl.when(jnp.logical_and(step == 0, edge == 1))
    def _():
        picked[...] = came[...]

    @pl.when(jnp.logical_and(step == 0, edge == 0))
    def _():
        picked[...] = mine[...]

    hidden, d_gate, d_up = picked[0], picked[1], picked[2]
    if masked:
        chosen = other[...] == order[1 + step]
        hidden = jnp.where(chosen, hidden, jnp.zeros_like(hidden))
        d_gate = jnp.where(chosen, d_gate, jnp.zeros_like(d_gate))
        d_up = jnp.where(chosen, d_up, jnp.zeros_like(d_up))
    sums[0] += weight[...] * dot(hidden, wd[0], ((1,), (0,)))
    sums[1] += dot(d_gate, wg[0], ((1,), (1,))) + dot(d_up, wu[0], ((1,), (1,)))
    d_down[0] = dot(hidden, rg[...], ((0,), (0,))).astype(BF16)

    if closing:

        @pl.when(jnp.logical_and(j == pl.num_programs(0) - 1, step == pl.num_programs(1) - 1))
        def _():
            size = pieces[0].shape[1]
            for n, piece in enumerate(pieces):
                piece[...] = sums[:, n * size : (n + 1) * size].astype(BF16)


def post_products(chunk, order, mine, came, rg, weight, other, w_gate, w_up, w_down, state, pieces):
    group, start, width = chunk
    experts, depth, units = w_gate.shape
    rows = rg.shape[0]
    sub = min(SUB, width)
    first, count = (0, 1) if group == 0 else (1, experts - 1)
    base = start // sub
    const = lambda j, e, order: (0, 0)
    whole = lambda j, e, order: (0, 0, 0)
    column = lambda j, e, order: (order[first + e], 0, base + j)
    row = lambda j, e, order: (order[first + e], base + j, 0)
    part = lambda j, e, order: (0, 0, j)
    opening = state is None
    sums_spec = pl.BlockSpec((2, rows, depth), whole)
    in_specs = [
        pl.BlockSpec((3, rows, sub), part),
        pl.BlockSpec((3, rows, sub), part),
        pl.BlockSpec((rows, depth), const),
        pl.BlockSpec((rows, 1), const),
        pl.BlockSpec((rows, 1), const),
        pl.BlockSpec((1, depth, sub), column),
        pl.BlockSpec((1, depth, sub), column),
        pl.BlockSpec((1, sub, depth), row),
    ]
    operands = [order, mine, came, rg, weight, other, w_gate, w_up, w_down]
    aliases = {}
    if not opening:
        in_specs += [sums_spec, pl.BlockSpec(memory_space=pl.ANY)]
        aliases = {len(operands): 0, len(operands) + 1: 1}
        operands += list(state)
    out_specs = [sums_spec, pl.BlockSpec((1, sub, depth), row)]
    out_shape = [
        jax.ShapeDtypeStruct((2, rows, depth), F32),
        jax.ShapeDtypeStruct((experts, units, depth), BF16),
    ]
    if pieces:
        out_specs += [pl.BlockSpec((2, rows // pieces, depth), whole)] * pieces
        out_shape += [jax.ShapeDtypeStruct((2, rows // pieces, depth), BF16)] * pieces
    return pl.pallas_call(
        functools.partial(post_kernel, group == 1, opening, pieces > 0),
        grid_spec=pltpu.PrefetchScalarGridSpec(
            num_scalar_prefetch=1,
            grid=(width // sub, count),
            in_specs=in_specs,
            out_specs=out_specs,
            scratch_shapes=[pltpu.VMEM((3, rows, sub), BF16)],
        ),
        out_shape=out_shape,
        input_output_aliases=aliases,
        compiler_params=pltpu.CompilerParams(vmem_limit_bytes=VMEM_LIMIT),
        cost_estimate=pl.CostEstimate(
            flops=8 * rows * depth * width * count,
            bytes_accessed=8 * depth * width * count + 16 * rows * depth,
            transcendentals=0,
        ),
        name="post",
    )(*operands)


def activations(gate, up, d_hidden):
    sigmoid = jax.nn.sigmoid(gate)
    active = gate * sigmoid
    hidden = (active * up).astype(BF16)
    d_gate = (d_hidden * up * sigmoid * (1.0 + gate * (1.0 - sigmoid))).astype(BF16)
    d_up = (d_hidden * active).astype(BF16)
    return jnp.stack([hidden, d_gate, d_up], 0)


def shift(x, step, size):
    return lax.ppermute(x, "tensor", [(i, (i - step) % size) for i in range(size)])


def chunk_plan(units):
    width = min(512, units)
    blocks = [(start, width) for start in range(0, units, width)]
    plan = [(0,) + blocks[0]]
    for n in range(len(blocks) - 1):
        plan += [(1,) + blocks[n], (0,) + blocks[n + 1]]
    plan = plan[:-1] + [(1,) + blocks[-1], plan[-1]] if len(blocks) > 1 else plan + [(1,) + blocks[-1]]
    return plan


def on_device(sections, parts, tokens, combine, expert_ids, expert_counts, w_gate, w_up, w_down, cotangent):
    total = combine.shape[0]
    local = tokens.shape[0]
    experts = w_gate.shape[0]
    me = lax.axis_index("tensor")
    place = lax.axis_index("section")

    x = jnp.concatenate([tokens] + [shift(tokens, n, parts) for n in range(1, parts)], 0)
    cot = jnp.concatenate([cotangent] + [shift(cotangent, n, parts) for n in range(1, parts)], 0)

    def turned(v):
        return lax.dynamic_slice_in_dim(jnp.concatenate([v, v], 0), me * local, total, 0)

    weights, ids = turned(combine), turned(expert_ids)
    common = jnp.argmax(expert_counts).astype(jnp.int32)
    ranks = jnp.arange(experts - 1, dtype=jnp.int32)
    line = sections == 4
    edge = jnp.logical_or(place == 0, place == sections - 1) if line else jnp.zeros((), bool)
    order = jnp.concatenate(
        [common[None], ranks + (ranks >= common).astype(jnp.int32), edge.astype(jnp.int32)[None]]
    )
    is_first = ids[:, :1] == common
    other = jnp.where(is_first, ids[:, 1:], ids[:, :1])
    weight = (
        jnp.where(is_first, weights[:, :1], weights[:, 1:]),
        jnp.where(is_first, weights[:, 1:], weights[:, :1]),
    )
    rg = tuple((w * cot.astype(F32)).astype(BF16) for w in weight)

    plan = chunk_plan(w_gate.shape[2])
    count = len(plan)
    own, sent, summed, mine, came = {}, {}, {}, {}, {}
    state = None

    def send(v, pairs):
        return lax.ppermute(v, "section", pairs)

    def begin(k, after):
        own[k], send_k = partial_products(
            plan[k], order, x, rg[plan[k][0]], other, w_gate, w_up, w_down, after
        )
        sent[k] = send(send_k, [(0, 1), (3, 2)]) if line else None

    def merge(k):
        if not line:
            return None
        summed[k] = own[k] + sent[k].astype(F32)
        packed = summed[k].astype(BF16)
        sent[k] = send(packed, [(1, 2), (2, 1)])
        return packed

    def finish(k):
        if line:
            full = summed[k] + sent[k].astype(F32)
            mine[k] = activations(full[0], full[1], full[2])
            came[k] = send(mine[k], [(1, 0), (2, 3)])
        else:
            full = lax.psum(own[k], "section")
            mine[k] = came[k] = activations(full[0], full[1], full[2])

    for k in range(2):
        begin(k, ())
    for step in range(count + 2):
        after = ()
        if step < count:
            packed = merge(step)
            after = () if packed is None else (packed,)
        if 1 <= step <= count:
            finish(step - 1)
        if step + 2 < count:
            begin(step + 2, after)
        if step >= 2:
            k = step - 2
            group = plan[k][0]
            state = post_products(
                plan[k], order, mine[k], came[k], rg[group], weight[group], other,
                w_gate, w_up, w_down, state, parts if k == count - 1 else 0,
            )
    d_down = state[1]
    pieces = state[2:]
    result = pieces[0].astype(F32)
    for n in range(1, parts):
        result += lax.ppermute(
            pieces[n], "tensor", [(i, (i + n) % parts) for i in range(parts)]
        ).astype(F32)
    result = result.astype(BF16)
    return result[0], result[1], d_down


def solution(mesh):
    in_specs = (
        P("tensor", "section"),
        P(),
        P(),
        P(),
        P(None, "section", "tensor"),
        P(None, "section", "tensor"),
        P(None, "tensor", "section"),
        P("tensor", "section"),
    )
    out_specs = (P("tensor", "section"), P("tensor", "section"), P(None, "tensor", "section"))
    return jax.shard_map(
        functools.partial(on_device, mesh.shape["section"], mesh.shape["tensor"]),
        mesh=mesh,
        in_specs=in_specs,
        out_specs=out_specs,
        check_vma=False,
    )
```

time: 986 us -> 265 us (0.27)
  the two profiles are of different devices: /device:TPU:0 before, /device:TPU:9 now
where the time goes in v1:
time: 265 us; the launch traced here: 264 us
  Pallas kernels  124 us (47%)
  starting transfers between devices  81 us (31%)
  waiting for transfers between devices  43.8 us (17%)
  other arithmetic  11.2 us (4%)
    pallas_call x8, Pallas kernels, post_products(): pl.pallas_call(functools.partial(post_kernel, group == 1, opening, pieces...  71.5 us
    pallas_call x8, Pallas kernels, partial_products(): pl.pallas_call(functools.partial(partial_kernel, group == 1), grid_spec=p...  52.8 us
    ppermute x24, starting transfers between devices, send(): return lax.ppermute(v, 'section', pairs)  52.1 us
    ppermute x24, waiting for transfers between devices, send(): return lax.ppermute(v, 'section', pairs)  31.5 us
    ppermute x14, starting transfers between devices, shift(): lax.ppermute(x, 'tensor', [(i, (i - step) % size) for i in range(size)])  16.3 us
    ppermute x7, starting transfers between devices, on_device(): lax.ppermute(pieces[n], 'tensor', [(i, (i + n) % parts) for i in range(pa...  12.6 us
    ppermute x7, waiting for transfers between devices, on_device(): lax.ppermute(pieces[n], 'tensor', [(i, (i + n) % parts) for i in range(pa...  9.57 us
  transfers between devices with their start and end apart: 45, of which 12 were waited for; matrix products, arithmetic and copies ran while one was open for 5% of the time, Pallas kernels for 43%

profile of v1, /device:TPU:9, one launch (start us, length us, event | category | flops | bytes accessed | tf_op | source)
XLA Modules:
  0.0 263.9 jit_solution(7113133279892919188)
XLA Ops:
  1.4 2.2 collective-permute-start.8
  3.6 1.3 collective-permute-start.9
  4.9 1.2 collective-permute-start.10
  6.1 1.0 constant_dynamic-update-slice_fusion.15
  7.1 0.8 fusion.19
  8.0 0.8 fusion.18
  12.8 1.9 collective-permute-start.13
  14.8 2.0 collective-permute-start.1
  16.8 3.0 %collective-permute-start.2 = (bf16[24,1536]{1,0:T(8,128)(2,1)S(1)}, bf16[24,1536]{1,0:T(8,128)(2,1)S(1)}, u32[]{:S(2)}, u32[]{:S(2)}) collective-permute-start(bf16[24,1536]{1,0:T(8,128)(2,1)S(1)} %copy-done.3), channel_id=1, source_target_pairs={{0,5},{1,6},{2,7},{3,0},{4,1},{5,2},{6,3},{7,4},{8,13},{9,14},{10,... | collective-permute-start | bytes 221192 | tf_op jit(solution)/shard_map/ppermute | solution.py:205
  21.8 1.7 collective-permute-start.6
  23.6 1.7 collective-permute-done.4
  25.3 1.0 collective-permute-done.5
  26.3 3.9 %partial.12 = (f32[3,192,512]{2,1,0:T(8,128)S(1)}, bf16[3,192,512]{2,1,0:T(8,128)(2,1)S(1)}) custom-call(s32[5]{0:T(128)S(1)} %pad_add_fusion.order, bf16[192,1536]{1,0:T(8,128)(2,1)S(1)} %constant_dynamic-update-slice_fusion.x, bf16[192,1536]{1,0:T(8,128)(2,1)S(1)} %get-tuple-element.113.rg, s32[192,1]{1,0:T(8,128)S(1)} %select_n.21.other, ...), custom_call_target="tpu_custom_call" | custom-call | flops 905969664 | bytes 6488064 | tf_op jit(solution)/shard_map/partial/pallas_call | solution.py:63
  30.2 1.3 collective-permute-start.20
  31.5 9.3 %partial.8 = (f32[3,192,512]{2,1,0:T(8,128)S(1)}, bf16[3,192,512]{2,1,0:T(8,128)(2,1)S(1)}) custom-call(s32[5]{0:T(128)S(1)} %pad_add_fusion.order, bf16[192,1536]{1,0:T(8,128)(2,1)S(1)} %constant_dynamic-update-slice_fusion.x, bf16[192,1536]{1,0:T(8,128)(2,1)S(1)} %get-tuple-element.112.rg, s32[192,1]{1,0:T(8,128)S(1)} %select_n.21.other, ...), custom_call_target="tpu_custom_call" | custom-call | flops 2717908992 | bytes 15925248 | tf_op jit(solution)/shard_map/partial/pallas_call | solution.py:63
  40.8 1.3 collective-permute-start.14
  42.1 2.8 %collective-permute-done.20 = bf16[3,192,512]{2,1,0:T(8,128)(2,1)S(1)} collective-permute-done((bf16[3,192,512]{2,1,0:T(8,128)(2,1)S(1)}, bf16[3,192,512]{2,1,0:T(8,128)(2,1)S(1)}, u32[]{:S(2)}, u32[]{:S(2)}) %collective-permute-start.20) | collective-permute-done | bytes 589856 | tf_op jit(solution)/shard_map/ppermute | solution.py:253
  45.1 3.2 %collective-permute-start.36 = (bf16[3,192,512]{2,1,0:T(8,128)(2,1)S(1)}, bf16[3,192,512]{2,1,0:T(8,128)(2,1)S(1)}, u32[]{:S(2)}, u32[]{:S(2)}) collective-permute-start(bf16[3,192,512]{2,1,0:T(8,128)(2,1)S(1)} %fusion.6.rest_0_), channel_id=1, source_target_pairs={{8,16},{16,8},{9,17},{17,9},{10,18},{18,10},{11,19},{19,11},{12,20... | collective-permute-start | bytes 1769480 | tf_op jit(solution)/shard_map/ppermute | solution.py:253
  48.3 9.9 %collective-permute-done.14 = bf16[3,192,512]{2,1,0:T(8,128)(2,1)S(1)} collective-permute-done((bf16[3,192,512]{2,1,0:T(8,128)(2,1)S(1)}, bf16[3,192,512]{2,1,0:T(8,128)(2,1)S(1)}, u32[]{:S(2)}, u32[]{:S(2)}) %collective-permute-start.14) | collective-permute-done | bytes 589856 | tf_op jit(solution)/shard_map/ppermute | solution.py:253
  58.4 3.2 %collective-permute-start.34 = (bf16[3,192,512]{2,1,0:T(8,128)(2,1)S(1)}, bf16[3,192,512]{2,1,0:T(8,128)(2,1)S(1)}, u32[]{:S(2)}, u32[]{:S(2)}) collective-permute-start(bf16[3,192,512]{2,1,0:T(8,128)(2,1)S(1)} %fusion.2.rest_0_), channel_id=1, source_target_pairs={{8,16},{16,8},{9,17},{17,9},{10,18},{18,10},{11,19},{19,11},{12,20... | collective-permute-start | bytes 1769480 | tf_op jit(solution)/shard_map/ppermute | solution.py:253
  61.6 3.9 %partial.13 = (f32[3,192,512]{2,1,0:T(8,128)S(1)}, bf16[3,192,512]{2,1,0:T(8,128)(2,1)S(1)}) custom-call(s32[5]{0:T(128)S(1)} %pad_add_fusion.order, bf16[192,1536]{1,0:T(8,128)(2,1)S(1)} %constant_dynamic-update-slice_fusion.x, bf16[192,1536]{1,0:T(8,128)(2,1)S(1)} %get-tuple-element.113.rg, s32[192,1]{1,0:T(8,128)S(1)} %select_n.21.other, ...), custom_call_target="tpu_custom_call" | custom-call | flops 905969664 | bytes 6488064 | tf_op jit(solution)/shard_map/partial/pallas_call | solution.py:63
  65.5 1.3 collective-permute-start.21
  66.8 9.3 %partial.9 = (f32[3,192,512]{2,1,0:T(8,128)S(1)}, bf16[3,192,512]{2,1,0:T(8,128)(2,1)S(1)}) custom-call(s32[5]{0:T(128)S(1)} %pad_add_fusion.order, bf16[192,1536]{1,0:T(8,128)(2,1)S(1)} %constant_dynamic-update-slice_fusion.x, bf16[192,1536]{1,0:T(8,128)(2,1)S(1)} %get-tuple-element.112.rg, s32[192,1]{1,0:T(8,128)S(1)} %select_n.21.other, ...), custom_call_target="tpu_custom_call" | custom-call | flops 2717908992 | bytes 15925248 | tf_op jit(solution)/shard_map/partial/pallas_call | solution.py:63
  76.1 1.3 collective-permute-start.15
  78.0 4.1 %collective-permute-start.37 = (bf16[3,192,512]{2,1,0:T(8,128)(2,1)S(1)}, bf16[3,192,512]{2,1,0:T(8,128)(2,1)S(1)}, u32[]{:S(2)}, u32[]{:S(2)}) collective-permute-start(bf16[3,192,512]{2,1,0:T(8,128)(2,1)S(1)} %pad_maximum_fusion.7.mine), channel_id=1, source_target_pairs={{8,0},{16,24},{9,1},{17,25},{10,2},{18,26},{11,3},{19,27},{12,4},{... | collective-permute-start | bytes 1769480 | tf_op jit(solution)/shard_map/ppermute | solution.py:253
  82.3 2.1 collective-permute-start.32
  84.4 9.0 %collective-permute-done.15 = bf16[3,192,512]{2,1,0:T(8,128)(2,1)S(1)} collective-permute-done((bf16[3,192,512]{2,1,0:T(8,128)(2,1)S(1)}, bf16[3,192,512]{2,1,0:T(8,128)(2,1)S(1)}, u32[]{:S(2)}, u32[]{:S(2)}) %collective-permute-start.15) | collective-permute-done | bytes 589856 | tf_op jit(solution)/shard_map/ppermute | solution.py:253
  93.6 2.1 collective-permute-start.30
  95.7 9.3 %partial.10 = (f32[3,192,512]{2,1,0:T(8,128)S(1)}, bf16[3,192,512]{2,1,0:T(8,128)(2,1)S(1)}) custom-call(s32[5]{0:T(128)S(1)} %pad_add_fusion.order, bf16[192,1536]{1,0:T(8,128)(2,1)S(1)} %constant_dynamic-update-slice_fusion.x, bf16[192,1536]{1,0:T(8,128)(2,1)S(1)} %get-tuple-element.112.rg, s32[192,1]{1,0:T(8,128)S(1)} %select_n.21.other, ...), custom_call_target="tpu_custom_call" | custom-call | flops 2717908992 | bytes 15925248 | tf_op jit(solution)/shard_map/partial/pallas_call | solution.py:63
  105.1 1.3 collective-permute-start.16
  107.0 4.1 %collective-permute-start.35 = (bf16[3,192,512]{2,1,0:T(8,128)(2,1)S(1)}, bf16[3,192,512]{2,1,0:T(8,128)(2,1)S(1)}, u32[]{:S(2)}, u32[]{:S(2)}) collective-permute-start(bf16[3,192,512]{2,1,0:T(8,128)(2,1)S(1)} %pad_maximum_fusion.6.mine), channel_id=1, source_target_pairs={{8,0},{16,24},{9,1},{17,25},{10,2},{18,26},{11,3},{19,27},{12,4},{... | collective-permute-start | bytes 1769480 | tf_op jit(solution)/shard_map/ppermute | solution.py:253
  111.1 3.9 %partial.14 = (f32[3,192,512]{2,1,0:T(8,128)S(1)}, bf16[3,192,512]{2,1,0:T(8,128)(2,1)S(1)}) custom-call(s32[5]{0:T(128)S(1)} %pad_add_fusion.order, bf16[192,1536]{1,0:T(8,128)(2,1)S(1)} %constant_dynamic-update-slice_fusion.x, bf16[192,1536]{1,0:T(8,128)(2,1)S(1)} %get-tuple-element.113.rg, s32[192,1]{1,0:T(8,128)S(1)} %select_n.21.other, ...), custom_call_target="tpu_custom_call" | custom-call | flops 905969664 | bytes 6488064 | tf_op jit(solution)/shard_map/partial/pallas_call | solution.py:63
  114.9 4.3 %collective-permute-done.16 = bf16[3,192,512]{2,1,0:T(8,128)(2,1)S(1)} collective-permute-done((bf16[3,192,512]{2,1,0:T(8,128)(2,1)S(1)}, bf16[3,192,512]{2,1,0:T(8,128)(2,1)S(1)}, u32[]{:S(2)}, u32[]{:S(2)}) %collective-permute-start.16) | collective-permute-done | bytes 589856 | tf_op jit(solution)/shard_map/ppermute | solution.py:253
  119.2 1.3 collective-permute-start.22
  120.7 3.9 %partial.11 = (f32[3,192,512]{2,1,0:T(8,128)S(1)}, bf16[3,192,512]{2,1,0:T(8,128)(2,1)S(1)}) custom-call(s32[5]{0:T(128)S(1)} %pad_add_fusion.order, bf16[192,1536]{1,0:T(8,128)(2,1)S(1)} %constant_dynamic-update-slice_fusion.x, bf16[192,1536]{1,0:T(8,128)(2,1)S(1)} %get-tuple-element.113.rg, s32[192,1]{1,0:T(8,128)S(1)} %select_n.21.other, ...), custom_call_target="tpu_custom_call" | custom-call | flops 905969664 | bytes 6488064 | tf_op jit(solution)/shard_map/partial/pallas_call | solution.py:63
  124.6 3.2 %collective-permute-start.26 = (bf16[3,192,512]{2,1,0:T(8,128)(2,1)S(1)}, bf16[3,192,512]{2,1,0:T(8,128)(2,1)S(1)}, u32[]{:S(2)}, u32[]{:S(2)}) collective-permute-start(bf16[3,192,512]{2,1,0:T(8,128)(2,1)S(1)} %fusion.4.rest_0_), channel_id=1, source_target_pairs={{8,16},{16,8},{9,17},{17,9},{10,18},{18,10},{11,19},{19,11},{12,20... | collective-permute-start | bytes 1769480 | tf_op jit(solution)/shard_map/ppermute | solution.py:253
  128.4 1.7 collective-permute-start.33
  130.8 1.7 collective-permute-done.22
  132.5 1.3 collective-permute-start.31
  134.0 3.2 %collective-permute-start.28 = (bf16[3,192,512]{2,1,0:T(8,128)(2,1)S(1)}, bf16[3,192,512]{2,1,0:T(8,128)(2,1)S(1)}, u32[]{:S(2)}, u32[]{:S(2)}) collective-permute-start(bf16[3,192,512]{2,1,0:T(8,128)(2,1)S(1)} %fusion.8.rest_0_), channel_id=1, source_target_pairs={{8,16},{16,8},{9,17},{17,9},{10,18},{18,10},{11,19},{19,11},{12,20... | collective-permute-start | bytes 1769480 | tf_op jit(solution)/shard_map/ppermute | solution.py:253
  137.2 5.5 %post.8 = (f32[2,192,1536]{2,1,0:T(8,128)S(1)}, bf16[4,2048,1536]{2,1,0:T(8,128)(2,1)}) custom-call(s32[5]{0:T(128)S(1)} %pad_add_fusion.order, bf16[3,192,512]{2,1,0:T(8,128)(2,1)S(1)} %pad_maximum_fusion.7.mine, bf16[3,192,512]{2,1,0:T(8,128)(2,1)S(1)} %collective-permute-done.37.came, bf16[192,1536]{1,0:T(8,128)(2,1)S(1)} %get-tuple-element.113.rg, ...), custom_call_target="tpu_custom_call" | custom-call | flops 1207959552 | bytes 11010048 | tf_op jit(solution)/shard_map/post/pallas_call | solution.py:174
  142.7 9.3 %partial.15 = (f32[3,192,512]{2,1,0:T(8,128)S(1)}, bf16[3,192,512]{2,1,0:T(8,128)(2,1)S(1)}) custom-call(s32[5]{0:T(128)S(1)} %pad_add_fusion.order, bf16[192,1536]{1,0:T(8,128)(2,1)S(1)} %constant_dynamic-update-slice_fusion.x, bf16[192,1536]{1,0:T(8,128)(2,1)S(1)} %get-tuple-element.112.rg, s32[192,1]{1,0:T(8,128)S(1)} %select_n.21.other, ...), custom_call_target="tpu_custom_call" | custom-call | flops 2717908992 | bytes 15925248 | tf_op jit(solution)/shard_map/partial/pallas_call | solution.py:63
  152.1 1.3 collective-permute-start.23
  153.4 12.2 %post.9 = (f32[2,192,1536]{2,1,0:T(8,128)S(1)}, bf16[4,2048,1536]{2,1,0:T(8,128)(2,1)}) custom-call(s32[5]{0:T(128)S(1)} %pad_add_fusion.order, bf16[3,192,512]{2,1,0:T(8,128)(2,1)S(1)} %pad_maximum_fusion.6.mine, bf16[3,192,512]{2,1,0:T(8,128)(2,1)S(1)} %collective-permute-done.35.came, ...), custom_call_target="tpu_custom_call", output_to_operand_aliasing={{0}: (9, {}), {1}: (10, {})} | custom-call | flops 3623878656 | bytes 23592960 | tf_op jit(solution)/shard_map/post/pallas_call | solution.py:174
  165.6 1.3 collective-permute-start.17
  167.5 4.1 %collective-permute-start.29 = (bf16[3,192,512]{2,1,0:T(8,128)(2,1)S(1)}, bf16[3,192,512]{2,1,0:T(8,128)(2,1)S(1)}, u32[]{:S(2)}, u32[]{:S(2)}) collective-permute-start(bf16[3,192,512]{2,1,0:T(8,128)(2,1)S(1)} %pad_maximum_fusion.3.mine), channel_id=1, source_target_pairs={{8,0},{16,24},{9,1},{17,25},{10,2},{18,26},{11,3},{19,27},{12,4},{... | collective-permute-start | bytes 1769480 | tf_op jit(solution)/shard_map/ppermute | solution.py:253
  172.2 1.3 collective-permute-start.27
  173.8 3.7 %collective-permute-done.17 = bf16[3,192,512]{2,1,0:T(8,128)(2,1)S(1)} collective-permute-done((bf16[3,192,512]{2,1,0:T(8,128)(2,1)S(1)}, bf16[3,192,512]{2,1,0:T(8,128)(2,1)S(1)}, u32[]{:S(2)}, u32[]{:S(2)}) %collective-permute-start.17) | collective-permute-done | bytes 589856 | tf_op jit(solution)/shard_map/ppermute | solution.py:253
  177.5 2.1 collective-permute-start.24
  179.8 3.2 %collective-permute-start.18 = (bf16[3,192,512]{2,1,0:T(8,128)(2,1)S(1)}, bf16[3,192,512]{2,1,0:T(8,128)(2,1)S(1)}, u32[]{:S(2)}, u32[]{:S(2)}) collective-permute-start(bf16[3,192,512]{2,1,0:T(8,128)(2,1)S(1)} %fusion.5), channel_id=1, source_target_pairs={{8,16},{16,8},{9,17},{17,9},{10,18},{18,10},{11,19},{19,11},{12,20... | collective-permute-start | bytes 1769480 | tf_op jit(solution)/shard_map/ppermute | solution.py:253
  183.0 5.7 %post.10 = (f32[2,192,1536]{2,1,0:T(8,128)S(1)}, bf16[4,2048,1536]{2,1,0:T(8,128)(2,1)}) custom-call(s32[5]{0:T(128)S(1)} %pad_add_fusion.order, bf16[3,192,512]{2,1,0:T(8,128)(2,1)S(1)} %pad_maximum_fusion.5.mine, bf16[3,192,512]{2,1,0:T(8,128)(2,1)S(1)} %collective-permute-done.33.came, ...), custom_call_target="tpu_custom_call", output_to_operand_aliasing={{0}: (9, {}), {1}: (10, {})} | custom-call | flops 1207959552 | bytes 11010048 | tf_op jit(solution)/shard_map/post/pallas_call | solution.py:174
  188.7 12.2 %post.11 = (f32[2,192,1536]{2,1,0:T(8,128)S(1)}, bf16[4,2048,1536]{2,1,0:T(8,128)(2,1)}) custom-call(s32[5]{0:T(128)S(1)} %pad_add_fusion.order, bf16[3,192,512]{2,1,0:T(8,128)(2,1)S(1)} %pad_maximum_fusion.4.mine, bf16[3,192,512]{2,1,0:T(8,128)(2,1)S(1)} %collective-permute-done.31.came, ...), custom_call_target="tpu_custom_call", output_to_operand_aliasing={{0}: (9, {}), {1}: (10, {})} | custom-call | flops 3623878656 | bytes 23592960 | tf_op jit(solution)/shard_map/post/pallas_call | solution.py:174
  201.5 1.3 collective-permute-start.25
  203.5 1.5 collective-permute-start.19
  205.0 5.7 %post.12 = (f32[2,192,1536]{2,1,0:T(8,128)S(1)}, bf16[4,2048,1536]{2,1,0:T(8,128)(2,1)}) custom-call(s32[5]{0:T(128)S(1)} %pad_add_fusion.order, bf16[3,192,512]{2,1,0:T(8,128)(2,1)S(1)} %pad_maximum_fusion.3.mine, bf16[3,192,512]{2,1,0:T(8,128)(2,1)S(1)} %collective-permute-done.29.came, ...), custom_call_target="tpu_custom_call", output_to_operand_aliasing={{0}: (9, {}), {1}: (10, {})} | custom-call | flops 1207959552 | bytes 11010048 | tf_op jit(solution)/shard_map/post/pallas_call | solution.py:174
  210.7 12.2 %post.13 = (f32[2,192,1536]{2,1,0:T(8,128)S(1)}, bf16[4,2048,1536]{2,1,0:T(8,128)(2,1)}) custom-call(s32[5]{0:T(128)S(1)} %pad_add_fusion.order, bf16[3,192,512]{2,1,0:T(8,128)(2,1)S(1)} %pad_maximum_fusion.2.mine, bf16[3,192,512]{2,1,0:T(8,128)(2,1)S(1)} %collective-permute-done.27.came, ...), custom_call_target="tpu_custom_call", output_to_operand_aliasing={{0}: (9, {}), {1}: (10, {})} | custom-call | flops 3623878656 | bytes 23592960 | tf_op jit(solution)/shard_map/post/pallas_call | solution.py:174
  222.9 12.2 %post.14 = (f32[2,192,1536]{2,1,0:T(8,128)S(1)}, bf16[4,2048,1536]{2,1,0:T(8,128)(2,1)}) custom-call(s32[5]{0:T(128)S(1)} %pad_add_fusion.order, bf16[3,192,512]{2,1,0:T(8,128)(2,1)S(1)} %pad_maximum_fusion.1.mine, bf16[3,192,512]{2,1,0:T(8,128)(2,1)S(1)} %collective-permute-done.25.came, ...), custom_call_target="tpu_custom_call", output_to_operand_aliasing={{0}: (9, {}), {1}: (10, {})} | custom-call | flops 3623878656 | bytes 23592960 | tf_op jit(solution)/shard_map/post/pallas_call | solution.py:174
  235.1 5.8 %post.15 = (f32[2,192,1536]{2,1,0:T(8,128)S(1)}, bf16[4,2048,1536]{2,1,0:T(8,128)(2,1)}, bf16[2,24,1536]{2,1,0:T(8,128)(2,1)S(1)}, bf16[2,24,1536]{2,1,0:T(8,128...) custom-call(s32[5]{0:T(128)S(1)} %pad_add_fusion.order, ...), custom_call_target="tpu_custom_call", output_to_operand_aliasing={{0}: (9, {}), {1}: (10, {})} | custom-call | flops 1207959552 | bytes 11010048 | tf_op jit(solution)/shard_map/post/pallas_call | solution.py:174
  240.9 6.5 %collective-permute-start.38 = (bf16[2,24,1536]{2,1,0:T(8,128)(2,1)S(1)}, bf16[2,24,1536]{2,1,0:T(8,128)(2,1)S(1)}, u32[]{:S(2)}, u32[]{:S(2)}) collective-permute-start(bf16[2,24,1536]{2,1,0:T(8,128)(2,1)S(1)} %get-tuple-element.75), channel_id=1, source_target_pairs={{0,1},{1,2},{2,3},{3,4},{4,5},{5,6},{6,7},{7,0},{8,9},{9,10},{10,1... | collective-permute-start | bytes 442376 | tf_op jit(solution)/shard_map/ppermute | solution.py:300
  247.4 1.3 collective-permute-start.39
  249.8 2.9 %collective-permute-start.42 = (bf16[2,24,1536]{2,1,0:T(8,128)(2,1)S(1)}, bf16[2,24,1536]{2,1,0:T(8,128)(2,1)S(1)}, u32[]{:S(2)}, u32[]{:S(2)}) collective-permute-start(bf16[2,24,1536]{2,1,0:T(8,128)(2,1)S(1)} %get-tuple-element.79), channel_id=1, source_target_pairs={{0,5},{1,6},{2,7},{3,0},{4,1},{5,2},{6,3},{7,4},{8,13},{9,14},{10,... | collective-permute-start | bytes 442376 | tf_op jit(solution)/shard_map/ppermute | solution.py:300
  253.5 2.8 %collective-permute-done.39 = bf16[2,24,1536]{2,1,0:T(8,128)(2,1)S(1)} collective-permute-done((bf16[2,24,1536]{2,1,0:T(8,128)(2,1)S(1)}, bf16[2,24,1536]{2,1,0:T(8,128)(2,1)S(1)}, u32[]{:S(2)}, u32[]{:S(2)}) %collective-permute-start.39) | collective-permute-done | bytes 147488 | tf_op jit(solution)/shard_map/ppermute | solution.py:300
  256.3 2.0 collective-permute-done.40
  258.3 4.7 %collective-permute-done.41 = bf16[2,24,1536]{2,1,0:T(8,128)(2,1)S(1)} collective-permute-done((bf16[2,24,1536]{2,1,0:T(8,128)(2,1)S(1)}, bf16[2,24,1536]{2,1,0:T(8,128)(2,1)S(1)}, u32[]{:S(2)}, u32[]{:S(2)}) %collective-permute-start.41) | collective-permute-done | bytes 147488 | tf_op jit(solution)/shard_map/ppermute | solution.py:300
  (115 shorter events, 15.9 us)
Async XLA Ops:
  0.6 8.5 %copy-start = (s32[4]{0:T(128)S(1)}, s32[4]{0:T(128)}, u32[]{:S(2)}) copy-start(s32[4]{0:T(128)} %param.11) | copy-start | bytes 52
  0.6 11.6 %copy-start.2 = (bf16[24,1536]{1,0:T(8,128)(2,1)S(1)}, bf16[24,1536]{1,0:T(8,128)(2,1)}, u32[]{:S(2)}) copy-start(bf16[24,1536]{1,0:T(8,128)(2,1)} %param.15) | copy-start | bytes 221188
  0.7 10.8 %copy-start.3 = (bf16[24,1536]{1,0:T(8,128)(2,1)S(1)}, bf16[24,1536]{1,0:T(8,128)(2,1)}, u32[]{:S(2)}) copy-start(bf16[24,1536]{1,0:T(8,128)(2,1)} %param.8) | copy-start | bytes 221188
  0.7 11.6 %collective-permute-start.7 = (bf16[24,1536]{1,0:T(8,128)(2,1)}, bf16[24,1536]{1,0:T(8,128)(2,1)S(1)}, u32[]{:S(2)}, u32[]{:S(2)}) collective-permute-start(bf16[24,1536]{1,0:T(8,128)(2,1)} %param.15), channel_id=1, source_target_pairs={{0,7},{1,0},{2,1},{3,2},{4,3},{5,4},{6,5},{7,6},{8,15},{9,8},{10,9... | collective-permute-start | bytes 221192 | tf_op jit(solution)/shard_map/ppermute | solution.py:205
  1.4 11.4 %collective-permute-start.8 = (bf16[24,1536]{1,0:T(8,128)(2,1)}, bf16[24,1536]{1,0:T(8,128)(2,1)S(1)}, u32[]{:S(2)}, u32[]{:S(2)}) collective-permute-start(bf16[24,1536]{1,0:T(8,128)(2,1)} %param.15), channel_id=1, source_target_pairs={{0,6},{1,7},{2,0},{3,1},{4,2},{5,3},{6,4},{7,5},{8,14},{9,15},{10,... | collective-permute-start | bytes 221192 | tf_op jit(solution)/shard_map/ppermute | solution.py:205
  3.6 11.1 %collective-permute-start.9 = (bf16[24,1536]{1,0:T(8,128)(2,1)}, bf16[24,1536]{1,0:T(8,128)(2,1)S(1)}, u32[]{:S(2)}, u32[]{:S(2)}) collective-permute-start(bf16[24,1536]{1,0:T(8,128)(2,1)} %param.15), channel_id=1, source_target_pairs={{0,5},{1,6},{2,7},{3,0},{4,1},{5,2},{6,3},{7,4},{8,13},{9,14},{10,... | collective-permute-start | bytes 221192 | tf_op jit(solution)/shard_map/ppermute | solution.py:205
  4.9 9.9 %collective-permute-start.10 = (bf16[24,1536]{1,0:T(8,128)(2,1)}, bf16[24,1536]{1,0:T(8,128)(2,1)S(1)}, u32[]{:S(2)}, u32[]{:S(2)}) collective-permute-start(bf16[24,1536]{1,0:T(8,128)(2,1)} %param.15), channel_id=1, source_target_pairs={{0,4},{1,5},{2,6},{3,7},{4,0},{5,1},{6,2},{7,3},{8,12},{9,13},{10,... | collective-permute-start | bytes 221192 | tf_op jit(solution)/shard_map/ppermute | solution.py:205
  6.1 10.7 %collective-permute-start.11 = (bf16[24,1536]{1,0:T(8,128)(2,1)}, bf16[24,1536]{1,0:T(8,128)(2,1)S(1)}, u32[]{:S(2)}, u32[]{:S(2)}) collective-permute-start(bf16[24,1536]{1,0:T(8,128)(2,1)} %param.15), channel_id=1, source_target_pairs={{0,3},{1,4},{2,5},{3,6},{4,7},{5,0},{6,1},{7,2},{8,11},{9,12},{10,... | collective-permute-start | bytes 221192 | tf_op jit(solution)/shard_map/ppermute | solution.py:205
  12.2 7.6 %collective-permute-start.12 = (bf16[24,1536]{1,0:T(8,128)(2,1)S(1)}, bf16[24,1536]{1,0:T(8,128)(2,1)S(1)}, u32[]{:S(2)}, u32[]{:S(2)}) collective-permute-start(bf16[24,1536]{1,0:T(8,128)(2,1)S(1)} %copy-done.2), channel_id=1, source_target_pairs={{0,2},{1,3},{2,4},{3,5},{4,6},{5,7},{6,0},{7,1},{8,10},{9,11},{10,... | collective-permute-start | bytes 221192 | tf_op jit(solution)/shard_map/ppermute | solution.py:205
  12.8 7.3 %collective-permute-start.13 = (bf16[24,1536]{1,0:T(8,128)(2,1)S(1)}, bf16[24,1536]{1,0:T(8,128)(2,1)S(1)}, u32[]{:S(2)}, u32[]{:S(2)}) collective-permute-start(bf16[24,1536]{1,0:T(8,128)(2,1)S(1)} %copy-done.2), channel_id=1, source_target_pairs={{0,1},{1,2},{2,3},{3,4},{4,5},{5,6},{6,7},{7,0},{8,9},{9,10},{10,1... | collective-permute-start | bytes 221192 | tf_op jit(solution)/shard_map/ppermute | solution.py:205
  14.7 6.5 %collective-permute-start = (bf16[24,1536]{1,0:T(8,128)(2,1)S(1)}, bf16[24,1536]{1,0:T(8,128)(2,1)S(1)}, u32[]{:S(2)}, u32[]{:S(2)}) collective-permute-start(bf16[24,1536]{1,0:T(8,128)(2,1)S(1)} %copy-done.3), channel_id=1, source_target_pairs={{0,7},{1,0},{2,1},{3,2},{4,3},{5,4},{6,5},{7,6},{8,15},{9,8},{10,9... | collective-permute-start | bytes 221192 | tf_op jit(solution)/shard_map/ppermute | solution.py:205
  14.8 7.0 %collective-permute-start.1 = (bf16[24,1536]{1,0:T(8,128)(2,1)S(1)}, bf16[24,1536]{1,0:T(8,128)(2,1)S(1)}, u32[]{:S(2)}, u32[]{:S(2)}) collective-permute-start(bf16[24,1536]{1,0:T(8,128)(2,1)S(1)} %copy-done.3), channel_id=1, source_target_pairs={{0,6},{1,7},{2,0},{3,1},{4,2},{5,3},{6,4},{7,5},{8,14},{9,15},{10,... | collective-permute-start | bytes 221192 | tf_op jit(solution)/shard_map/ppermute | solution.py:205
  16.8 6.7 %collective-permute-start.2 = (bf16[24,1536]{1,0:T(8,128)(2,1)S(1)}, bf16[24,1536]{1,0:T(8,128)(2,1)S(1)}, u32[]{:S(2)}, u32[]{:S(2)}) collective-permute-start(bf16[24,1536]{1,0:T(8,128)(2,1)S(1)} %copy-done.3), channel_id=1, source_target_pairs={{0,5},{1,6},{2,7},{3,0},{4,1},{5,2},{6,3},{7,4},{8,13},{9,14},{10,... | collective-permute-start | bytes 221192 | tf_op jit(solution)/shard_map/ppermute | solution.py:205
  19.8 3.7 %collective-permute-start.3 = (bf16[24,1536]{1,0:T(8,128)(2,1)S(1)}, bf16[24,1536]{1,0:T(8,128)(2,1)S(1)}, u32[]{:S(2)}, u32[]{:S(2)}) collective-permute-start(bf16[24,1536]{1,0:T(8,128)(2,1)S(1)} %copy-done.3), channel_id=1, source_target_pairs={{0,4},{1,5},{2,6},{3,7},{4,0},{5,1},{6,2},{7,3},{8,12},{9,13},{10,... | collective-permute-start | bytes 221192 | tf_op jit(solution)/shard_map/ppermute | solution.py:205
  20.1 5.1 %collective-permute-start.4 = (bf16[24,1536]{1,0:T(8,128)(2,1)S(1)}, bf16[24,1536]{1,0:T(8,128)(2,1)S(1)}, u32[]{:S(2)}, u32[]{:S(2)}) collective-permute-start(bf16[24,1536]{1,0:T(8,128)(2,1)S(1)} %copy-done.3), channel_id=1, source_target_pairs={{0,3},{1,4},{2,5},{3,6},{4,7},{5,0},{6,1},{7,2},{8,11},{9,12},{10,... | collective-permute-start | bytes 221192 | tf_op jit(solution)/shard_map/ppermute | solution.py:205
  21.2 5.2 %collective-permute-start.5 = (bf16[24,1536]{1,0:T(8,128)(2,1)S(1)}, bf16[24,1536]{1,0:T(8,128)(2,1)S(1)}, u32[]{:S(2)}, u32[]{:S(2)}) collective-permute-start(bf16[24,1536]{1,0:T(8,128)(2,1)S(1)} %copy-done.3), channel_id=1, source_target_pairs={{0,2},{1,3},{2,4},{3,5},{4,6},{5,7},{6,0},{7,1},{8,10},{9,11},{10,... | collective-permute-start | bytes 221192 | tf_op jit(solution)/shard_map/ppermute | solution.py:205
  21.8 4.5 %collective-permute-start.6 = (bf16[24,1536]{1,0:T(8,128)(2,1)S(1)}, bf16[24,1536]{1,0:T(8,128)(2,1)S(1)}, u32[]{:S(2)}, u32[]{:S(2)}) collective-permute-start(bf16[24,1536]{1,0:T(8,128)(2,1)S(1)} %copy-done.3), channel_id=1, source_target_pairs={{0,1},{1,2},{2,3},{3,4},{4,5},{5,6},{6,7},{7,0},{8,9},{9,10},{10,1... | collective-permute-start | bytes 221192 | tf_op jit(solution)/shard_map/ppermute | solution.py:205
  30.2 14.7 %collective-permute-start.20 = (bf16[3,192,512]{2,1,0:T(8,128)(2,1)S(1)}, bf16[3,192,512]{2,1,0:T(8,128)(2,1)S(1)}, u32[]{:S(2)}, u32[]{:S(2)}) collective-permute-start(bf16[3,192,512]{2,1,0:T(8,128)(2,1)S(1)} %get-tuple-element.53), channel_id=1, source_target_pairs={{0,8},{24,16},{1,9},{25,17},{2,10},{26,18},{3,11},{27,19},{4,12},{... | collective-permute-start | bytes 1769480 | tf_op jit(solution)/shard_map/ppermute | solution.py:253
  40.8 17.3 %collective-permute-start.14 = (bf16[3,192,512]{2,1,0:T(8,128)(2,1)S(1)}, bf16[3,192,512]{2,1,0:T(8,128)(2,1)S(1)}, u32[]{:S(2)}, u32[]{:S(2)}) collective-permute-start(bf16[3,192,512]{2,1,0:T(8,128)(2,1)S(1)} %get-tuple-element.45), channel_id=1, source_target_pairs={{0,8},{24,16},{1,9},{25,17},{2,10},{26,18},{3,11},{27,19},{4,12},{... | collective-permute-start | bytes 1769480 | tf_op jit(solution)/shard_map/ppermute | solution.py:253
  45.1 32.3 %collective-permute-start.36 = (bf16[3,192,512]{2,1,0:T(8,128)(2,1)S(1)}, bf16[3,192,512]{2,1,0:T(8,128)(2,1)S(1)}, u32[]{:S(2)}, u32[]{:S(2)}) collective-permute-start(bf16[3,192,512]{2,1,0:T(8,128)(2,1)S(1)} %fusion.6.rest_0_), channel_id=1, source_target_pairs={{8,16},{16,8},{9,17},{17,9},{10,18},{18,10},{11,19},{19,11},{12,20... | collective-permute-start | bytes 1769480 | tf_op jit(solution)/shard_map/ppermute | solution.py:253
  58.4 48.0 %collective-permute-start.34 = (bf16[3,192,512]{2,1,0:T(8,128)(2,1)S(1)}, bf16[3,192,512]{2,1,0:T(8,128)(2,1)S(1)}, u32[]{:S(2)}, u32[]{:S(2)}) collective-permute-start(bf16[3,192,512]{2,1,0:T(8,128)(2,1)S(1)} %fusion.2.rest_0_), channel_id=1, source_target_pairs={{8,16},{16,8},{9,17},{17,9},{10,18},{18,10},{11,19},{19,11},{12,20... | collective-permute-start | bytes 1769480 | tf_op jit(solution)/shard_map/ppermute | solution.py:253
  65.5 16.7 %collective-permute-start.21 = (bf16[3,192,512]{2,1,0:T(8,128)(2,1)S(1)}, bf16[3,192,512]{2,1,0:T(8,128)(2,1)S(1)}, u32[]{:S(2)}, u32[]{:S(2)}) collective-permute-start(bf16[3,192,512]{2,1,0:T(8,128)(2,1)S(1)} %get-tuple-element.55), channel_id=1, source_target_pairs={{0,8},{24,16},{1,9},{25,17},{2,10},{26,18},{3,11},{27,19},{4,12},{... | collective-permute-start | bytes 1769480 | tf_op jit(solution)/shard_map/ppermute | solution.py:253
  76.1 17.3 %collective-permute-start.15 = (bf16[3,192,512]{2,1,0:T(8,128)(2,1)S(1)}, bf16[3,192,512]{2,1,0:T(8,128)(2,1)S(1)}, u32[]{:S(2)}, u32[]{:S(2)}) collective-permute-start(bf16[3,192,512]{2,1,0:T(8,128)(2,1)S(1)} %get-tuple-element.47), channel_id=1, source_target_pairs={{0,8},{24,16},{1,9},{25,17},{2,10},{26,18},{3,11},{27,19},{4,12},{... | collective-permute-start | bytes 1769480 | tf_op jit(solution)/shard_map/ppermute | solution.py:253
  78.0 56.0 %collective-permute-start.37 = (bf16[3,192,512]{2,1,0:T(8,128)(2,1)S(1)}, bf16[3,192,512]{2,1,0:T(8,128)(2,1)S(1)}, u32[]{:S(2)}, u32[]{:S(2)}) collective-permute-start(bf16[3,192,512]{2,1,0:T(8,128)(2,1)S(1)} %pad_maximum_fusion.7.mine), channel_id=1, source_target_pairs={{8,0},{16,24},{9,1},{17,25},{10,2},{18,26},{11,3},{19,27},{12,4},{... | collective-permute-start | bytes 1769480 | tf_op jit(solution)/shard_map/ppermute | solution.py:253
  82.3 42.3 %collective-permute-start.32 = (bf16[3,192,512]{2,1,0:T(8,128)(2,1)S(1)}, bf16[3,192,512]{2,1,0:T(8,128)(2,1)S(1)}, u32[]{:S(2)}, u32[]{:S(2)}) collective-permute-start(bf16[3,192,512]{2,1,0:T(8,128)(2,1)S(1)} %fusion.7.rest_0_), channel_id=1, source_target_pairs={{8,16},{16,8},{9,17},{17,9},{10,18},{18,10},{11,19},{19,11},{12,20... | collective-permute-start | bytes 1769480 | tf_op jit(solution)/shard_map/ppermute | solution.py:253
  93.6 34.8 %collective-permute-start.30 = (bf16[3,192,512]{2,1,0:T(8,128)(2,1)S(1)}, bf16[3,192,512]{2,1,0:T(8,128)(2,1)S(1)}, u32[]{:S(2)}, u32[]{:S(2)}) collective-permute-start(bf16[3,192,512]{2,1,0:T(8,128)(2,1)S(1)} %fusion.3.rest_0_), channel_id=1, source_target_pairs={{8,16},{16,8},{9,17},{17,9},{10,18},{18,10},{11,19},{19,11},{12,20... | collective-permute-start | bytes 1769480 | tf_op jit(solution)/shard_map/ppermute | solution.py:253
  105.1 14.2 %collective-permute-start.16 = (bf16[3,192,512]{2,1,0:T(8,128)(2,1)S(1)}, bf16[3,192,512]{2,1,0:T(8,128)(2,1)S(1)}, u32[]{:S(2)}, u32[]{:S(2)}) collective-permute-start(bf16[3,192,512]{2,1,0:T(8,128)(2,1)S(1)} %get-tuple-element.49), channel_id=1, source_target_pairs={{0,8},{24,16},{1,9},{25,17},{2,10},{26,18},{3,11},{27,19},{4,12},{... | collective-permute-start | bytes 1769480 | tf_op jit(solution)/shard_map/ppermute | solution.py:253
  107.0 45.1 %collective-permute-start.35 = (bf16[3,192,512]{2,1,0:T(8,128)(2,1)S(1)}, bf16[3,192,512]{2,1,0:T(8,128)(2,1)S(1)}, u32[]{:S(2)}, u32[]{:S(2)}) collective-permute-start(bf16[3,192,512]{2,1,0:T(8,128)(2,1)S(1)} %pad_maximum_fusion.6.mine), channel_id=1, source_target_pairs={{8,0},{16,24},{9,1},{17,25},{10,2},{18,26},{11,3},{19,27},{12,4},{... | collective-permute-start | bytes 1769480 | tf_op jit(solution)/shard_map/ppermute | solution.py:253
  119.2 13.2 %collective-permute-start.22 = (bf16[3,192,512]{2,1,0:T(8,128)(2,1)S(1)}, bf16[3,192,512]{2,1,0:T(8,128)(2,1)S(1)}, u32[]{:S(2)}, u32[]{:S(2)}) collective-permute-start(bf16[3,192,512]{2,1,0:T(8,128)(2,1)S(1)} %get-tuple-element.57), channel_id=1, source_target_pairs={{0,8},{24,16},{1,9},{25,17},{2,10},{26,18},{3,11},{27,19},{4,12},{... | collective-permute-start | bytes 1769480 | tf_op jit(solution)/shard_map/ppermute | solution.py:253
  124.6 42.9 %collective-permute-start.26 = (bf16[3,192,512]{2,1,0:T(8,128)(2,1)S(1)}, bf16[3,192,512]{2,1,0:T(8,128)(2,1)S(1)}, u32[]{:S(2)}, u32[]{:S(2)}) collective-permute-start(bf16[3,192,512]{2,1,0:T(8,128)(2,1)S(1)} %fusion.4.rest_0_), channel_id=1, source_target_pairs={{8,16},{16,8},{9,17},{17,9},{10,18},{18,10},{11,19},{19,11},{12,20... | collective-permute-start | bytes 1769480 | tf_op jit(solution)/shard_map/ppermute | solution.py:253
  128.4 51.3 %collective-permute-start.33 = (bf16[3,192,512]{2,1,0:T(8,128)(2,1)S(1)}, bf16[3,192,512]{2,1,0:T(8,128)(2,1)S(1)}, u32[]{:S(2)}, u32[]{:S(2)}) collective-permute-start(bf16[3,192,512]{2,1,0:T(8,128)(2,1)S(1)} %pad_maximum_fusion.5.mine), channel_id=1, source_target_pairs={{8,0},{16,24},{9,1},{17,25},{10,2},{18,26},{11,3},{19,27},{12,4},{... | collective-permute-start | bytes 1769480 | tf_op jit(solution)/shard_map/ppermute | solution.py:253
  132.5 56.2 %collective-permute-start.31 = (bf16[3,192,512]{2,1,0:T(8,128)(2,1)S(1)}, bf16[3,192,512]{2,1,0:T(8,128)(2,1)S(1)}, u32[]{:S(2)}, u32[]{:S(2)}) collective-permute-start(bf16[3,192,512]{2,1,0:T(8,128)(2,1)S(1)} %pad_maximum_fusion.4.mine), channel_id=1, source_target_pairs={{8,0},{16,24},{9,1},{17,25},{10,2},{18,26},{11,3},{19,27},{12,4},{... | collective-permute-start | bytes 1769480 | tf_op jit(solution)/shard_map/ppermute | solution.py:253
  134.0 31.6 %collective-permute-start.28 = (bf16[3,192,512]{2,1,0:T(8,128)(2,1)S(1)}, bf16[3,192,512]{2,1,0:T(8,128)(2,1)S(1)}, u32[]{:S(2)}, u32[]{:S(2)}) collective-permute-start(bf16[3,192,512]{2,1,0:T(8,128)(2,1)S(1)} %fusion.8.rest_0_), channel_id=1, source_target_pairs={{8,16},{16,8},{9,17},{17,9},{10,18},{18,10},{11,19},{19,11},{12,20... | collective-permute-start | bytes 1769480 | tf_op jit(solution)/shard_map/ppermute | solution.py:253
  152.1 20.1 %collective-permute-start.23 = (bf16[3,192,512]{2,1,0:T(8,128)(2,1)S(1)}, bf16[3,192,512]{2,1,0:T(8,128)(2,1)S(1)}, u32[]{:S(2)}, u32[]{:S(2)}) collective-permute-start(bf16[3,192,512]{2,1,0:T(8,128)(2,1)S(1)} %get-tuple-element.59), channel_id=1, source_target_pairs={{0,8},{24,16},{1,9},{25,17},{2,10},{26,18},{3,11},{27,19},{4,12},{... | collective-permute-start | bytes 1769480 | tf_op jit(solution)/shard_map/ppermute | solution.py:253
  165.6 11.9 %collective-permute-start.17 = (bf16[3,192,512]{2,1,0:T(8,128)(2,1)S(1)}, bf16[3,192,512]{2,1,0:T(8,128)(2,1)S(1)}, u32[]{:S(2)}, u32[]{:S(2)}) collective-permute-start(bf16[3,192,512]{2,1,0:T(8,128)(2,1)S(1)} %get-tuple-element.51), channel_id=1, source_target_pairs={{0,8},{24,16},{1,9},{25,17},{2,10},{26,18},{3,11},{27,19},{4,12},{... | collective-permute-start | bytes 1769480 | tf_op jit(solution)/shard_map/ppermute | solution.py:253
  167.5 37.5 %collective-permute-start.29 = (bf16[3,192,512]{2,1,0:T(8,128)(2,1)S(1)}, bf16[3,192,512]{2,1,0:T(8,128)(2,1)S(1)}, u32[]{:S(2)}, u32[]{:S(2)}) collective-permute-start(bf16[3,192,512]{2,1,0:T(8,128)(2,1)S(1)} %pad_maximum_fusion.3.mine), channel_id=1, source_target_pairs={{8,0},{16,24},{9,1},{17,25},{10,2},{18,26},{11,3},{19,27},{12,4},{... | collective-permute-start | bytes 1769480 | tf_op jit(solution)/shard_map/ppermute | solution.py:253
  172.2 38.5 %collective-permute-start.27 = (bf16[3,192,512]{2,1,0:T(8,128)(2,1)S(1)}, bf16[3,192,512]{2,1,0:T(8,128)(2,1)S(1)}, u32[]{:S(2)}, u32[]{:S(2)}) collective-permute-start(bf16[3,192,512]{2,1,0:T(8,128)(2,1)S(1)} %pad_maximum_fusion.2.mine), channel_id=1, source_target_pairs={{8,0},{16,24},{9,1},{17,25},{10,2},{18,26},{11,3},{19,27},{12,4},{... | collective-permute-start | bytes 1769480 | tf_op jit(solution)/shard_map/ppermute | solution.py:253
  177.5 23.4 %collective-permute-start.24 = (bf16[3,192,512]{2,1,0:T(8,128)(2,1)S(1)}, bf16[3,192,512]{2,1,0:T(8,128)(2,1)S(1)}, u32[]{:S(2)}, u32[]{:S(2)}) collective-permute-start(bf16[3,192,512]{2,1,0:T(8,128)(2,1)S(1)} %fusion.9), channel_id=1, source_target_pairs={{8,16},{16,8},{9,17},{17,9},{10,18},{18,10},{11,19},{19,11},{12,20... | collective-permute-start | bytes 1769480 | tf_op jit(solution)/shard_map/ppermute | solution.py:253
  179.8 23.1 %collective-permute-start.18 = (bf16[3,192,512]{2,1,0:T(8,128)(2,1)S(1)}, bf16[3,192,512]{2,1,0:T(8,128)(2,1)S(1)}, u32[]{:S(2)}, u32[]{:S(2)}) collective-permute-start(bf16[3,192,512]{2,1,0:T(8,128)(2,1)S(1)} %fusion.5), channel_id=1, source_target_pairs={{8,16},{16,8},{9,17},{17,9},{10,18},{18,10},{11,19},{19,11},{12,20... | collective-permute-start | bytes 1769480 | tf_op jit(solution)/shard_map/ppermute | solution.py:253
  201.5 21.4 %collective-permute-start.25 = (bf16[3,192,512]{2,1,0:T(8,128)(2,1)S(1)}, bf16[3,192,512]{2,1,0:T(8,128)(2,1)S(1)}, u32[]{:S(2)}, u32[]{:S(2)}) collective-permute-start(bf16[3,192,512]{2,1,0:T(8,128)(2,1)S(1)} %pad_maximum_fusion.1.mine), channel_id=1, source_target_pairs={{8,0},{16,24},{9,1},{17,25},{10,2},{18,26},{11,3},{19,27},{12,4},{... | collective-permute-start | bytes 1769480 | tf_op jit(solution)/shard_map/ppermute | solution.py:253
  203.5 31.7 %collective-permute-start.19 = (bf16[3,192,512]{2,1,0:T(8,128)(2,1)S(1)}, bf16[3,192,512]{2,1,0:T(8,128)(2,1)S(1)}, u32[]{:S(2)}, u32[]{:S(2)}) collective-permute-start(bf16[3,192,512]{2,1,0:T(8,128)(2,1)S(1)} %pad_maximum_fusion.mine), channel_id=1, source_target_pairs={{8,0},{16,24},{9,1},{17,25},{10,2},{18,26},{11,3},{19,27},{12,4},{... | collective-permute-start | bytes 1769480 | tf_op jit(solution)/shard_map/ppermute | solution.py:253
  235.1 28.8 %copy-start.1 = (s32[4]{0:T(128)S(1)}, s32[4]{0:T(128)}, u32[]{:S(2)}) copy-start(s32[4]{0:T(128)} %param.11) | copy-start | bytes 52
  240.9 11.8 %collective-permute-start.38 = (bf16[2,24,1536]{2,1,0:T(8,128)(2,1)S(1)}, bf16[2,24,1536]{2,1,0:T(8,128)(2,1)S(1)}, u32[]{:S(2)}, u32[]{:S(2)}) collective-permute-start(bf16[2,24,1536]{2,1,0:T(8,128)(2,1)S(1)} %get-tuple-element.75), channel_id=1, source_target_pairs={{0,1},{1,2},{2,3},{3,4},{4,5},{5,6},{6,7},{7,0},{8,9},{9,10},{10,1... | collective-permute-start | bytes 442376 | tf_op jit(solution)/shard_map/ppermute | solution.py:300
  247.4 8.9 %collective-permute-start.39 = (bf16[2,24,1536]{2,1,0:T(8,128)(2,1)S(1)}, bf16[2,24,1536]{2,1,0:T(8,128)(2,1)S(1)}, u32[]{:S(2)}, u32[]{:S(2)}) collective-permute-start(bf16[2,24,1536]{2,1,0:T(8,128)(2,1)S(1)} %get-tuple-element.76), channel_id=1, source_target_pairs={{0,2},{1,3},{2,4},{3,5},{4,6},{5,7},{6,0},{7,1},{8,10},{9,11},{10,... | collective-permute-start | bytes 442376 | tf_op jit(solution)/shard_map/ppermute | solution.py:300
  248.7 9.6 %collective-permute-start.40 = (bf16[2,24,1536]{2,1,0:T(8,128)(2,1)S(1)}, bf16[2,24,1536]{2,1,0:T(8,128)(2,1)S(1)}, u32[]{:S(2)}, u32[]{:S(2)}) collective-permute-start(bf16[2,24,1536]{2,1,0:T(8,128)(2,1)S(1)} %get-tuple-element.77), channel_id=1, source_target_pairs={{0,3},{1,4},{2,5},{3,6},{4,7},{5,0},{6,1},{7,2},{8,11},{9,12},{10,... | collective-permute-start | bytes 442376 | tf_op jit(solution)/shard_map/ppermute | solution.py:300
  249.5 13.6 %collective-permute-start.41 = (bf16[2,24,1536]{2,1,0:T(8,128)(2,1)S(1)}, bf16[2,24,1536]{2,1,0:T(8,128)(2,1)S(1)}, u32[]{:S(2)}, u32[]{:S(2)}) collective-permute-start(bf16[2,24,1536]{2,1,0:T(8,128)(2,1)S(1)} %get-tuple-element.78), channel_id=1, source_target_pairs={{0,4},{1,5},{2,6},{3,7},{4,0},{5,1},{6,2},{7,3},{8,12},{9,13},{10,... | collective-permute-start | bytes 442376 | tf_op jit(solution)/shard_map/ppermute | solution.py:300
  249.8 13.3 %collective-permute-start.42 = (bf16[2,24,1536]{2,1,0:T(8,128)(2,1)S(1)}, bf16[2,24,1536]{2,1,0:T(8,128)(2,1)S(1)}, u32[]{:S(2)}, u32[]{:S(2)}) collective-permute-start(bf16[2,24,1536]{2,1,0:T(8,128)(2,1)S(1)} %get-tuple-element.79), channel_id=1, source_target_pairs={{0,5},{1,6},{2,7},{3,0},{4,1},{5,2},{6,3},{7,4},{8,13},{9,14},{10,... | collective-permute-start | bytes 442376 | tf_op jit(solution)/shard_map/ppermute | solution.py:300
  252.7 10.4 %collective-permute-start.43 = (bf16[2,24,1536]{2,1,0:T(8,128)(2,1)S(1)}, bf16[2,24,1536]{2,1,0:T(8,128)(2,1)S(1)}, u32[]{:S(2)}, u32[]{:S(2)}) collective-permute-start(bf16[2,24,1536]{2,1,0:T(8,128)(2,1)S(1)} %get-tuple-element.80), channel_id=1, source_target_pairs={{0,6},{1,7},{2,0},{3,1},{4,2},{5,3},{6,4},{7,5},{8,14},{9,15},{10,... | collective-permute-start | bytes 442376 | tf_op jit(solution)/shard_map/ppermute | solution.py:300
  256.3 6.8 %collective-permute-start.44 = (bf16[2,24,1536]{2,1,0:T(8,128)(2,1)S(1)}, bf16[2,24,1536]{2,1,0:T(8,128)(2,1)S(1)}, u32[]{:S(2)}, u32[]{:S(2)}) collective-permute-start(bf16[2,24,1536]{2,1,0:T(8,128)(2,1)S(1)} %get-tuple-element.81), channel_id=1, source_target_pairs={{0,7},{1,0},{2,1},{3,2},{4,3},{5,4},{6,5},{7,6},{8,15},{9,8},{10,9... | collective-permute-start | bytes 442376 | tf_op jit(solution)/shard_map/ppermute | solution.py:300

commit v2 on v0

v2 whole, which is shorter than its diff:
```python
import functools

import jax
import jax.numpy as jnp
import numpy as np
from jax import lax
from jax.experimental import pallas as pl
from jax.experimental.pallas import tpu as pltpu
from jax.sharding import PartitionSpec as P

SUB = 256
SLOTS = 4
F32 = jnp.float32
BF16 = jnp.bfloat16
COST_SCALE = 16
VMEM_LIMIT = 40 * 1024 * 1024
ANY = pl.BlockSpec(memory_space=pl.ANY)
VMEM = pl.BlockSpec(memory_space=pltpu.VMEM)
EXPERT, UNIT, GROUP, COLUMN, FIRST, LAST, FIELDS = 0, 1, 2, 3, 4, 5, 6


def dot(a, b, contract):
    return lax.dot_general(a, b, ((contract[0], contract[1]), ((), ())), preferred_element_type=F32)


def weight_copies(field, i, weights, buffers, sems):
    slot = lax.rem(i, SLOTS)
    expert = field(i, EXPERT)
    units = pl.ds(pl.multiple_of(field(i, COLUMN), SUB), SUB)
    wg, wu, wd = weights
    return (
        pltpu.make_async_copy(wg.at[expert, :, units], buffers[0].at[slot], sems.at[slot, 0]),
        pltpu.make_async_copy(wu.at[expert, :, units], buffers[1].at[slot], sems.at[slot, 1]),
        pltpu.make_async_copy(wd.at[expert, units, :], buffers[2].at[slot], sems.at[slot, 2]),
    )


def begin_all(copies):
    for copy in copies:
        copy.start()


def wait_all(copies):
    for copy in copies:
        copy.wait()


def partial_kernel(base, blocks, units, deps, table, other, x, rg, wg, wu, wd, *rest):
    own, send, zero, xv, rgv, b0, b1, b2, ownv, sendv, wsem, isem, osem = rest[deps:]
    zero[...] = jnp.zeros_like(zero)
    field = lambda i, n: table[(base + i) * FIELDS + n]
    fetch = lambda i: weight_copies(field, i, (wg, wu, wd), (b0, b1, b2), wsem)
    inputs = (pltpu.make_async_copy(x, xv, isem.at[0]), pltpu.make_async_copy(rg, rgv, isem.at[1]))
    inputs[0].start()
    begin_all(fetch(0))
    inputs[1].start()
    for i in range(1, min(SLOTS - 1, blocks)):
        begin_all(fetch(i))
    wait_all(inputs)

    def leave(unit):
        return (
            pltpu.make_async_copy(ownv.at[unit], own.at[unit], osem.at[unit, 0]),
            pltpu.make_async_copy(sendv.at[unit], send.at[unit], osem.at[unit, 1]),
        )

    def body(i, carry):
        @pl.when(i + (SLOTS - 1) < blocks)
        def _():
            begin_all(fetch(i + (SLOTS - 1)))

        wait_all(fetch(i))
        slot, unit, group = lax.rem(i, SLOTS), field(i, UNIT), field(i, GROUP)
        keep = jnp.logical_or(other[...] == field(i, EXPERT), field(i, FIRST) == 1)
        terms = (
            dot(xv[...], b0[slot], ((1,), (0,))),
            dot(xv[...], b1[slot], ((1,), (0,))),
            dot(rgv[group], b2[slot], ((1,), (1,))),
        )
        for n, term in enumerate(terms):
            ownv[unit, n] = jnp.where(keep, term, ownv[unit, n])

        @pl.when(field(i, LAST) == 1)
        def _():
            for n in range(3):
                sendv[unit, n] = ownv[unit, n].astype(BF16)
            begin_all(leave(unit))

        return carry

    lax.fori_loop(0, blocks, body, 0)
    for unit in range(units):
        wait_all(leave(unit))


def partial_products(base, blocks, units, table, x, rg, other, weights, after):
    experts, depth, _ = weights[0].shape
    rows = x.shape[0]
    shape = (units, 3, rows, SUB)
    return pl.pallas_call(
        functools.partial(partial_kernel, base, blocks, units, len(after)),
        grid_spec=pltpu.PrefetchScalarGridSpec(
            num_scalar_prefetch=1,
            grid=(),
            in_specs=[VMEM] + [ANY] * (5 + len(after)),
            out_specs=[ANY, ANY, VMEM],
            scratch_shapes=[
                pltpu.VMEM((rows, depth), BF16),
                pltpu.VMEM((2, rows, depth), BF16),
                pltpu.VMEM((SLOTS, depth, SUB), BF16),
                pltpu.VMEM((SLOTS, depth, SUB), BF16),
                pltpu.VMEM((SLOTS, SUB, depth), BF16),
                pltpu.VMEM(shape, F32),
                pltpu.VMEM(shape, BF16),
                pltpu.SemaphoreType.DMA((SLOTS, 3)),
                pltpu.SemaphoreType.DMA((2,)),
                pltpu.SemaphoreType.DMA((units, 2)),
            ],
        ),
        out_shape=[
            jax.ShapeDtypeStruct(shape, F32),
            jax.ShapeDtypeStruct(shape, BF16),
            jax.ShapeDtypeStruct((1, SUB), F32),
        ],
        compiler_params=pltpu.CompilerParams(vmem_limit_bytes=VMEM_LIMIT),
        cost_estimate=pl.CostEstimate(
            flops=6 * rows * depth * SUB * blocks // COST_SCALE,
            bytes_accessed=6 * depth * SUB * blocks // COST_SCALE,
            transcendentals=0,
        ),
        name="partial",
    )(table, other, x, rg, *weights, *after)


def post_kernel(base, blocks, units, deps, opening, closing, table, other, weight, mine, came, rg, wg, wu, wd, *rest):
    if not opening:
        sums_in, rest = rest[0], rest[2:]
    outs, scratch = rest[deps : deps + 3], rest[deps + 3 :]
    d_down = outs[0]
    if not closing:
        outs[2][...] = jnp.zeros_like(outs[2])
    act, rgv, b0, b1, b2, sums, ddv, wsem, isem, dsem = scratch
    field = lambda i, n: table[(base + i) * FIELDS + n]
    edge = table[table.shape[0] - 1]
    fetch = lambda i: weight_copies(field, i, (wg, wu, wd), (b0, b1, b2), wsem)
    take_mine = pltpu.make_async_copy(mine, act, isem.at[0])
    take_came = pltpu.make_async_copy(came, act, isem.at[0])
    take_rg = pltpu.make_async_copy(rg, rgv, isem.at[1])

    @pl.when(edge == 1)
    def _():
        take_came.start()

    @pl.when(edge == 0)
    def _():
        take_mine.start()

    begin_all(fetch(0))
    take_rg.start()
    if opening:
        sums[...] = jnp.zeros_like(sums)
    else:
        take_sums = pltpu.make_async_copy(sums_in, sums, isem.at[2])
        take_sums.start()
    for i in range(1, min(SLOTS - 1, blocks)):
        begin_all(fetch(i))
    take_mine.wait()
    take_rg.wait()
    if not opening:
        take_sums.wait()

    def leave(i):
        slot = lax.rem(i, 2)
        units = pl.ds(pl.multiple_of(field(i, COLUMN), SUB), SUB)
        return pltpu.make_async_copy(ddv.at[slot], d_down.at[field(i, EXPERT), units, :], dsem.at[slot])

    def body(i, carry):
        @pl.when(i + (SLOTS - 1) < blocks)
        def _():
            begin_all(fetch(i + (SLOTS - 1)))

        wait_all(fetch(i))

        @pl.when(i >= 2)
        def _():
            leave(i - 2).wait()

        slot, unit, group = lax.rem(i, SLOTS), field(i, UNIT), field(i, GROUP)
        keep = jnp.logical_or(other[...] == field(i, EXPERT), group == 0)
        hidden, d_gate, d_up = (
            jnp.where(keep, act[unit, n], jnp.zeros(act.shape[2:], BF16)) for n in range(3)
        )
        sums[0] += weight[group] * dot(hidden, b2[slot], ((1,), (0,)))
        sums[1] += dot(d_gate, b0[slot], ((1,), (1,))) + dot(d_up, b1[slot], ((1,), (1,)))
        ddv[lax.rem(i, 2)] = dot(hidden, rgv[group], ((0,), (0,))).astype(BF16)
        leave(i).start()
        return carry

    lax.fori_loop(0, blocks, body, 0)
    if closing:
        half = sums.shape[1] // 2
        outs[1][...] = sums[:, :half]
        outs[2][...] = sums[:, half:]
    else:
        put = pltpu.make_async_copy(sums, outs[1], isem.at[2])
        put.start()
    for i in range(max(blocks - 2, 0), blocks):
        leave(i).wait()
    if not closing:
        put.wait()


def post_products(base, blocks, units, table, mine, came, rg, weight, other, weights, state, after, closing):
    experts, depth, width = weights[0].shape
    rows = rg.shape[1]
    opening = state is None
    operands = [table, other, weight, mine, came, rg, *weights]
    in_specs = [VMEM, VMEM] + [ANY] * 6
    aliases = {}
    if not opening:
        aliases = {len(operands) + 1: 0}
        if not closing:
            aliases[len(operands)] = 1
        in_specs += [ANY, ANY]
        operands += [state[1], state[0]]
    in_specs += [ANY] * len(after)
    operands += list(after)
    out_shape = [jax.ShapeDtypeStruct((experts, width, depth), BF16)]
    out_specs = [ANY]
    if closing:
        out_shape += [jax.ShapeDtypeStruct((2, rows // 2, depth), F32)] * 2
        out_specs += [VMEM] * 2
    else:
        out_shape += [jax.ShapeDtypeStruct((2, rows, depth), F32), jax.ShapeDtypeStruct((1, SUB), F32)]
        out_specs += [ANY, VMEM]
    return pl.pallas_call(
        functools.partial(post_kernel, base, blocks, units, len(after), opening, closing),
        grid_spec=pltpu.PrefetchScalarGridSpec(
            num_scalar_prefetch=1,
            grid=(),
            in_specs=in_specs,
            out_specs=out_specs,
            scratch_shapes=[
                pltpu.VMEM((units, 3, rows, SUB), BF16),
                pltpu.VMEM((2, rows, depth), BF16),
                pltpu.VMEM((SLOTS, depth, SUB), BF16),
                pltpu.VMEM((SLOTS, depth, SUB), BF16),
                pltpu.VMEM((SLOTS, SUB, depth), BF16),
                pltpu.VMEM((2, rows, depth), F32),
                pltpu.VMEM((2, SUB, depth), BF16),
                pltpu.SemaphoreType.DMA((SLOTS, 3)),
                pltpu.SemaphoreType.DMA((3,)),
                pltpu.SemaphoreType.DMA((2,)),
            ],
        ),
        out_shape=out_shape,
        input_output_aliases=aliases,
        compiler_params=pltpu.CompilerParams(vmem_limit_bytes=VMEM_LIMIT),
        cost_estimate=pl.CostEstimate(
            flops=8 * rows * depth * SUB * blocks // COST_SCALE,
            bytes_accessed=8 * depth * SUB * blocks // COST_SCALE,
            transcendentals=0,
        ),
        name="post",
    )(*operands)


def activations(gate, up, d_hidden):
    sigmoid = jax.nn.sigmoid(gate)
    active = gate * sigmoid
    hidden = (active * up).astype(BF16)
    d_gate = (d_hidden * up * sigmoid * (1.0 + gate * (1.0 - sigmoid))).astype(BF16)
    d_up = (d_hidden * active).astype(BF16)
    return jnp.stack([hidden, d_gate, d_up], 1)


def chunk_plan(units):
    starts = list(range(0, units, SUB))
    first = [(0, s) for s in starts]
    second = [(1, s) for s in starts]
    if len(starts) < 8:
        return [[a, b] for a, b in zip(first, second)]
    head, tail, spare = first[:3], first[-2:], first[3:-2]
    plan = [head]
    groups = -(-len(second) // 2)
    for n in range(groups):
        extra = spare[n * len(spare) // (groups - 1) : (n + 1) * len(spare) // (groups - 1)] if n < groups - 1 else []
        plan.append(second[2 * n : 2 * n + 2] + extra)
    return plan + [tail]


def block_table(plan, experts):
    rows, spans = [], []
    for chunk in plan:
        base = len(rows)
        for unit, (group, start) in enumerate(chunk):
            ranks = [0] if group == 0 else list(range(1, experts))
            for rank in ranks:
                rows.append((rank, unit, group, start, int(rank == ranks[0]), int(rank == ranks[-1])))
        spans.append((base, len(rows) - base, len(chunk)))
    return np.array(rows, np.int32), spans


def sequence(count):
    steps = [("partial", k) for k in range(min(3, count))]
    for k in range(count + 2):
        if k < count and not (count == 6 and k == 5):
            steps.append(("merge", k))
        if 1 <= k <= count and not (count == 6 and k == 6):
            steps.append(("finish", k - 1))
        if count == 6 and k == 4:
            steps.append(("merge", 5))
        if count == 6 and k == 5:
            steps.append(("finish", 5))
        if k >= 2:
            steps.append(("post", k - 2))
        if k + 3 < count:
            steps.append(("partial", k + 3))
    return steps


def on_device(sections, parts, tokens, combine, expert_ids, expert_counts, w_gate, w_up, w_down, cotangent):
    total = combine.shape[0]
    local = tokens.shape[0]
    experts = w_gate.shape[0]
    weights = (w_gate, w_up, w_down)
    chips = parts // 2
    me = lax.axis_index("tensor")
    place = lax.axis_index("section")
    chip, core = me // 2, me % 2

    pair = jnp.stack([tokens, cotangent], 0)
    near = jnp.concatenate(
        [pair]
        + [lax.ppermute(pair, "tensor", [(i, (i - 2 * n) % parts) for i in range(parts)]) for n in range(1, chips)],
        1,
    )
    swap = [(i, i ^ 1) for i in range(parts)]
    far = lax.ppermute(near, "tensor", swap)
    full = jnp.concatenate([near, far], 1)
    x, cot = full[0], full[1]

    def turned(v):
        v = v.reshape(chips, 2, local, v.shape[1])
        v = jnp.where(core == 1, v[:, ::-1], v).transpose(1, 0, 2, 3)
        v = lax.dynamic_slice_in_dim(jnp.concatenate([v, v], 1), chip, chips, 1)
        return v.reshape(total, v.shape[3])

    scale, ids = turned(combine), turned(expert_ids)
    common = jnp.argmax(expert_counts).astype(jnp.int32)
    is_first = ids[:, :1] == common
    other = jnp.where(is_first, ids[:, 1:], ids[:, :1])
    weight = jnp.stack(
        [
            jnp.where(is_first, scale[:, :1], scale[:, 1:]),
            jnp.where(is_first, scale[:, 1:], scale[:, :1]),
        ],
        0,
    )
    rg = (weight * cot.astype(F32)[None]).astype(BF16)

    plan = chunk_plan(w_gate.shape[2])
    rows, spans = block_table(plan, experts)
    line = sections == 4
    edge = jnp.logical_or(place == 0, place == sections - 1) if line else jnp.zeros((), bool)
    rank = jnp.asarray(rows[:, EXPERT])
    expert = jnp.where(rank == 0, common, rank - (rank <= common).astype(jnp.int32))
    table = jnp.concatenate([expert[:, None], jnp.asarray(rows[:, 1:])], 1).reshape(-1)
    table = jnp.concatenate([table, edge.astype(jnp.int32)[None]])

    count = len(plan)
    own, sent, summed, mine, came = {}, {}, {}, {}, {}
    state = None
    after = ()

    def send(v, pairs):
        return lax.ppermute(v, "section", pairs)

    for name, k in sequence(count):
        if name == "partial":
            own[k], packed, zero = partial_products(*spans[k], table, x, rg, other, weights, after)
            sent[k] = send(packed, [(0, 1), (3, 2)]) if line else None
            after = (zero,)
        elif name == "merge" and line:
            summed[k] = own[k] + (sent[k].astype(F32) + zero)
            packed = summed[k].astype(BF16)
            sent[k] = send(packed, [(1, 2), (2, 1)])
            after += (packed,)
        elif name == "finish" and line:
            all_of = summed[k] + (sent[k].astype(F32) + zero)
            mine[k] = activations(all_of[:, 0], all_of[:, 1], all_of[:, 2])
            came[k] = send(mine[k], [(1, 0), (2, 3)])
            after += (mine[k],)
        elif name == "finish":
            all_of = lax.psum(own[k], "section")
            mine[k] = came[k] = activations(all_of[:, 0], all_of[:, 1], all_of[:, 2])
        elif name == "post":
            *state, zero = post_products(
                *spans[k], table, mine[k], came[k], rg, weight, other, weights, state, after, k == count - 1
            )
            after = (zero,)
    (d_down, keep), give = state, zero
    both = keep + lax.ppermute(give, "tensor", swap)
    result = both[:, :local]
    for n in range(1, chips):
        piece = both[:, n * local : (n + 1) * local].astype(BF16)
        result += lax.ppermute(piece, "tensor", [(i, (i + 2 * n) % parts) for i in range(parts)]).astype(F32)
    return result[0].astype(BF16), result[1].astype(BF16), d_down


def solution(mesh):
    in_specs = (
        P("tensor", "section"),
        P(),
        P(),
        P(),
        P(None, "section", "tensor"),
        P(None, "section", "tensor"),
        P(None, "tensor", "section"),
        P("tensor", "section"),
    )
    out_specs = (P("tensor", "section"), P("tensor", "section"), P(None, "tensor", "section"))
    return jax.shard_map(
        functools.partial(on_device, mesh.shape["section"], mesh.shape["tensor"]),
        mesh=mesh,
        in_specs=in_specs,
        out_specs=out_specs,
        check_vma=False,
    )
```

time: 986 us -> 206 us (0.21); the launches traced: 975 us -> 205 us
  matrix products: 388 us -> 0 us
  waiting for transfers between devices: 331 us -> 32.8 us
  local copies, waits for them, and re-layouts: 107 us -> 2.86 us
  Pallas kernels: 0 us -> 98 us
  loops' own time: 80.1 us -> 0 us
  starting transfers between devices: 0.9 us -> 60.3 us
  other arithmetic: 32.1 us -> 10.1 us
  blocking collectives: 21.4 us -> 0 us
  between operations: 14.5 us -> 1.34 us
    dot_general x44 -> x0, matrix products: 388 us -> none  [the longest x21 127 us: apply_block(): lax.dot_general(segment, matrix, (((1,), (1,)), ((), ())), preferred_elem...]
    reduce_scatter x5 -> x0, waiting for transfers between devices: 250 us -> none  [the longest x1 131 us: on_device(): lax.psum_scatter(up_part, 'section', scatter_dimension=1, tiled=True)]
    pallas_call x0 -> x12, Pallas kernels: none -> 98 us  [the longest x6 55.8 us: post_products(): pl.pallas_call(functools.partial(post_kernel, base, blocks, units, len(af...]
    another operation x6 -> x0, loops' own time: 80.1 us -> none  [blocked_product(): result = lax.map(apply_block, (blocks, block_expert))]
    all_gather x3 -> x0, waiting for transfers between devices: 79.5 us -> none  [the longest x1 71.2 us: on_device(): lax.all_gather(up_share, 'section', axis=1, tiled=True)]
    ppermute x0 -> x26, starting transfers between devices: none -> 60.3 us  [the longest x18 50.6 us: send(): return lax.ppermute(v, 'section', pairs)]
    ppermute x0 -> x26, waiting for transfers between devices: none -> 32.8 us  [the longest x18 20.9 us: send(): return lax.ppermute(v, 'section', pairs)]
    gather x6 -> x0, local copies, waits for them, and re-layouts: 28.9 us -> none  [the longest x2 10.7 us: on_device(): grad_terms = jnp.sum(d_rows[slot_pairs], 1)]
  transfers between devices with their start and end apart: 8 -> 26, of which waited for: 4 -> 10; matrix products, arithmetic and copies ran while one was open for 48% -> 5% of each run, Pallas kernels for 0% -> 42%
where the time goes in v2:
time: 206 us; the launch traced here: 205 us
  Pallas kernels  98 us (48%)
  starting transfers between devices  60.3 us (29%)
  waiting for transfers between devices  32.8 us (16%)
  other arithmetic  10.1 us (5%)
  local copies, waits for them, and re-layouts  2.86 us (1%)
    pallas_call x6, Pallas kernels, post_products(): pl.pallas_call(functools.partial(post_kernel, base, blocks, units, len(af...  55.8 us
    ppermute x18, starting transfers between devices, send(): return lax.ppermute(v, 'section', pairs)  50.6 us
    pallas_call x6, Pallas kernels, partial_products(): pl.pallas_call(functools.partial(partial_kernel, base, blocks, units, len...  42.2 us
    ppermute x18, waiting for transfers between devices, send(): return lax.ppermute(v, 'section', pairs)  20.9 us
    ppermute x3, waiting for transfers between devices, on_device(): lax.ppermute(piece, 'tensor', [(i, (i + 2 * n) % parts) for i in range(pa...  5.56 us
    ppermute x3, starting transfers between devices, on_device(): lax.ppermute(pair, 'tensor', [(i, (i - 2 * n) % parts) for i in range(par...  5.06 us
    ppermute x3, starting transfers between devices, on_device(): lax.ppermute(piece, 'tensor', [(i, (i + 2 * n) % parts) for i in range(pa...  4.5 us
  transfers between devices with their start and end apart: 26, of which 10 were waited for; matrix products, arithmetic and copies ran while one was open for 5% of the time, Pallas kernels for 42%

profile of v2, /device:TPU:0, one launch (start us, length us, event | category | flops | bytes accessed | tf_op | source)
XLA Modules:
  0.0 205.5 jit_solution(14602896287160265723)
XLA Ops:
  0.7 1.0 pad_maximum_fusion.8
  1.7 3.0 %collective-permute-start.1 = (bf16[2,24,1536]{2,1,0:T(8,128)(2,1)S(1)}, bf16[2,24,1536]{2,1,0:T(8,128)(2,1)S(1)}, u32[]{:S(2)}, u32[]{:S(2)}) collective-permute-start(bf16[2,24,1536]{2,1,0:T(8,128)(2,1)S(1)} %get-tuple-element.108), channel_id=1, source_target_pairs={{0,4},{1,5},{2,6},{3,7},{4,0},{5,1},{6,2},{7,3},{8,12},{9,13},{10,... | collective-permute-start | bytes 442376 | tf_op jit(solution)/shard_map/ppermute | solution.py:335
  4.7 1.4 collective-permute-start
  6.2 0.6 collective-permute-start.2
  6.8 0.7 iota_reduce_fusion
  7.4 0.8 reshape.32
  8.2 0.8 reshape.30
  9.4 0.7 select_bitcast_fusion.1
  10.3 0.7 fusion.20
  11.5 1.5 collective-permute-done.2
  13.2 1.9 collective-permute-done.3
  15.5 5.3 %partial.6 = (f32[3,3,192,256]{3,2,1,0:T(8,128)S(1)}, bf16[3,3,192,256]{3,2,1,0:T(8,128)(2,1)S(1)}, f32[1,256]{1,0:T(1,128)S(1)}) custom-call(s32[193]{0:T(256)S(1)} %pad_add_fusion.1.table, s32[192,1]{1,0:T(8,128)S(1)} %slice_select_fusion.other, bf16[192,1536]{1,0:T(8,128)(2,1)S(1)} %get-tuple-element.100.x, ...), custom_call_target="tpu_custom_call" | custom-call | flops 84934656 | bytes 442368 | tf_op jit(solution)/shard_map/partial/pallas_call | solution.py:100
  20.8 3.7 %collective-permute-start.4 = (bf16[3,3,192,256]{3,2,1,0:T(8,128)(2,1)S(1)}, bf16[3,3,192,256]{3,2,1,0:T(8,128)(2,1)S(1)}, u32[]{:S(2)}, u32[]{:S(2)}) collective-permute-start(bf16[3,3,192,256]{3,2,1,0:T(8,128)(2,1)S(1)} %get-tuple-element.42), channel_id=1, source_target_pairs={{0,8},{24,16},{1,9},{25,17},{2,10},{26,18},{3,11},{27,19},{4,12},{... | collective-permute-start | bytes 2654216 | tf_op jit(solution)/shard_map/ppermute | solution.py:377
  24.5 8.4 %partial.7 = (f32[3,3,192,256]{3,2,1,0:T(8,128)S(1)}, bf16[3,3,192,256]{3,2,1,0:T(8,128)(2,1)S(1)}, f32[1,256]{1,0:T(1,128)S(1)}) custom-call(s32[193]{0:T(256)S(1)} %pad_add_fusion.1.table, s32[192,1]{1,0:T(8,128)S(1)} %slice_select_fusion.other, bf16[192,1536]{1,0:T(8,128)(2,1)S(1)} %get-tuple-element.100.x, ...), custom_call_target="tpu_custom_call" | custom-call | flops 198180864 | bytes 1032192 | tf_op jit(solution)/shard_map/partial/pallas_call | solution.py:100
  32.9 1.3 collective-permute-start.7
  34.3 8.4 %partial.8 = (f32[3,3,192,256]{3,2,1,0:T(8,128)S(1)}, bf16[3,3,192,256]{3,2,1,0:T(8,128)(2,1)S(1)}, f32[1,256]{1,0:T(1,128)S(1)}) custom-call(s32[193]{0:T(256)S(1)} %pad_add_fusion.1.table, s32[192,1]{1,0:T(8,128)S(1)} %slice_select_fusion.other, bf16[192,1536]{1,0:T(8,128)(2,1)S(1)} %get-tuple-element.100.x, ...), custom_call_target="tpu_custom_call" | custom-call | flops 198180864 | bytes 1032192 | tf_op jit(solution)/shard_map/partial/pallas_call | solution.py:100
  42.6 1.8 collective-permute-done.4
  44.7 0.7 collective-permute-start.5
  45.5 7.2 %collective-permute-start.8 = (bf16[3,3,192,256]{3,2,1,0:T(8,128)(2,1)S(1)}, bf16[3,3,192,256]{3,2,1,0:T(8,128)(2,1)S(1)}, u32[]{:S(2)}, u32[]{:S(2)}) collective-permute-start(bf16[3,3,192,256]{3,2,1,0:T(8,128)(2,1)S(1)} %get-tuple-element.51), channel_id=1, source_target_pairs={{0,8},{24,16},{1,9},{25,17},{2,10},{26,18},{3,11},{27,19},{4,12},{... | collective-permute-start | bytes 2654216 | tf_op jit(solution)/shard_map/ppermute | solution.py:377
  52.7 8.4 %partial.9 = (f32[3,3,192,256]{3,2,1,0:T(8,128)S(1)}, bf16[3,3,192,256]{3,2,1,0:T(8,128)(2,1)S(1)}, f32[1,256]{1,0:T(1,128)S(1)}) custom-call(s32[193]{0:T(256)S(1)} %pad_add_fusion.1.table, s32[192,1]{1,0:T(8,128)S(1)} %slice_select_fusion.other, bf16[192,1536]{1,0:T(8,128)(2,1)S(1)} %get-tuple-element.100.x, ...), custom_call_target="tpu_custom_call" | custom-call | flops 198180864 | bytes 1032192 | tf_op jit(solution)/shard_map/partial/pallas_call | solution.py:100
  61.1 2.4 %collective-permute-done.7 = bf16[3,3,192,256]{3,2,1,0:T(8,128)(2,1)S(1)} collective-permute-done((bf16[3,3,192,256]{3,2,1,0:T(8,128)(2,1)S(1)}, bf16[3,3,192,256]{3,2,1,0:T(8,128)(2,1)S(1)}, u32[]{:S(2)}, u32[]{:S(2)}) %collective-permute-start.7) | collective-permute-done | bytes 884768 | tf_op jit(solution)/shard_map/ppermute | solution.py:377
  63.4 0.7 fusion.1
  64.1 0.7 collective-permute-start.9
  64.8 10.5 %collective-permute-start.12 = (bf16[3,3,192,256]{3,2,1,0:T(8,128)(2,1)S(1)}, bf16[3,3,192,256]{3,2,1,0:T(8,128)(2,1)S(1)}, u32[]{:S(2)}, u32[]{:S(2)}) collective-permute-start(bf16[3,3,192,256]{3,2,1,0:T(8,128)(2,1)S(1)} %get-tuple-element.59), channel_id=1, source_target_pairs={{0,8},{24,16},{1,9},{25,17},{2,10},{26,18},{3,11},{27,19},{4,12},{... | collective-permute-start | bytes 2654216 | tf_op jit(solution)/shard_map/ppermute | solution.py:377
  75.3 0.4 multiply_convert_fusion.12
  75.8 1.3 collective-permute-start.6
  77.1 7.4 %partial.10 = (f32[2,3,192,256]{3,2,1,0:T(8,128)S(1)}, bf16[2,3,192,256]{3,2,1,0:T(8,128)(2,1)S(1)}, f32[1,256]{1,0:T(1,128)S(1)}) custom-call(s32[193]{0:T(256)S(1)} %pad_add_fusion.1.table, s32[192,1]{1,0:T(8,128)S(1)} %slice_select_fusion.other, bf16[192,1536]{1,0:T(8,128)(2,1)S(1)} %get-tuple-element.100.x, ...), custom_call_target="tpu_custom_call" | custom-call | flops 169869312 | bytes 884736 | tf_op jit(solution)/shard_map/partial/pallas_call | solution.py:100
  84.5 0.7 add_add_fusion.3
  85.2 0.7 collective-permute-start.13
  85.9 11.1 %collective-permute-start.16 = (bf16[2,3,192,256]{3,2,1,0:T(8,128)(2,1)S(1)}, bf16[2,3,192,256]{3,2,1,0:T(8,128)(2,1)S(1)}, u32[]{:S(2)}, u32[]{:S(2)}) collective-permute-start(bf16[2,3,192,256]{3,2,1,0:T(8,128)(2,1)S(1)} %get-tuple-element.64), channel_id=1, source_target_pairs={{0,8},{24,16},{1,9},{25,17},{2,10},{26,18},{3,11},{27,19},{4,12},{... | collective-permute-start | bytes 1769480 | tf_op jit(solution)/shard_map/ppermute | solution.py:377
  97.0 0.4 multiply_convert_fusion.9
  97.4 1.3 collective-permute-start.11
  98.7 6.7 %post.6 = (bf16[4,2048,1536]{2,1,0:T(8,128)(2,1)}, f32[2,192,1536]{2,1,0:T(8,128)S(1)}, f32[1,256]{1,0:T(1,128)S(1)}) custom-call(s32[193]{0:T(256)S(1)} %pad_add_fusion.1.table, s32[192,1]{1,0:T(8,128)S(1)} %slice_select_fusion.other, f32[2,192,1]{2,1,0:T(8,128)S(1)} %get-tuple-element.105.weight, ...), custom_call_target="tpu_custom_call" | custom-call | flops 113246208 | bytes 589824 | tf_op jit(solution)/shard_map/post/pallas_call | solution.py:236
  105.5 4.4 %partial.11 = (f32[2,3,192,256]{3,2,1,0:T(8,128)S(1)}, bf16[2,3,192,256]{3,2,1,0:T(8,128)(2,1)S(1)}, f32[1,256]{1,0:T(1,128)S(1)}) custom-call(s32[193]{0:T(256)S(1)} %pad_add_fusion.1.table, s32[192,1]{1,0:T(8,128)S(1)} %slice_select_fusion.other, bf16[192,1536]{1,0:T(8,128)(2,1)S(1)} %get-tuple-element.100.x, ...), custom_call_target="tpu_custom_call" | custom-call | flops 56623104 | bytes 294912 | tf_op jit(solution)/shard_map/partial/pallas_call | solution.py:100
  109.9 4.8 %collective-permute-start.10 = (bf16[2,3,192,256]{3,2,1,0:T(8,128)(2,1)S(1)}, bf16[2,3,192,256]{3,2,1,0:T(8,128)(2,1)S(1)}, u32[]{:S(2)}, u32[]{:S(2)}) collective-permute-start(bf16[2,3,192,256]{3,2,1,0:T(8,128)(2,1)S(1)} %get-tuple-element.54), channel_id=1, source_target_pairs={{0,8},{24,16},{1,9},{25,17},{2,10},{26,18},{3,11},{27,19},{4,12},{... | collective-permute-start | bytes 1769480 | tf_op jit(solution)/shard_map/ppermute | solution.py:377
  114.7 0.7 add_add_fusion.1
  115.4 0.7 collective-permute-start.17
  116.1 0.4 multiply_convert_fusion.6
  116.6 1.3 collective-permute-start.15
  117.9 11.2 %post.7 = (bf16[4,2048,1536]{2,1,0:T(8,128)(2,1)}, f32[2,192,1536]{2,1,0:T(8,128)S(1)}, f32[1,256]{1,0:T(1,128)S(1)}) custom-call(s32[193]{0:T(256)S(1)} %pad_add_fusion.1.table, s32[192,1]{1,0:T(8,128)S(1)} %slice_select_fusion.other, f32[2,192,1]{2,1,0:T(8,128)S(1)} %get-tuple-element.105.weight, ...), custom_call_target="tpu_custom_call", output_to_operand_aliasing={{0}: (10, {}), {1}: (9, {})} | custom-call | flops 264241152 | bytes 1376256 | tf_op jit(solution)/shard_map/post/pallas_call | solution.py:236
  129.1 0.4 fusion.5
  129.5 0.7 collective-permute-start.19
  130.2 0.7 collective-permute-start.14
  130.9 0.4 add_add_fusion
  131.3 0.4 multiply_convert_fusion.3
  131.7 1.3 collective-permute-start.21
  133.0 3.1 %collective-permute-done.15.came = bf16[3,3,192,256]{3,2,1,0:T(8,128)(2,1)S(1)} collective-permute-done((bf16[3,3,192,256]{3,2,1,0:T(8,128)(2,1)S(1)}, bf16[3,3,192,256]{3,2,1,0:T(8,128)(2,1)S(1)}, u32[]{:S(2)}, u32[]{:S(2)}) %collective-permute-start.15) | collective-permute-done | bytes 884768 | tf_op jit(solution)/shard_map/ppermute | solution.py:377
  136.1 11.2 %post.8 = (bf16[4,2048,1536]{2,1,0:T(8,128)(2,1)}, f32[2,192,1536]{2,1,0:T(8,128)S(1)}, f32[1,256]{1,0:T(1,128)S(1)}) custom-call(s32[193]{0:T(256)S(1)} %pad_add_fusion.1.table, s32[192,1]{1,0:T(8,128)S(1)} %slice_select_fusion.other, f32[2,192,1]{2,1,0:T(8,128)S(1)} %get-tuple-element.105.weight, ...), custom_call_target="tpu_custom_call", output_to_operand_aliasing={{0}: (10, {}), {1}: (9, {})} | custom-call | flops 264241152 | bytes 1376256 | tf_op jit(solution)/shard_map/post/pallas_call | solution.py:236
  147.3 0.5 add_add_fusion.8
  147.8 0.5 multiply_convert_fusion.15
  148.4 1.3 collective-permute-start.20
  149.8 1.3 collective-permute-start.18
  151.1 3.8 %collective-permute-done.21.came = bf16[3,3,192,256]{3,2,1,0:T(8,128)(2,1)S(1)} collective-permute-done((bf16[3,3,192,256]{3,2,1,0:T(8,128)(2,1)S(1)}, bf16[3,3,192,256]{3,2,1,0:T(8,128)(2,1)S(1)}, u32[]{:S(2)}, u32[]{:S(2)}) %collective-permute-start.21) | collective-permute-done | bytes 884768 | tf_op jit(solution)/shard_map/ppermute | solution.py:377
  154.9 11.2 %post.9 = (bf16[4,2048,1536]{2,1,0:T(8,128)(2,1)}, f32[2,192,1536]{2,1,0:T(8,128)S(1)}, f32[1,256]{1,0:T(1,128)S(1)}) custom-call(s32[193]{0:T(256)S(1)} %pad_add_fusion.1.table, s32[192,1]{1,0:T(8,128)S(1)} %slice_select_fusion.other, f32[2,192,1]{2,1,0:T(8,128)S(1)} %get-tuple-element.105.weight, ...), custom_call_target="tpu_custom_call", output_to_operand_aliasing={{0}: (10, {}), {1}: (9, {})} | custom-call | flops 264241152 | bytes 1376256 | tf_op jit(solution)/shard_map/post/pallas_call | solution.py:236
  166.1 9.9 %collective-permute-done.20.came = bf16[2,3,192,256]{3,2,1,0:T(8,128)(2,1)S(1)} collective-permute-done((bf16[2,3,192,256]{3,2,1,0:T(8,128)(2,1)S(1)}, bf16[2,3,192,256]{3,2,1,0:T(8,128)(2,1)S(1)}, u32[]{:S(2)}, u32[]{:S(2)}) %collective-permute-start.20) | collective-permute-done | bytes 589856 | tf_op jit(solution)/shard_map/ppermute | solution.py:377
  175.9 10.0 %post.10 = (bf16[4,2048,1536]{2,1,0:T(8,128)(2,1)}, f32[2,192,1536]{2,1,0:T(8,128)S(1)}, f32[1,256]{1,0:T(1,128)S(1)}) custom-call(s32[193]{0:T(256)S(1)} %pad_add_fusion.1.table, s32[192,1]{1,0:T(8,128)S(1)} %slice_select_fusion.other, f32[2,192,1]{2,1,0:T(8,128)S(1)} %get-tuple-element.105.weight, ...), custom_call_target="tpu_custom_call", output_to_operand_aliasing={{0}: (10, {}), {1}: (9, {})} | custom-call | flops 226492416 | bytes 1179648 | tf_op jit(solution)/shard_map/post/pallas_call | solution.py:236
  186.0 5.6 %post.11 = (bf16[4,2048,1536]{2,1,0:T(8,128)(2,1)}, f32[2,96,1536]{2,1,0:T(8,128)S(1)}, f32[2,96,1536]{2,1,0:T(8,128)S(1)}) custom-call(s32[193]{0:T(256)S(1)} %pad_add_fusion.1.table, s32[192,1]{1,0:T(8,128)S(1)} %slice_select_fusion.other, f32[2,192,1]{2,1,0:T(8,128)S(1)} %get-tuple-element.105.weight, ...), custom_call_target="tpu_custom_call", output_to_operand_aliasing={{0}: (10, {})} | custom-call | flops 75497472 | bytes 393216 | tf_op jit(solution)/shard_map/post/pallas_call | solution.py:236
  191.6 2.8 %collective-permute-done.22 = f32[2,96,1536]{2,1,0:T(8,128)S(1)} collective-permute-done((f32[2,96,1536]{2,1,0:T(8,128)S(1)}, f32[2,96,1536]{2,1,0:T(8,128)S(1)}, u32[]{:S(2)}, u32[]{:S(2)}) %collective-permute-start.22) | collective-permute-done | bytes 1179680 | tf_op jit(solution)/shard_map/ppermute | solution.py:403
  194.6 1.6 collective-permute-start.23
  196.3 1.4 collective-permute-start.25
  197.6 1.5 collective-permute-start.24
  199.1 3.1 %collective-permute-done.23 = bf16[2,24,1536]{2,1,0:T(8,128)(2,1)S(1)} collective-permute-done((bf16[2,24,1536]{2,1,0:T(8,128)(2,1)S(1)}, bf16[2,24,1536]{2,1,0:T(8,128)(2,1)S(1)}, u32[]{:S(2)}, u32[]{:S(2)}) %collective-permute-start.23) | collective-permute-done | bytes 147488 | tf_op jit(solution)/shard_map/ppermute | solution.py:407
  202.3 2.4 %collective-permute-done.25 = bf16[2,24,1536]{2,1,0:T(8,128)(2,1)S(1)} collective-permute-done((bf16[2,24,1536]{2,1,0:T(8,128)(2,1)S(1)}, bf16[2,24,1536]{2,1,0:T(8,128)(2,1)S(1)}, u32[]{:S(2)}, u32[]{:S(2)}) %collective-permute-start.25) | collective-permute-done | bytes 147488 | tf_op jit(solution)/shard_map/ppermute | solution.py:407
  204.8 0.7 slice_bitcast_fusion.2
  (66 shorter events, 2.7 us)
Async XLA Ops:
  0.6 6.1 %copy-start = (s32[4]{0:T(128)S(1)}, s32[4]{0:T(128)}, u32[]{:S(2)}) copy-start(s32[4]{0:T(128)} %param.13) | copy-start | bytes 52
  0.6 9.7 %copy-start.5 = (pred[32]{0:T(512)(128)(4,1)S(1)}, pred[32]{0:T(512)(128)(4,1)}, u32[]{:S(2)}) copy-start(pred[32]{0:T(512)(128)(4,1)} %constant.53) | copy-start | bytes 100
  0.7 9.7 %copy-start.6 = (s32[32]{0:T(128)S(1)}, s32[32]{0:T(128)}, u32[]{:S(2)}) copy-start(s32[32]{0:T(128)} %constant.51.clone) | copy-start | bytes 388
  0.7 10.3 %copy-start.4 = (s32[32,5]{0,1:T(8,128)S(1)}, s32[32,5]{0,1:T(8,128)}, u32[]{:S(2)}) copy-start(s32[32,5]{0,1:T(8,128)} %constant.52.clone) | copy-start | bytes 1924
  0.7 12.3 %copy-start.2 = (bf16[24,1536]{1,0:T(8,128)(2,1)S(1)}, bf16[24,1536]{1,0:T(8,128)(2,1)}, u32[]{:S(2)}) copy-start(bf16[24,1536]{1,0:T(8,128)(2,1)} %param.17) | copy-start | bytes 221188
  0.7 12.3 %copy-start.3 = (bf16[24,1536]{1,0:T(8,128)(2,1)S(1)}, bf16[24,1536]{1,0:T(8,128)(2,1)}, u32[]{:S(2)}) copy-start(bf16[24,1536]{1,0:T(8,128)(2,1)} %param.10) | copy-start | bytes 221188
  1.7 9.8 %collective-permute-start.1 = (bf16[2,24,1536]{2,1,0:T(8,128)(2,1)S(1)}, bf16[2,24,1536]{2,1,0:T(8,128)(2,1)S(1)}, u32[]{:S(2)}, u32[]{:S(2)}) collective-permute-start(bf16[2,24,1536]{2,1,0:T(8,128)(2,1)S(1)} %get-tuple-element.108), channel_id=1, source_target_pairs={{0,4},{1,5},{2,6},{3,7},{4,0},{5,1},{6,2},{7,3},{8,12},{9,13},{10,... | collective-permute-start | bytes 442376 | tf_op jit(solution)/shard_map/ppermute | solution.py:335
  4.7 6.7 %collective-permute-start = (bf16[2,24,1536]{2,1,0:T(8,128)(2,1)S(1)}, bf16[2,24,1536]{2,1,0:T(8,128)(2,1)S(1)}, u32[]{:S(2)}, u32[]{:S(2)}) collective-permute-start(bf16[2,24,1536]{2,1,0:T(8,128)(2,1)S(1)} %get-tuple-element.108), channel_id=1, source_target_pairs={{0,6},{1,7},{2,0},{3,1},{4,2},{5,3},{6,4},{7,5},{8,14},{9,15},{10,... | collective-permute-start | bytes 442376 | tf_op jit(solution)/shard_map/ppermute | solution.py:335
  6.2 6.8 %collective-permute-start.2 = (bf16[2,24,1536]{2,1,0:T(8,128)(2,1)S(1)}, bf16[2,24,1536]{2,1,0:T(8,128)(2,1)S(1)}, u32[]{:S(2)}, u32[]{:S(2)}) collective-permute-start(bf16[2,24,1536]{2,1,0:T(8,128)(2,1)S(1)} %get-tuple-element.108), channel_id=1, source_target_pairs={{0,2},{1,3},{2,4},{3,5},{4,6},{5,7},{6,0},{7,1},{8,10},{9,11},{10,... | collective-permute-start | bytes 442376 | tf_op jit(solution)/shard_map/ppermute | solution.py:335
  13.0 2.1 %collective-permute-start.3 = (bf16[2,96,1536]{2,1,0:T(8,128)(2,1)S(1)}, bf16[2,96,1536]{2,1,0:T(8,128)(2,1)S(1)}, u32[]{:S(2)}, u32[]{:S(2)}) collective-permute-start(bf16[2,96,1536]{2,1,0:T(8,128)(2,1)S(1)} %pad_maximum_fusion.4), channel_id=1, source_target_pairs={{0,1},{1,0},{2,3},{3,2},{4,5},{5,4},{6,7},{7,6},{8,9},{9,8},{10,11... | collective-permute-start | bytes 1769480 | tf_op jit(solution)/shard_map/ppermute | solution.py:339
  20.8 23.6 %collective-permute-start.4 = (bf16[3,3,192,256]{3,2,1,0:T(8,128)(2,1)S(1)}, bf16[3,3,192,256]{3,2,1,0:T(8,128)(2,1)S(1)}, u32[]{:S(2)}, u32[]{:S(2)}) collective-permute-start(bf16[3,3,192,256]{3,2,1,0:T(8,128)(2,1)S(1)} %get-tuple-element.42), channel_id=1, source_target_pairs={{0,8},{24,16},{1,9},{25,17},{2,10},{26,18},{3,11},{27,19},{4,12},{... | collective-permute-start | bytes 2654216 | tf_op jit(solution)/shard_map/ppermute | solution.py:377
  32.9 30.5 %collective-permute-start.7 = (bf16[3,3,192,256]{3,2,1,0:T(8,128)(2,1)S(1)}, bf16[3,3,192,256]{3,2,1,0:T(8,128)(2,1)S(1)}, u32[]{:S(2)}, u32[]{:S(2)}) collective-permute-start(bf16[3,3,192,256]{3,2,1,0:T(8,128)(2,1)S(1)} %get-tuple-element.48), channel_id=1, source_target_pairs={{0,8},{24,16},{1,9},{25,17},{2,10},{26,18},{3,11},{27,19},{4,12},{... | collective-permute-start | bytes 2654216 | tf_op jit(solution)/shard_map/ppermute | solution.py:377
  44.7 18.7 %collective-permute-start.5 = (bf16[3,3,192,256]{3,2,1,0:T(8,128)(2,1)S(1)}, bf16[3,3,192,256]{3,2,1,0:T(8,128)(2,1)S(1)}, u32[]{:S(2)}, u32[]{:S(2)}) collective-permute-start(bf16[3,3,192,256]{3,2,1,0:T(8,128)(2,1)S(1)} %fusion.rest_1_), channel_id=1, source_target_pairs={{8,16},{16,8},{9,17},{17,9},{10,18},{18,10},{11,19},{19,11},{12,20... | collective-permute-start | bytes 2654216 | tf_op jit(solution)/shard_map/ppermute | solution.py:377
  45.5 39.0 %collective-permute-start.8 = (bf16[3,3,192,256]{3,2,1,0:T(8,128)(2,1)S(1)}, bf16[3,3,192,256]{3,2,1,0:T(8,128)(2,1)S(1)}, u32[]{:S(2)}, u32[]{:S(2)}) collective-permute-start(bf16[3,3,192,256]{3,2,1,0:T(8,128)(2,1)S(1)} %get-tuple-element.51), channel_id=1, source_target_pairs={{0,8},{24,16},{1,9},{25,17},{2,10},{26,18},{3,11},{27,19},{4,12},{... | collective-permute-start | bytes 2654216 | tf_op jit(solution)/shard_map/ppermute | solution.py:377
  64.1 20.4 %collective-permute-start.9 = (bf16[3,3,192,256]{3,2,1,0:T(8,128)(2,1)S(1)}, bf16[3,3,192,256]{3,2,1,0:T(8,128)(2,1)S(1)}, u32[]{:S(2)}, u32[]{:S(2)}) collective-permute-start(bf16[3,3,192,256]{3,2,1,0:T(8,128)(2,1)S(1)} %get-tuple-element.118.rest_1_), channel_id=1, source_target_pairs={{8,16},{16,8},{9,17},{17,9},{10,18},{18,10},{11,19},{19,11},{12,20... | collective-permute-start | bytes 2654216 | tf_op jit(solution)/shard_map/ppermute | solution.py:377
  64.8 49.8 %collective-permute-start.12 = (bf16[3,3,192,256]{3,2,1,0:T(8,128)(2,1)S(1)}, bf16[3,3,192,256]{3,2,1,0:T(8,128)(2,1)S(1)}, u32[]{:S(2)}, u32[]{:S(2)}) collective-permute-start(bf16[3,3,192,256]{3,2,1,0:T(8,128)(2,1)S(1)} %get-tuple-element.59), channel_id=1, source_target_pairs={{0,8},{24,16},{1,9},{25,17},{2,10},{26,18},{3,11},{27,19},{4,12},{... | collective-permute-start | bytes 2654216 | tf_op jit(solution)/shard_map/ppermute | solution.py:377
  75.8 23.0 %collective-permute-start.6 = (bf16[3,3,192,256]{3,2,1,0:T(8,128)(2,1)S(1)}, bf16[3,3,192,256]{3,2,1,0:T(8,128)(2,1)S(1)}, u32[]{:S(2)}, u32[]{:S(2)}) collective-permute-start(bf16[3,3,192,256]{3,2,1,0:T(8,128)(2,1)S(1)} %pad_maximum_fusion.rest_2_.mine), channel_id=1, source_target_pairs={{8,0},{16,24},{9,1},{17,25},{10,2},{18,26},{11,3},{19,27},{12,4},{... | collective-permute-start | bytes 2654216 | tf_op jit(solution)/shard_map/ppermute | solution.py:377
  85.2 29.5 %collective-permute-start.13 = (bf16[3,3,192,256]{3,2,1,0:T(8,128)(2,1)S(1)}, bf16[3,3,192,256]{3,2,1,0:T(8,128)(2,1)S(1)}, u32[]{:S(2)}, u32[]{:S(2)}) collective-permute-start(bf16[3,3,192,256]{3,2,1,0:T(8,128)(2,1)S(1)} %get-tuple-element.117.rest_1_), channel_id=1, source_target_pairs={{8,16},{16,8},{9,17},{17,9},{10,18},{18,10},{11,19},{19,11},{12,20... | collective-permute-start | bytes 2654216 | tf_op jit(solution)/shard_map/ppermute | solution.py:377
  85.9 43.2 %collective-permute-start.16 = (bf16[2,3,192,256]{3,2,1,0:T(8,128)(2,1)S(1)}, bf16[2,3,192,256]{3,2,1,0:T(8,128)(2,1)S(1)}, u32[]{:S(2)}, u32[]{:S(2)}) collective-permute-start(bf16[2,3,192,256]{3,2,1,0:T(8,128)(2,1)S(1)} %get-tuple-element.64), channel_id=1, source_target_pairs={{0,8},{24,16},{1,9},{25,17},{2,10},{26,18},{3,11},{27,19},{4,12},{... | collective-permute-start | bytes 1769480 | tf_op jit(solution)/shard_map/ppermute | solution.py:377
  97.4 20.5 %collective-permute-start.11 = (bf16[3,3,192,256]{3,2,1,0:T(8,128)(2,1)S(1)}, bf16[3,3,192,256]{3,2,1,0:T(8,128)(2,1)S(1)}, u32[]{:S(2)}, u32[]{:S(2)}) collective-permute-start(bf16[3,3,192,256]{3,2,1,0:T(8,128)(2,1)S(1)} %pad_maximum_fusion.1.rest_2_.mine), channel_id=1, source_target_pairs={{8,0},{16,24},{9,1},{17,25},{10,2},{18,26},{11,3},{19,27},{12,4},{... | collective-permute-start | bytes 2654216 | tf_op jit(solution)/shard_map/ppermute | solution.py:377
  109.9 19.3 %collective-permute-start.10 = (bf16[2,3,192,256]{3,2,1,0:T(8,128)(2,1)S(1)}, bf16[2,3,192,256]{3,2,1,0:T(8,128)(2,1)S(1)}, u32[]{:S(2)}, u32[]{:S(2)}) collective-permute-start(bf16[2,3,192,256]{3,2,1,0:T(8,128)(2,1)S(1)} %get-tuple-element.54), channel_id=1, source_target_pairs={{0,8},{24,16},{1,9},{25,17},{2,10},{26,18},{3,11},{27,19},{4,12},{... | collective-permute-start | bytes 1769480 | tf_op jit(solution)/shard_map/ppermute | solution.py:377
  115.4 15.5 %collective-permute-start.17 = (bf16[3,3,192,256]{3,2,1,0:T(8,128)(2,1)S(1)}, bf16[3,3,192,256]{3,2,1,0:T(8,128)(2,1)S(1)}, u32[]{:S(2)}, u32[]{:S(2)}) collective-permute-start(bf16[3,3,192,256]{3,2,1,0:T(8,128)(2,1)S(1)} %get-tuple-element.115.rest_3_), channel_id=1, source_target_pairs={{8,16},{16,8},{9,17},{17,9},{10,18},{18,10},{11,19},{19,11},{12,20... | collective-permute-start | bytes 2654216 | tf_op jit(solution)/shard_map/ppermute | solution.py:377
  116.6 19.5 %collective-permute-start.15 = (bf16[3,3,192,256]{3,2,1,0:T(8,128)(2,1)S(1)}, bf16[3,3,192,256]{3,2,1,0:T(8,128)(2,1)S(1)}, u32[]{:S(2)}, u32[]{:S(2)}) collective-permute-start(bf16[3,3,192,256]{3,2,1,0:T(8,128)(2,1)S(1)} %pad_maximum_fusion.2.rest_4_.mine), channel_id=1, source_target_pairs={{8,0},{16,24},{9,1},{17,25},{10,2},{18,26},{11,3},{19,27},{12,4},{... | collective-permute-start | bytes 2654216 | tf_op jit(solution)/shard_map/ppermute | solution.py:377
  129.5 17.8 %collective-permute-start.19 = (bf16[2,3,192,256]{3,2,1,0:T(8,128)(2,1)S(1)}, bf16[2,3,192,256]{3,2,1,0:T(8,128)(2,1)S(1)}, u32[]{:S(2)}, u32[]{:S(2)}) collective-permute-start(bf16[2,3,192,256]{3,2,1,0:T(8,128)(2,1)S(1)} %get-tuple-element.112.rest_3_), channel_id=1, source_target_pairs={{8,16},{16,8},{9,17},{17,9},{10,18},{18,10},{11,19},{19,11},{12,20... | collective-permute-start | bytes 1769480 | tf_op jit(solution)/shard_map/ppermute | solution.py:377
  130.2 17.1 %collective-permute-start.14 = (bf16[2,3,192,256]{3,2,1,0:T(8,128)(2,1)S(1)}, bf16[2,3,192,256]{3,2,1,0:T(8,128)(2,1)S(1)}, u32[]{:S(2)}, u32[]{:S(2)}) collective-permute-start(bf16[2,3,192,256]{3,2,1,0:T(8,128)(2,1)S(1)} %get-tuple-element.113.rest_5_), channel_id=1, source_target_pairs={{8,16},{16,8},{9,17},{17,9},{10,18},{18,10},{11,19},{19,11},{12,20... | collective-permute-start | bytes 1769480 | tf_op jit(solution)/shard_map/ppermute | solution.py:377
  131.7 23.1 %collective-permute-start.21 = (bf16[3,3,192,256]{3,2,1,0:T(8,128)(2,1)S(1)}, bf16[3,3,192,256]{3,2,1,0:T(8,128)(2,1)S(1)}, u32[]{:S(2)}, u32[]{:S(2)}) collective-permute-start(bf16[3,3,192,256]{3,2,1,0:T(8,128)(2,1)S(1)} %pad_maximum_fusion.3.rest_4_.mine), channel_id=1, source_target_pairs={{8,0},{16,24},{9,1},{17,25},{10,2},{18,26},{11,3},{19,27},{12,4},{... | collective-permute-start | bytes 2654216 | tf_op jit(solution)/shard_map/ppermute | solution.py:377
  148.4 27.5 %collective-permute-start.20 = (bf16[2,3,192,256]{3,2,1,0:T(8,128)(2,1)S(1)}, bf16[2,3,192,256]{3,2,1,0:T(8,128)(2,1)S(1)}, u32[]{:S(2)}, u32[]{:S(2)}) collective-permute-start(bf16[2,3,192,256]{3,2,1,0:T(8,128)(2,1)S(1)} %pad_maximum_fusion.6.rest_3_.mine), channel_id=1, source_target_pairs={{8,0},{16,24},{9,1},{17,25},{10,2},{18,26},{11,3},{19,27},{12,4},{... | collective-permute-start | bytes 1769480 | tf_op jit(solution)/shard_map/ppermute | solution.py:377
  149.8 36.1 %collective-permute-start.18 = (bf16[2,3,192,256]{3,2,1,0:T(8,128)(2,1)S(1)}, bf16[2,3,192,256]{3,2,1,0:T(8,128)(2,1)S(1)}, u32[]{:S(2)}, u32[]{:S(2)}) collective-permute-start(bf16[2,3,192,256]{3,2,1,0:T(8,128)(2,1)S(1)} %pad_maximum_fusion.5.rest_4_.mine), channel_id=1, source_target_pairs={{8,0},{16,24},{9,1},{17,25},{10,2},{18,26},{11,3},{19,27},{12,4},{... | collective-permute-start | bytes 1769480 | tf_op jit(solution)/shard_map/ppermute | solution.py:377
  191.5 2.9 %collective-permute-start.22 = (f32[2,96,1536]{2,1,0:T(8,128)S(1)}, f32[2,96,1536]{2,1,0:T(8,128)S(1)}, u32[]{:S(2)}, u32[]{:S(2)}) collective-permute-start(f32[2,96,1536]{2,1,0:T(8,128)S(1)} %get-tuple-element.75), channel_id=1, source_target_pairs={{0,1},{1,0},{2,3},{3,2},{4,5},{5,4},{6,7},{7,6},{8,9},{9,8},{10,11... | collective-permute-start | bytes 3538952 | tf_op jit(solution)/shard_map/ppermute | solution.py:403
  194.4 11.0 %copy-start.1 = (s32[4]{0:T(128)S(1)}, s32[4]{0:T(128)}, u32[]{:S(2)}) copy-start(s32[4]{0:T(128)} %param.13) | copy-start | bytes 52
  194.6 7.6 %collective-permute-start.23 = (bf16[2,24,1536]{2,1,0:T(8,128)(2,1)S(1)}, bf16[2,24,1536]{2,1,0:T(8,128)(2,1)S(1)}, u32[]{:S(2)}, u32[]{:S(2)}) collective-permute-start(bf16[2,24,1536]{2,1,0:T(8,128)(2,1)S(1)} %get-tuple-element.101), channel_id=1, source_target_pairs={{0,2},{1,3},{2,4},{3,5},{4,6},{5,7},{6,0},{7,1},{8,10},{9,11},{10,... | collective-permute-start | bytes 442376 | tf_op jit(solution)/shard_map/ppermute | solution.py:407
  196.3 8.4 %collective-permute-start.25 = (bf16[2,24,1536]{2,1,0:T(8,128)(2,1)S(1)}, bf16[2,24,1536]{2,1,0:T(8,128)(2,1)S(1)}, u32[]{:S(2)}, u32[]{:S(2)}) collective-permute-start(bf16[2,24,1536]{2,1,0:T(8,128)(2,1)S(1)} %get-tuple-element.102), channel_id=1, source_target_pairs={{0,6},{1,7},{2,0},{3,1},{4,2},{5,3},{6,4},{7,5},{8,14},{9,15},{10,... | collective-permute-start | bytes 442376 | tf_op jit(solution)/shard_map/ppermute | solution.py:407
  197.6 7.1 %collective-permute-start.24 = (bf16[2,24,1536]{2,1,0:T(8,128)(2,1)S(1)}, bf16[2,24,1536]{2,1,0:T(8,128)(2,1)S(1)}, u32[]{:S(2)}, u32[]{:S(2)}) collective-permute-start(bf16[2,24,1536]{2,1,0:T(8,128)(2,1)S(1)} %get-tuple-element.103), channel_id=1, source_target_pairs={{0,4},{1,5},{2,6},{3,7},{4,0},{5,1},{6,2},{7,3},{8,12},{9,13},{10,... | collective-permute-start | bytes 442376 | tf_op jit(solution)/shard_map/ppermute | solution.py:407

commit v3 on v2

v3 whole, which is shorter than its diff:
```python
import functools

import jax
import jax.numpy as jnp
from jax import lax
from jax.experimental import pallas as pl
from jax.experimental.pallas import tpu as pltpu
from jax.sharding import PartitionSpec as P

SUB = 512
EARLY = 2
SLOTS = EARLY + 1
F32 = jnp.float32
BF16 = jnp.bfloat16
COST_SCALE = 1
VMEM_LIMIT = 20 * 1024 * 1024
ANY = pl.BlockSpec(memory_space=pl.ANY)
HBM = pl.BlockSpec(memory_space=pltpu.HBM)
VMEM = pl.BlockSpec(memory_space=pltpu.VMEM)
EXPERT, UNIT, GROUP, COLUMN, FIRST, LAST, FIELDS = 0, 1, 2, 3, 4, 5, 6


def dot(a, b, contract):
    return lax.dot_general(a, b, ((contract[0], contract[1]), ((), ())), preferred_element_type=F32)


def fill_table(rows, base, head, table):
    order = {rank: head[0, rank] for rank in sorted({row[EXPERT] for row in rows})}
    for n, row in enumerate(rows):
        for field, value in enumerate(row):
            table[n * FIELDS + field] = order[value] if field == EXPERT else value
    return lambda i, field: table[(i - base) * FIELDS + field]


def weight_copies(field, i, weights, buffers, sems):
    slot = lax.rem(i, SLOTS)
    expert = field(i, EXPERT)
    units = pl.ds(pl.multiple_of(field(i, COLUMN), SUB), SUB)
    wg, wu, wd = weights
    return (
        pltpu.make_async_copy(wg.at[expert, :, units], buffers[0].at[slot], sems.at[slot, 0]),
        pltpu.make_async_copy(wu.at[expert, :, units], buffers[1].at[slot], sems.at[slot, 1]),
        pltpu.make_async_copy(wd.at[expert, units, :], buffers[2].at[slot], sems.at[slot, 2]),
    )


def over_blocks(span, total, fetch, work):
    base, end = span
    if base == 0:
        for i in range(min(EARLY, total)):
            begin_all(fetch(i))
    loaded = 0 if base == 0 else base + EARLY

    def body(i, carry):
        @pl.when(i + EARLY < total)
        def _():
            begin_all(fetch(i + EARLY))

        @pl.when(i >= loaded)
        def _():
            wait_all(fetch(i))

        work(i)
        return carry

    lax.fori_loop(base, end, body, 0)
    for i in range(max(end, loaded), min(end + EARLY, total)):
        wait_all(fetch(i))


def begin_all(copies):
    for copy in copies:
        copy.start()


def wait_all(copies):
    for copy in copies:
        copy.wait()


def partial_kernel(span, total, rows, first, deps, head, other, x, rg, wg, wu, wd, *rest):
    b0, b1, b2, own, send, zero, table, wsem = rest[deps + (0 if first else 3) :]
    field = fill_table(rows, span[0], head, table)
    fetch = lambda i: weight_copies(field, i, (wg, wu, wd), (b0, b1, b2), wsem)
    zero[...] = jnp.zeros_like(zero)

    def work(i):
        slot, unit, group = lax.rem(i, SLOTS), field(i, UNIT), field(i, GROUP)
        keep = jnp.logical_or(other[...] == field(i, EXPERT), field(i, FIRST) == 1)
        terms = (
            dot(x[...], b0[slot], ((1,), (0,))),
            dot(x[...], b1[slot], ((1,), (0,))),
            dot(rg[group], b2[slot], ((1,), (1,))),
        )
        for n, term in enumerate(terms):
            own[unit, n] = jnp.where(keep, term, own[unit, n])

        @pl.when(field(i, LAST) == 1)
        def _():
            for n in range(3):
                send[unit, n] = own[unit, n].astype(BF16)

    over_blocks(span, total, fetch, work)


def near_core(v):
    return pltpu.with_memory_space_constraint(v, pltpu.VMEM)


def slot_shapes(depth):
    return [pltpu.VMEM((SLOTS, depth, SUB), BF16)] * 2 + [pltpu.VMEM((SLOTS, SUB, depth), BF16)]


def in_hbm(v):
    return pltpu.with_memory_space_constraint(v, pltpu.HBM)


def cost(products, rows, depth, blocks):
    return pl.CostEstimate(
        flops=int(2 * products * rows * depth * SUB * blocks / COST_SCALE),
        bytes_accessed=int(6 * depth * SUB * blocks / COST_SCALE),
        transcendentals=0,
    )


def partial_products(span, units, blocks, head, x, rg, other, weights, slots, after):
    depth = weights[0].shape[1]
    rows = x.shape[0]
    shape = (units, 3, rows, SUB)
    first = slots is None
    seen = blocks[span[0] : span[1] + EARLY]
    operands = [near_core(v) for v in (head, other, x, rg)] + [in_hbm(w) for w in weights] + list(after)
    in_specs = [VMEM] * 4 + [HBM] * 3 + [ANY] * len(after)
    aliases = {}
    if not first:
        aliases = {len(operands) + n: n for n in range(3)}
        operands += [near_core(v) for v in slots]
        in_specs += [VMEM] * 3
    out = pl.pallas_call(
        functools.partial(partial_kernel, span, len(blocks), seen, first, len(after)),
        in_specs=in_specs,
        out_specs=[VMEM] * 6,
        scratch_shapes=[pltpu.SMEM((len(seen) * FIELDS,), jnp.int32), pltpu.SemaphoreType.DMA((SLOTS, 3))],
        out_shape=slot_shapes(depth) + [pltpu.VMEM(shape, F32), pltpu.VMEM(shape, BF16), pltpu.VMEM((2, 1, SUB), F32)],
        input_output_aliases=aliases,
        compiler_params=pltpu.CompilerParams(vmem_limit_bytes=VMEM_LIMIT),
        cost_estimate=cost(3, rows, depth, span[1] - span[0]),
        name="partial",
    )(*operands)
    return out[:3], out[3], out[4], out[5]


def post_kernel(span, total, rows, deps, opening, closing, head, other, weight, mine, came, rg, wg, wu, wd, *rest):
    rest = rest[deps + 3 :]
    if not opening:
        sums_in, rest = rest[0], rest[2:]
    b0, b1, b2, d_down, sums, extra = rest[:6]
    ddv, table, wsem, dsem = rest[-4:]
    base, end = span
    field = fill_table(rows, base, head, table)
    edge = head[0, head.shape[1] - 1]
    fetch = lambda i: weight_copies(field, i, (wg, wu, wd), (b0, b1, b2), wsem)
    if closing:
        give, sums = sums, rest[6]
        sums[...] = jnp.zeros_like(sums) if opening else sums_in[...]
    else:
        extra[...] = jnp.zeros_like(extra)
        if opening:
            sums[...] = jnp.zeros_like(sums)

    def leave(i):
        slot = lax.rem(i, 2)
        units = pl.ds(pl.multiple_of(field(i, COLUMN), SUB), SUB)
        return pltpu.make_async_copy(ddv.at[slot], d_down.at[field(i, EXPERT), units, :], dsem.at[slot])

    def work(i):
        @pl.when(i >= base + 2)
        def _():
            leave(i - 2).wait()

        slot, unit, group = lax.rem(i, SLOTS), field(i, UNIT), field(i, GROUP)
        keep = jnp.logical_or(other[...] == field(i, EXPERT), group == 0)
        use_came = jnp.logical_and(keep, edge == 1)
        use_mine = jnp.logical_and(keep, edge == 0)
        hidden, d_gate, d_up = (
            jnp.where(use_came, came[unit, n], jnp.where(use_mine, mine[unit, n], jnp.zeros(mine.shape[2:], BF16)))
            for n in range(3)
        )
        ddv[lax.rem(i, 2)] = dot(hidden, rg[group], ((0,), (0,))).astype(BF16)
        leave(i).start()
        sums[0] += weight[group] * dot(hidden, b2[slot], ((1,), (0,)))
        sums[1] += dot(d_gate, b0[slot], ((1,), (1,))) + dot(d_up, b1[slot], ((1,), (1,)))

    over_blocks(span, total, fetch, work)
    if closing:
        half = sums.shape[1] // 2
        give[...] = sums[:, half:]
        extra[...] = sums[:, :half]
    for i in range(max(end - 2, base), end):
        leave(i).wait()


def post_products(span, blocks, head, mine, came, rg, weight, other, weights, slots, state, after, closing):
    experts, depth, width = weights[0].shape
    rows = rg.shape[1]
    opening = state is None
    seen = blocks[span[0] : span[1] + EARLY]
    operands = [near_core(v) for v in (head, other, weight, mine, came, rg)] + [in_hbm(w) for w in weights]
    operands += list(after)
    in_specs = [VMEM] * 6 + [HBM] * 3 + [ANY] * len(after) + [VMEM] * 3
    aliases = {len(operands) + n: n for n in range(3)}
    operands += [near_core(v) for v in slots]
    if not opening:
        aliases[len(operands) + 1] = 3
        if not closing:
            aliases[len(operands)] = 4
        in_specs += [VMEM, HBM]
        operands += [near_core(state[1]), in_hbm(state[0])]
    sums_shape = pltpu.VMEM((2, rows, depth), F32)
    out_shape = slot_shapes(depth) + [pltpu.HBM((experts, width, depth), BF16)]
    if closing:
        out_shape += [pltpu.VMEM((2, rows // 2, depth), F32)] * 2
    else:
        out_shape += [sums_shape, pltpu.VMEM((2, 1, SUB), F32)]
    out = pl.pallas_call(
        functools.partial(post_kernel, span, len(blocks), seen, len(after), opening, closing),
        in_specs=in_specs,
        out_specs=[VMEM] * 3 + [HBM, VMEM, VMEM],
        scratch_shapes=([sums_shape] if closing else [])
        + [
            pltpu.VMEM((2, SUB, depth), BF16),
            pltpu.SMEM((len(seen) * FIELDS,), jnp.int32),
            pltpu.SemaphoreType.DMA((SLOTS, 3)),
            pltpu.SemaphoreType.DMA((2,)),
        ],
        out_shape=out_shape,
        input_output_aliases=aliases,
        compiler_params=pltpu.CompilerParams(vmem_limit_bytes=VMEM_LIMIT),
        cost_estimate=cost(4, rows, depth, span[1] - span[0]),
        name="post",
    )(*operands)
    return out[:3], (out[3], out[4]), out[5]


def activations(gate, up, d_hidden):
    sigmoid = jax.nn.sigmoid(gate)
    active = gate * sigmoid
    hidden = (active * up).astype(BF16)
    d_gate = (d_hidden * up * sigmoid * (1.0 + gate * (1.0 - sigmoid))).astype(BF16)
    d_up = (d_hidden * active).astype(BF16)
    return jnp.stack([hidden, d_gate, d_up], 1)


def chunk_plan(units):
    starts = list(range(0, units, SUB))
    one, two = [[(0, s)] for s in starts], [[(1, s)] for s in starts]
    return one[:1] + two + one[1:]


def block_table(plan, steps, experts):
    rows, spans = [], {}
    for name, k in steps:
        if name not in ("partial", "post"):
            continue
        base = len(rows)
        for unit, (group, start) in enumerate(plan[k]):
            ranks = [0] if group == 0 else list(range(1, experts))
            for rank in ranks:
                rows.append((rank, unit, group, start, int(rank == ranks[0]), int(rank == ranks[-1])))
        spans[name, k] = (base, len(rows))
    return rows, spans


def sequence(count):
    if count != 8:
        return [(name, k) for k in range(count) for name in ("partial", "merge", "finish", "post")]
    return [(STEPS[word[0]], int(word[1:])) for word in ORDER]


STEPS = {"P": "partial", "M": "merge", "F": "finish", "Q": "post"}
ORDER = (
    "P0", "P1", "P2", "M0", "P3", "M1", "F0", "P4", "M2", "F1", "P5", "Q0",
    "M3", "F2", "Q1", "M4", "F3", "P6", "M5", "P7", "F4", "Q2", "M6", "F5",
    "Q3", "M7", "F6", "Q4", "Q5", "F7", "Q6", "Q7",
)


def on_device(sections, parts, tokens, combine, expert_ids, expert_counts, w_gate, w_up, w_down, cotangent):
    total = combine.shape[0]
    local = tokens.shape[0]
    experts = w_gate.shape[0]
    weights = (w_gate, w_up, w_down)
    chips = parts // 2
    me = lax.axis_index("tensor")
    place = lax.axis_index("section")
    chip, core = me // 2, me % 2

    pair = jnp.stack([tokens, cotangent], 0)
    near = jnp.concatenate(
        [pair]
        + [lax.ppermute(pair, "tensor", [(i, (i - 2 * n) % parts) for i in range(parts)]) for n in range(1, chips)],
        1,
    )
    swap = [(i, i ^ 1) for i in range(parts)]
    far = lax.ppermute(near, "tensor", swap)
    full = jnp.concatenate([near, far], 1)
    x, cot = full[0], full[1]

    def turned(v):
        v = v.reshape(chips, 2, local, v.shape[1])
        v = jnp.where(core == 1, v[:, ::-1], v).transpose(1, 0, 2, 3)
        v = lax.dynamic_slice_in_dim(jnp.concatenate([v, v], 1), chip, chips, 1)
        return v.reshape(total, v.shape[3])

    scale, ids = turned(combine), turned(expert_ids)
    common = jnp.argmax(expert_counts).astype(jnp.int32)
    is_first = ids[:, :1] == common
    other = jnp.where(is_first, ids[:, 1:], ids[:, :1])
    weight = jnp.stack(
        [
            jnp.where(is_first, scale[:, :1], scale[:, 1:]),
            jnp.where(is_first, scale[:, 1:], scale[:, :1]),
        ],
        0,
    )
    rg = (weight * cot.astype(F32)[None]).astype(BF16)

    plan = chunk_plan(w_gate.shape[2])
    count = len(plan)
    steps = sequence(count)
    blocks, spans = block_table(plan, steps, experts)
    line = sections == 4
    edge = jnp.logical_or(place == 0, place == sections - 1) if line else jnp.zeros((), bool)
    lane = jnp.arange(128, dtype=jnp.int32)
    head = jnp.where(lane == 0, common, lane - (lane <= common).astype(jnp.int32))
    head = jnp.where(lane == 127, edge.astype(jnp.int32), head)[None]

    own, sent, summed, mine, came = {}, {}, {}, {}, {}
    state = slots = None
    after = ()

    def send(v, pairs):
        return lax.ppermute(v, "section", pairs)

    for name, k in steps:
        if name == "partial":
            slots, own[k], packed, zero = partial_products(
                spans[name, k], len(plan[k]), blocks, head, x, rg, other, weights, slots, after
            )
            sent[k] = send(packed, [(0, 1), (3, 2)]) if line else None
            after = (zero,)
        elif name == "merge" and line:
            summed[k] = own[k] + (sent[k].astype(F32) + zero[0])
            packed = summed[k].astype(BF16)
            sent[k] = send(packed, [(1, 2), (2, 1)])
            after += (packed,)
        elif name == "finish" and line:
            all_of = summed[k] + (sent[k].astype(F32) + zero[1])
            mine[k] = activations(all_of[:, 0], all_of[:, 1], all_of[:, 2])
            came[k] = send(mine[k], [(1, 0), (2, 3)])
            after += (mine[k],)
        elif name == "finish":
            all_of = lax.psum(own[k], "section")
            mine[k] = came[k] = activations(all_of[:, 0], all_of[:, 1], all_of[:, 2])
        elif name == "post":
            slots, state, zero = post_products(
                spans[name, k], blocks, head, mine[k], came[k], rg, weight, other, weights, slots, state,
                after, k == count - 1,
            )
            after = (zero,)
    (d_down, give), keep = state, zero
    both = keep + lax.ppermute(give, "tensor", swap)
    result = both[:, :local]
    for n in range(1, chips):
        piece = both[:, n * local : (n + 1) * local].astype(BF16)
        result += lax.ppermute(piece, "tensor", [(i, (i + 2 * n) % parts) for i in range(parts)]).astype(F32)
    return result[0].astype(BF16), result[1].astype(BF16), d_down


def solution(mesh):
    in_specs = (
        P("tensor", "section"),
        P(),
        P(),
        P(),
        P(None, "section", "tensor"),
        P(None, "section", "tensor"),
        P(None, "tensor", "section"),
        P("tensor", "section"),
    )
    out_specs = (P("tensor", "section"), P("tensor", "section"), P(None, "tensor", "section"))
    return jax.shard_map(
        functools.partial(on_device, mesh.shape["section"], mesh.shape["tensor"]),
        mesh=mesh,
        in_specs=in_specs,
        out_specs=out_specs,
        check_vma=False,
    )
```

time: 206 us -> 186 us (0.903)
  Pallas kernels: 98 us -> 76.7 us
    pallas_call x12 -> x16, Pallas kernels: 98 us -> 76.7 us  [the longest x8 41.4 us: post_products(): pl.pallas_call(functools.partial(post_kernel, span, len(blocks), seen, le...]
    ppermute x18 -> x24, waiting for transfers between devices: 20.9 us -> 18.7 us  [send(): return lax.ppermute(v, 'section', pairs)]
    ppermute x18 -> x24, starting transfers between devices: 50.6 us -> 52.3 us  [send(): return lax.ppermute(v, 'section', pairs)]
  transfers between devices with their start and end apart: 26 -> 32, of which waited for: 10 -> 9; matrix products, arithmetic and copies ran while one was open for 5% -> 6% of each run, Pallas kernels for 42% -> 37%
where the time goes in v3:
time: 186 us; the launch traced here: 185 us
  Pallas kernels  76.7 us (41%)
  starting transfers between devices  60.9 us (33%)
  waiting for transfers between devices  32.2 us (17%)
  other arithmetic  11.2 us (6%)
  local copies, waits for them, and re-layouts  2.68 us (1%)
    ppermute x24, starting transfers between devices, send(): return lax.ppermute(v, 'section', pairs)  52.3 us
    pallas_call x8, Pallas kernels, post_products(): pl.pallas_call(functools.partial(post_kernel, span, len(blocks), seen, le...  41.4 us
    pallas_call x8, Pallas kernels, partial_products(): pl.pallas_call(functools.partial(partial_kernel, span, len(blocks), seen,...  35.4 us
    ppermute x24, waiting for transfers between devices, send(): return lax.ppermute(v, 'section', pairs)  18.7 us
    ppermute x3, waiting for transfers between devices, on_device(): lax.ppermute(piece, 'tensor', [(i, (i + 2 * n) % parts) for i in range(pa...  5.69 us
    ppermute x3, starting transfers between devices, on_device(): lax.ppermute(pair, 'tensor', [(i, (i - 2 * n) % parts) for i in range(par...  5.04 us
  transfers between devices with their start and end apart: 32, of which 9 were waited for; matrix products, arithmetic and copies ran while one was open for 6% of the time, Pallas kernels for 37%

profile of v3, /device:TPU:0, one launch (start us, length us, event | category | flops | bytes accessed | tf_op | source)
XLA Modules:
  0.0 185.3 jit_solution(174615728987316069)
XLA Ops:
  0.7 1.0 pad_maximum_fusion.10
  1.6 3.9 %collective-permute-start = (bf16[2,24,1536]{2,1,0:T(8,128)(2,1)S(1)}, bf16[2,24,1536]{2,1,0:T(8,128)(2,1)S(1)}, u32[]{:S(2)}, u32[]{:S(2)}) collective-permute-start(bf16[2,24,1536]{2,1,0:T(8,128)(2,1)S(1)} %get-tuple-element.228), channel_id=1, source_target_pairs={{0,6},{1,7},{2,0},{3,1},{4,2},{5,3},{6,4},{7,5},{8,14},{9,15},{10,... | collective-permute-start | bytes 442376 | tf_op jit(solution)/shard_map/ppermute | solution.py:301
  5.6 0.5 collective-permute-start.1
  6.1 0.6 collective-permute-start.2
  6.7 0.8 reshape.366
  7.7 0.8 reshape.368
  8.7 0.7 iota_reduce_fusion
  9.3 0.7 select_bitcast_fusion.1
  10.3 0.7 compare_select_fusion.1.head
  11.1 3.0 %collective-permute-done.1 = bf16[2,24,1536]{2,1,0:T(8,128)(2,1)S(1)} collective-permute-done((bf16[2,24,1536]{2,1,0:T(8,128)(2,1)S(1)}, bf16[2,24,1536]{2,1,0:T(8,128)(2,1)S(1)}, u32[]{:S(2)}, u32[]{:S(2)}) %collective-permute-start.1) | collective-permute-done | bytes 147488 | tf_op jit(solution)/shard_map/ppermute | solution.py:301
  14.3 1.9 %collective-permute-done.3 = bf16[2,96,1536]{2,1,0:T(8,128)(2,1)S(1)} collective-permute-done((bf16[2,96,1536]{2,1,0:T(8,128)(2,1)S(1)}, bf16[2,96,1536]{2,1,0:T(8,128)(2,1)S(1)}, u32[]{:S(2)}, u32[]{:S(2)}) %collective-permute-start.3) | collective-permute-done | bytes 589856 | tf_op jit(solution)/shard_map/ppermute | solution.py:305
  16.6 5.3 %partial.8 = (bf16[3,1536,512]{2,1,0:T(8,128)(2,1)S(1)}, bf16[3,1536,512]{2,1,0:T(8,128)(2,1)S(1)}, bf16[3,512,1536]{2,1,0:T(8,128)(2,1)S(1)}, f32[1,3,192,512]{...) custom-call(s32[1,128]{1,0:T(1,128)S(1)} %compare_select_fusion.1.head, ...), custom_call_target="tpu_custom_call" | custom-call | flops 905969664 | bytes 4718592 | tf_op jit(solution)/shard_map/partial/pallas_call | solution.py:139
  21.9 3.5 %collective-permute-start.5 = (bf16[1,3,192,512]{3,2,1,0:T(8,128)(2,1)S(1)}, bf16[1,3,192,512]{3,2,1,0:T(8,128)(2,1)S(1)}, u32[]{:S(2)}, u32[]{:S(2)}) collective-permute-start(bf16[1,3,192,512]{3,2,1,0:T(8,128)(2,1)S(1)} %get-tuple-element.110), channel_id=1, source_target_pairs={{0,8},{24,16},{1,9},{25,17},{2,10},{26,18},{3,11},{27,19},{4,12},{... | collective-permute-start | bytes 1769480 | tf_op jit(solution)/shard_map/ppermute | solution.py:343
  25.4 5.6 %partial.9 = (bf16[3,1536,512]{2,1,0:T(8,128)(2,1)S(1)}, bf16[3,1536,512]{2,1,0:T(8,128)(2,1)S(1)}, bf16[3,512,1536]{2,1,0:T(8,128)(2,1)S(1)}, f32[1,3,192,512]{...) custom-call(s32[1,128]{1,0:T(1,128)S(1)} %compare_select_fusion.1.he, ...), custom_call_target="tpu_custom_call", output_to_operand_aliasing={{0}: (8, {}), {1}: (9, {}), {2}: (10, {})} | custom-call | flops 2717908992 | bytes 14155776 | tf_op jit(solution)/shard_map/partial/pallas_call | solution.py:139
  31.0 5.6 %partial.10 = (bf16[3,1536,512]{2,1,0:T(8,128)(2,1)S(1)}, bf16[3,1536,512]{2,1,0:T(8,128)(2,1)S(1)}, bf16[3,512,1536]{2,1,0:T(8,128)(2,1)S(1)}, f32[1,3,192,512]...) custom-call(s32[1,128]{1,0:T(1,128)S(1)} %compare_select_fusion.1.he, ...), custom_call_target="tpu_custom_call", output_to_operand_aliasing={{0}: (8, {}), {1}: (9, {}), {2}: (10, {})} | custom-call | flops 2717908992 | bytes 14155776 | tf_op jit(solution)/shard_map/partial/pallas_call | solution.py:139
  36.6 1.3 collective-permute-start.4
  37.9 1.3 collective-permute-start.10
  39.5 0.7 collective-permute-start.7
  40.2 5.6 %partial.11 = (bf16[3,1536,512]{2,1,0:T(8,128)(2,1)S(1)}, bf16[3,1536,512]{2,1,0:T(8,128)(2,1)S(1)}, bf16[3,512,1536]{2,1,0:T(8,128)(2,1)S(1)}, f32[1,3,192,512]...) custom-call(s32[1,128]{1,0:T(1,128)S(1)} %compare_select_fusion.1.he, ...), custom_call_target="tpu_custom_call", output_to_operand_aliasing={{0}: (9, {}), {1}: (10, {}), {2}: (11, {})} | custom-call | flops 2717908992 | bytes 14155776 | tf_op jit(solution)/shard_map/partial/pallas_call | solution.py:139
  45.8 5.7 %collective-permute-done.4 = bf16[1,3,192,512]{3,2,1,0:T(8,128)(2,1)S(1)} collective-permute-done((bf16[1,3,192,512]{3,2,1,0:T(8,128)(2,1)S(1)}, bf16[1,3,192,512]{3,2,1,0:T(8,128)(2,1)S(1)}, u32[]{:S(2)}, u32[]{:S(2)}) %collective-permute-start.4) | collective-permute-done | bytes 589856 | tf_op jit(solution)/shard_map/ppermute | solution.py:343
  51.8 0.7 collective-permute-start.6
  52.5 7.2 %collective-permute-start.11 = (bf16[1,3,192,512]{3,2,1,0:T(8,128)(2,1)S(1)}, bf16[1,3,192,512]{3,2,1,0:T(8,128)(2,1)S(1)}, u32[]{:S(2)}, u32[]{:S(2)}) collective-permute-start(bf16[1,3,192,512]{3,2,1,0:T(8,128)(2,1)S(1)} %get-tuple-element.130), channel_id=1, source_target_pairs={{0,8},{24,16},{1,9},{25,17},{2,10},{26,18},{3,11},{27,19},{4,12},{... | collective-permute-start | bytes 1769480 | tf_op jit(solution)/shard_map/ppermute | solution.py:343
  60.4 1.3 collective-permute-start.9
  61.7 5.6 %partial.12 = (bf16[3,1536,512]{2,1,0:T(8,128)(2,1)S(1)}, bf16[3,1536,512]{2,1,0:T(8,128)(2,1)S(1)}, bf16[3,512,1536]{2,1,0:T(8,128)(2,1)S(1)}, f32[1,3,192,512]...) custom-call(s32[1,128]{1,0:T(1,128)S(1)} %compare_select_fusion.1.he, ...), custom_call_target="tpu_custom_call", output_to_operand_aliasing={{0}: (10, {}), {1}: (11, {}), {2}: (12, {})} | custom-call | flops 2717908992 | bytes 14155776 | tf_op jit(solution)/shard_map/partial/pallas_call | solution.py:139
  68.2 0.7 collective-permute-start.12
  68.9 1.3 collective-permute-start.8
  70.2 7.6 %collective-permute-start.13 = (bf16[1,3,192,512]{3,2,1,0:T(8,128)(2,1)S(1)}, bf16[1,3,192,512]{3,2,1,0:T(8,128)(2,1)S(1)}, u32[]{:S(2)}, u32[]{:S(2)}) collective-permute-start(bf16[1,3,192,512]{3,2,1,0:T(8,128)(2,1)S(1)} %get-tuple-element.138), channel_id=1, source_target_pairs={{0,8},{24,16},{1,9},{25,17},{2,10},{26,18},{3,11},{27,19},{4,12},{... | collective-permute-start | bytes 1769480 | tf_op jit(solution)/shard_map/ppermute | solution.py:343
  77.8 2.6 %partial.13 = (bf16[3,1536,512]{2,1,0:T(8,128)(2,1)S(1)}, bf16[3,1536,512]{2,1,0:T(8,128)(2,1)S(1)}, bf16[3,512,1536]{2,1,0:T(8,128)(2,1)S(1)}, f32[1,3,192,512]...) custom-call(s32[1,128]{1,0:T(1,128)S(1)} %compare_select_fusion.1.he, ...), custom_call_target="tpu_custom_call", output_to_operand_aliasing={{0}: (10, {}), {1}: (11, {}), {2}: (12, {})} | custom-call | flops 905969664 | bytes 4718592 | tf_op jit(solution)/shard_map/partial/pallas_call | solution.py:139
  80.4 1.3 collective-permute-start.15
  81.8 3.2 %post.8 = (bf16[3,1536,512]{2,1,0:T(8,128)(2,1)S(1)}, bf16[3,1536,512]{2,1,0:T(8,128)(2,1)S(1)}, bf16[3,512,1536]{2,1,0:T(8,128)(2,1)S(1)}, bf16[4,2048,1536]{2,...) custom-call(s32[1,128]{1,0:T(1,128)S(1)} %compare_select_fusion.1.he, ...), custom_call_target="tpu_custom_call", output_to_operand_aliasing={{0}: (10, {}), {1}: (11, {}), {2}: (12, {})} | custom-call | flops 1207959552 | bytes 4718592 | tf_op jit(solution)/shard_map/post/pallas_call | solution.py:225
  85.2 0.9 collective-permute-start.14
  86.7 1.3 collective-permute-start.18
  88.3 7.6 %post.9 = (bf16[3,1536,512]{2,1,0:T(8,128)(2,1)S(1)}, bf16[3,1536,512]{2,1,0:T(8,128)(2,1)S(1)}, bf16[3,512,1536]{2,1,0:T(8,128)(2,1)S(1)}, bf16[4,2048,1536]{2,...) custom-call(s32[1,128]{1,0:T(1,128)S(1)} %compare_select_fusion.1.he, ...), custom_call_target="tpu_custom_call", output_to_operand_aliasing={{0}: (12, {}), {1}: (13, {}), {2}: (14, {}), {3}: (16, {}),... | custom-call | flops 3623878656 | bytes 14155776 | tf_op jit(solution)/shard_map/post/pallas_call | solution.py:225
  96.2 0.7 collective-permute-start.19
  97.6 1.3 collective-permute-start.17
  98.9 2.6 %partial.14 = (bf16[3,1536,512]{2,1,0:T(8,128)(2,1)S(1)}, bf16[3,1536,512]{2,1,0:T(8,128)(2,1)S(1)}, bf16[3,512,1536]{2,1,0:T(8,128)(2,1)S(1)}, f32[1,3,192,512]...) custom-call(s32[1,128]{1,0:T(1,128)S(1)} %compare_select_fusion.1.he, ...), custom_call_target="tpu_custom_call", output_to_operand_aliasing={{0}: (10, {}), {1}: (11, {}), {2}: (12, {})} | custom-call | flops 905969664 | bytes 4718592 | tf_op jit(solution)/shard_map/partial/pallas_call | solution.py:139
  101.7 0.7 collective-permute-start.21
  102.5 2.6 %partial.15 = (bf16[3,1536,512]{2,1,0:T(8,128)(2,1)S(1)}, bf16[3,1536,512]{2,1,0:T(8,128)(2,1)S(1)}, bf16[3,512,1536]{2,1,0:T(8,128)(2,1)S(1)}, f32[1,3,192,512]...) custom-call(s32[1,128]{1,0:T(1,128)S(1)} %compare_select_fusion.1.he, ...), custom_call_target="tpu_custom_call", output_to_operand_aliasing={{0}: (9, {}), {1}: (10, {}), {2}: (11, {})} | custom-call | flops 905969664 | bytes 4718592 | tf_op jit(solution)/shard_map/partial/pallas_call | solution.py:139
  105.1 8.8 %collective-permute-start.20 = (bf16[1,3,192,512]{3,2,1,0:T(8,128)(2,1)S(1)}, bf16[1,3,192,512]{3,2,1,0:T(8,128)(2,1)S(1)}, u32[]{:S(2)}, u32[]{:S(2)}) collective-permute-start(bf16[1,3,192,512]{3,2,1,0:T(8,128)(2,1)S(1)} %get-tuple-element.158), channel_id=1, source_target_pairs={{0,8},{24,16},{1,9},{25,17},{2,10},{26,18},{3,11},{27,19},{4,12},{... | collective-permute-start | bytes 1769480 | tf_op jit(solution)/shard_map/ppermute | solution.py:343
  113.9 4.8 %collective-permute-start.16 = (bf16[1,3,192,512]{3,2,1,0:T(8,128)(2,1)S(1)}, bf16[1,3,192,512]{3,2,1,0:T(8,128)(2,1)S(1)}, u32[]{:S(2)}, u32[]{:S(2)}) collective-permute-start(bf16[1,3,192,512]{3,2,1,0:T(8,128)(2,1)S(1)} %get-tuple-element.149), channel_id=1, source_target_pairs={{0,8},{24,16},{1,9},{25,17},{2,10},{26,18},{3,11},{27,19},{4,12},{... | collective-permute-start | bytes 1769480 | tf_op jit(solution)/shard_map/ppermute | solution.py:343
  119.4 1.3 collective-permute-start.24
  120.7 7.6 %post.10 = (bf16[3,1536,512]{2,1,0:T(8,128)(2,1)S(1)}, bf16[3,1536,512]{2,1,0:T(8,128)(2,1)S(1)}, bf16[3,512,1536]{2,1,0:T(8,128)(2,1)S(1)}, bf16[4,2048,1536]{2...) custom-call(s32[1,128]{1,0:T(1,128)S(1)} %compare_select_fusion.1.he, ...), custom_call_target="tpu_custom_call", output_to_operand_aliasing={{0}: (11, {}), {1}: (12, {}), {2}: (13, {}), {3}: (15, {}),... | custom-call | flops 3623878656 | bytes 14155776 | tf_op jit(solution)/shard_map/post/pallas_call | solution.py:225
  128.6 0.7 collective-permute-start.25
  129.3 0.3 add_add_fusion.3
  130.0 1.3 collective-permute-start.23
  131.3 7.6 %post.11 = (bf16[3,1536,512]{2,1,0:T(8,128)(2,1)S(1)}, bf16[3,1536,512]{2,1,0:T(8,128)(2,1)S(1)}, bf16[3,512,1536]{2,1,0:T(8,128)(2,1)S(1)}, bf16[4,2048,1536]{2...) custom-call(s32[1,128]{1,0:T(1,128)S(1)} %compare_select_fusion.1.he, ...), custom_call_target="tpu_custom_call", output_to_operand_aliasing={{0}: (12, {}), {1}: (13, {}), {2}: (14, {}), {3}: (16, {}),... | custom-call | flops 3623878656 | bytes 14155776 | tf_op jit(solution)/shard_map/post/pallas_call | solution.py:225
  139.2 0.7 collective-permute-start.22
  139.9 0.3 add_add_fusion.1
  140.6 1.5 collective-permute-start.27
  142.1 7.6 %post.12 = (bf16[3,1536,512]{2,1,0:T(8,128)(2,1)S(1)}, bf16[3,1536,512]{2,1,0:T(8,128)(2,1)S(1)}, bf16[3,512,1536]{2,1,0:T(8,128)(2,1)S(1)}, bf16[4,2048,1536]{2...) custom-call(s32[1,128]{1,0:T(1,128)S(1)} %compare_select_fusion.1.he, ...), custom_call_target="tpu_custom_call", output_to_operand_aliasing={{0}: (12, {}), {1}: (13, {}), {2}: (14, {}), {3}: (16, {}),... | custom-call | flops 3623878656 | bytes 14155776 | tf_op jit(solution)/shard_map/post/pallas_call | solution.py:225
  149.8 3.1 %post.13 = (bf16[3,1536,512]{2,1,0:T(8,128)(2,1)S(1)}, bf16[3,1536,512]{2,1,0:T(8,128)(2,1)S(1)}, bf16[3,512,1536]{2,1,0:T(8,128)(2,1)S(1)}, bf16[4,2048,1536]{2...) custom-call(s32[1,128]{1,0:T(1,128)S(1)} %compare_select_fusion.1.he, ...), custom_call_target="tpu_custom_call", output_to_operand_aliasing={{0}: (10, {}), {1}: (11, {}), {2}: (12, {}), {3}: (14, {}),... | custom-call | flops 1207959552 | bytes 4718592 | tf_op jit(solution)/shard_map/post/pallas_call | solution.py:225
  152.9 0.3 add_add_fusion
  153.6 1.3 collective-permute-start.26
  154.9 4.0 %collective-permute-done.27.came = bf16[1,3,192,512]{3,2,1,0:T(8,128)(2,1)S(1)} collective-permute-done((bf16[1,3,192,512]{3,2,1,0:T(8,128)(2,1)S(1)}, bf16[1,3,192,512]{3,2,1,0:T(8,128)(2,1)S(1)}, u32[]{:S(2)}, u32[]{:S(2)}) %collective-permute-start.27) | collective-permute-done | bytes 589856 | tf_op jit(solution)/shard_map/ppermute | solution.py:343
  158.9 2.3 %post.14 = (bf16[3,1536,512]{2,1,0:T(8,128)(2,1)S(1)}, bf16[3,1536,512]{2,1,0:T(8,128)(2,1)S(1)}, bf16[3,512,1536]{2,1,0:T(8,128)(2,1)S(1)}, bf16[4,2048,1536]{2...) custom-call(s32[1,128]{1,0:T(1,128)S(1)} %compare_select_fusion.1.he, ...), custom_call_target="tpu_custom_call", output_to_operand_aliasing={{0}: (11, {}), {1}: (12, {}), {2}: (13, {}), {3}: (15, {}),... | custom-call | flops 1207959552 | bytes 4718592 | tf_op jit(solution)/shard_map/post/pallas_call | solution.py:225
  161.2 8.6 %collective-permute-done.26.came = bf16[1,3,192,512]{3,2,1,0:T(8,128)(2,1)S(1)} collective-permute-done((bf16[1,3,192,512]{3,2,1,0:T(8,128)(2,1)S(1)}, bf16[1,3,192,512]{3,2,1,0:T(8,128)(2,1)S(1)}, u32[]{:S(2)}, u32[]{:S(2)}) %collective-permute-start.26) | collective-permute-done | bytes 589856 | tf_op jit(solution)/shard_map/ppermute | solution.py:343
  169.9 2.3 %post.15 = (bf16[3,1536,512]{2,1,0:T(8,128)(2,1)S(1)}, bf16[3,1536,512]{2,1,0:T(8,128)(2,1)S(1)}, bf16[3,512,1536]{2,1,0:T(8,128)(2,1)S(1)}, bf16[4,2048,1536]{2...) custom-call(s32[1,128]{1,0:T(1,128)S(1)} %compare_select_fusion.1.he, ...), custom_call_target="tpu_custom_call", output_to_operand_aliasing={{0}: (10, {}), {1}: (11, {}), {2}: (12, {}), {3}: (14, {})} | custom-call | flops 1207959552 | bytes 4718592 | tf_op jit(solution)/shard_map/post/pallas_call | solution.py:225
  172.3 2.8 %collective-permute-done.28 = f32[2,96,1536]{2,1,0:T(8,128)S(1)} collective-permute-done((f32[2,96,1536]{2,1,0:T(8,128)S(1)}, f32[2,96,1536]{2,1,0:T(8,128)S(1)}, u32[]{:S(2)}, u32[]{:S(2)}) %collective-permute-start.28) | collective-permute-done | bytes 1179680 | tf_op jit(solution)/shard_map/ppermute | solution.py:372
  175.4 0.4 collective-permute-start.29
  175.7 0.8 collective-permute-start.30
  176.5 2.3 %collective-permute-start.31 = (bf16[2,24,1536]{2,1,0:T(8,128)(2,1)S(1)}, bf16[2,24,1536]{2,1,0:T(8,128)(2,1)S(1)}, u32[]{:S(2)}, u32[]{:S(2)}) collective-permute-start(bf16[2,24,1536]{2,1,0:T(8,128)(2,1)S(1)} %get-tuple-element.222), channel_id=1, source_target_pairs={{0,6},{1,7},{2,0},{3,1},{4,2},{5,3},{6,4},{7,5},{8,14},{9,15},{10,... | collective-permute-start | bytes 442376 | tf_op jit(solution)/shard_map/ppermute | solution.py:376
  178.9 4.2 %collective-permute-done.29 = bf16[2,24,1536]{2,1,0:T(8,128)(2,1)S(1)} collective-permute-done((bf16[2,24,1536]{2,1,0:T(8,128)(2,1)S(1)}, bf16[2,24,1536]{2,1,0:T(8,128)(2,1)S(1)}, u32[]{:S(2)}, u32[]{:S(2)}) %collective-permute-start.29) | collective-permute-done | bytes 147488 | tf_op jit(solution)/shard_map/ppermute | solution.py:376
  183.0 1.5 collective-permute-done.30
  184.6 0.7 slice_bitcast_fusion.2
  (96 shorter events, 8.2 us)
Async XLA Ops:
  0.6 8.0 %copy-start = (s32[4]{0:T(128)S(1)}, s32[4]{0:T(128)}, u32[]{:S(2)}) copy-start(s32[4]{0:T(128)} %param.11) | copy-start | bytes 52
  0.6 13.4 %copy-start.2 = (bf16[24,1536]{1,0:T(8,128)(2,1)S(1)}, bf16[24,1536]{1,0:T(8,128)(2,1)}, u32[]{:S(2)}) copy-start(bf16[24,1536]{1,0:T(8,128)(2,1)} %param.15) | copy-start | bytes 221188
  0.7 13.4 %copy-start.3 = (bf16[24,1536]{1,0:T(8,128)(2,1)S(1)}, bf16[24,1536]{1,0:T(8,128)(2,1)}, u32[]{:S(2)}) copy-start(bf16[24,1536]{1,0:T(8,128)(2,1)} %param.8) | copy-start | bytes 221188
  1.6 9.4 %collective-permute-start = (bf16[2,24,1536]{2,1,0:T(8,128)(2,1)S(1)}, bf16[2,24,1536]{2,1,0:T(8,128)(2,1)S(1)}, u32[]{:S(2)}, u32[]{:S(2)}) collective-permute-start(bf16[2,24,1536]{2,1,0:T(8,128)(2,1)S(1)} %get-tuple-element.228), channel_id=1, source_target_pairs={{0,6},{1,7},{2,0},{3,1},{4,2},{5,3},{6,4},{7,5},{8,14},{9,15},{10,... | collective-permute-start | bytes 442376 | tf_op jit(solution)/shard_map/ppermute | solution.py:301
  5.6 8.5 %collective-permute-start.1 = (bf16[2,24,1536]{2,1,0:T(8,128)(2,1)S(1)}, bf16[2,24,1536]{2,1,0:T(8,128)(2,1)S(1)}, u32[]{:S(2)}, u32[]{:S(2)}) collective-permute-start(bf16[2,24,1536]{2,1,0:T(8,128)(2,1)S(1)} %get-tuple-element.228), channel_id=1, source_target_pairs={{0,4},{1,5},{2,6},{3,7},{4,0},{5,1},{6,2},{7,3},{8,12},{9,13},{10,... | collective-permute-start | bytes 442376 | tf_op jit(solution)/shard_map/ppermute | solution.py:301
  6.1 8.0 %collective-permute-start.2 = (bf16[2,24,1536]{2,1,0:T(8,128)(2,1)S(1)}, bf16[2,24,1536]{2,1,0:T(8,128)(2,1)S(1)}, u32[]{:S(2)}, u32[]{:S(2)}) collective-permute-start(bf16[2,24,1536]{2,1,0:T(8,128)(2,1)S(1)} %get-tuple-element.228), channel_id=1, source_target_pairs={{0,2},{1,3},{2,4},{3,5},{4,6},{5,7},{6,0},{7,1},{8,10},{9,11},{10,... | collective-permute-start | bytes 442376 | tf_op jit(solution)/shard_map/ppermute | solution.py:301
  14.1 2.1 %collective-permute-start.3 = (bf16[2,96,1536]{2,1,0:T(8,128)(2,1)S(1)}, bf16[2,96,1536]{2,1,0:T(8,128)(2,1)S(1)}, u32[]{:S(2)}, u32[]{:S(2)}) collective-permute-start(bf16[2,96,1536]{2,1,0:T(8,128)(2,1)S(1)} %pad_maximum_fusion), channel_id=1, source_target_pairs={{0,1},{1,0},{2,3},{3,2},{4,5},{5,4},{6,7},{7,6},{8,9},{9,8},{10,11... | collective-permute-start | bytes 1769480 | tf_op jit(solution)/shard_map/ppermute | solution.py:305
  21.9 17.4 %collective-permute-start.5 = (bf16[1,3,192,512]{3,2,1,0:T(8,128)(2,1)S(1)}, bf16[1,3,192,512]{3,2,1,0:T(8,128)(2,1)S(1)}, u32[]{:S(2)}, u32[]{:S(2)}) collective-permute-start(bf16[1,3,192,512]{3,2,1,0:T(8,128)(2,1)S(1)} %get-tuple-element.110), channel_id=1, source_target_pairs={{0,8},{24,16},{1,9},{25,17},{2,10},{26,18},{3,11},{27,19},{4,12},{... | collective-permute-start | bytes 1769480 | tf_op jit(solution)/shard_map/ppermute | solution.py:343
  36.6 15.0 %collective-permute-start.4 = (bf16[1,3,192,512]{3,2,1,0:T(8,128)(2,1)S(1)}, bf16[1,3,192,512]{3,2,1,0:T(8,128)(2,1)S(1)}, u32[]{:S(2)}, u32[]{:S(2)}) collective-permute-start(bf16[1,3,192,512]{3,2,1,0:T(8,128)(2,1)S(1)} %get-tuple-element.103), channel_id=1, source_target_pairs={{0,8},{24,16},{1,9},{25,17},{2,10},{26,18},{3,11},{27,19},{4,12},{... | collective-permute-start | bytes 1769480 | tf_op jit(solution)/shard_map/ppermute | solution.py:343
  37.9 29.7 %collective-permute-start.10 = (bf16[1,3,192,512]{3,2,1,0:T(8,128)(2,1)S(1)}, bf16[1,3,192,512]{3,2,1,0:T(8,128)(2,1)S(1)}, u32[]{:S(2)}, u32[]{:S(2)}) collective-permute-start(bf16[1,3,192,512]{3,2,1,0:T(8,128)(2,1)S(1)} %get-tuple-element.120), channel_id=1, source_target_pairs={{0,8},{24,16},{1,9},{25,17},{2,10},{26,18},{3,11},{27,19},{4,12},{... | collective-permute-start | bytes 1769480 | tf_op jit(solution)/shard_map/ppermute | solution.py:343
  39.5 20.2 %collective-permute-start.7 = (bf16[1,3,192,512]{3,2,1,0:T(8,128)(2,1)S(1)}, bf16[1,3,192,512]{3,2,1,0:T(8,128)(2,1)S(1)}, u32[]{:S(2)}, u32[]{:S(2)}) collective-permute-start(bf16[1,3,192,512]{3,2,1,0:T(8,128)(2,1)S(1)} %fusion.rest_1_), channel_id=1, source_target_pairs={{8,16},{16,8},{9,17},{17,9},{10,18},{18,10},{11,19},{19,11},{12,20... | collective-permute-start | bytes 1769480 | tf_op jit(solution)/shard_map/ppermute | solution.py:343
  51.8 15.5 %collective-permute-start.6 = (bf16[1,3,192,512]{3,2,1,0:T(8,128)(2,1)S(1)}, bf16[1,3,192,512]{3,2,1,0:T(8,128)(2,1)S(1)}, u32[]{:S(2)}, u32[]{:S(2)}) collective-permute-start(bf16[1,3,192,512]{3,2,1,0:T(8,128)(2,1)S(1)} %fusion.1.rest_1_), channel_id=1, source_target_pairs={{8,16},{16,8},{9,17},{17,9},{10,18},{18,10},{11,19},{19,11},{12,20... | collective-permute-start | bytes 1769480 | tf_op jit(solution)/shard_map/ppermute | solution.py:343
  52.5 32.4 %collective-permute-start.11 = (bf16[1,3,192,512]{3,2,1,0:T(8,128)(2,1)S(1)}, bf16[1,3,192,512]{3,2,1,0:T(8,128)(2,1)S(1)}, u32[]{:S(2)}, u32[]{:S(2)}) collective-permute-start(bf16[1,3,192,512]{3,2,1,0:T(8,128)(2,1)S(1)} %get-tuple-element.130), channel_id=1, source_target_pairs={{0,8},{24,16},{1,9},{25,17},{2,10},{26,18},{3,11},{27,19},{4,12},{... | collective-permute-start | bytes 1769480 | tf_op jit(solution)/shard_map/ppermute | solution.py:343
  60.4 20.0 %collective-permute-start.9 = (bf16[1,3,192,512]{3,2,1,0:T(8,128)(2,1)S(1)}, bf16[1,3,192,512]{3,2,1,0:T(8,128)(2,1)S(1)}, u32[]{:S(2)}, u32[]{:S(2)}) collective-permute-start(bf16[1,3,192,512]{3,2,1,0:T(8,128)(2,1)S(1)} %pad_maximum_fusion.1.rest_2_.mine), channel_id=1, source_target_pairs={{8,0},{16,24},{9,1},{17,25},{10,2},{18,26},{11,3},{19,27},{12,4},{... | collective-permute-start | bytes 1769480 | tf_op jit(solution)/shard_map/ppermute | solution.py:343
  68.2 17.9 %collective-permute-start.12 = (bf16[1,3,192,512]{3,2,1,0:T(8,128)(2,1)S(1)}, bf16[1,3,192,512]{3,2,1,0:T(8,128)(2,1)S(1)}, u32[]{:S(2)}, u32[]{:S(2)}) collective-permute-start(bf16[1,3,192,512]{3,2,1,0:T(8,128)(2,1)S(1)} %fusion.2.rest_1_), channel_id=1, source_target_pairs={{8,16},{16,8},{9,17},{17,9},{10,18},{18,10},{11,19},{19,11},{12,20... | collective-permute-start | bytes 1769480 | tf_op jit(solution)/shard_map/ppermute | solution.py:343
  68.9 19.4 %collective-permute-start.8 = (bf16[1,3,192,512]{3,2,1,0:T(8,128)(2,1)S(1)}, bf16[1,3,192,512]{3,2,1,0:T(8,128)(2,1)S(1)}, u32[]{:S(2)}, u32[]{:S(2)}) collective-permute-start(bf16[1,3,192,512]{3,2,1,0:T(8,128)(2,1)S(1)} %pad_maximum_fusion.2.rest_2_.mine), channel_id=1, source_target_pairs={{8,0},{16,24},{9,1},{17,25},{10,2},{18,26},{11,3},{19,27},{12,4},{... | collective-permute-start | bytes 1769480 | tf_op jit(solution)/shard_map/ppermute | solution.py:343
  70.2 25.7 %collective-permute-start.13 = (bf16[1,3,192,512]{3,2,1,0:T(8,128)(2,1)S(1)}, bf16[1,3,192,512]{3,2,1,0:T(8,128)(2,1)S(1)}, u32[]{:S(2)}, u32[]{:S(2)}) collective-permute-start(bf16[1,3,192,512]{3,2,1,0:T(8,128)(2,1)S(1)} %get-tuple-element.138), channel_id=1, source_target_pairs={{0,8},{24,16},{1,9},{25,17},{2,10},{26,18},{3,11},{27,19},{4,12},{... | collective-permute-start | bytes 1769480 | tf_op jit(solution)/shard_map/ppermute | solution.py:343
  80.4 21.1 %collective-permute-start.15 = (bf16[1,3,192,512]{3,2,1,0:T(8,128)(2,1)S(1)}, bf16[1,3,192,512]{3,2,1,0:T(8,128)(2,1)S(1)}, u32[]{:S(2)}, u32[]{:S(2)}) collective-permute-start(bf16[1,3,192,512]{3,2,1,0:T(8,128)(2,1)S(1)} %get-tuple-element.144), channel_id=1, source_target_pairs={{0,8},{24,16},{1,9},{25,17},{2,10},{26,18},{3,11},{27,19},{4,12},{... | collective-permute-start | bytes 1769480 | tf_op jit(solution)/shard_map/ppermute | solution.py:343
  85.2 11.7 %collective-permute-start.14 = (bf16[1,3,192,512]{3,2,1,0:T(8,128)(2,1)S(1)}, bf16[1,3,192,512]{3,2,1,0:T(8,128)(2,1)S(1)}, u32[]{:S(2)}, u32[]{:S(2)}) collective-permute-start(bf16[1,3,192,512]{3,2,1,0:T(8,128)(2,1)S(1)} %fusion.3.rest_1_), channel_id=1, source_target_pairs={{8,16},{16,8},{9,17},{17,9},{10,18},{18,10},{11,19},{19,11},{12,20... | collective-permute-start | bytes 1769480 | tf_op jit(solution)/shard_map/ppermute | solution.py:343
  86.7 32.7 %collective-permute-start.18 = (bf16[1,3,192,512]{3,2,1,0:T(8,128)(2,1)S(1)}, bf16[1,3,192,512]{3,2,1,0:T(8,128)(2,1)S(1)}, u32[]{:S(2)}, u32[]{:S(2)}) collective-permute-start(bf16[1,3,192,512]{3,2,1,0:T(8,128)(2,1)S(1)} %pad_maximum_fusion.3.rest_2_.mine), channel_id=1, source_target_pairs={{8,0},{16,24},{9,1},{17,25},{10,2},{18,26},{11,3},{19,27},{12,4},{... | collective-permute-start | bytes 1769480 | tf_op jit(solution)/shard_map/ppermute | solution.py:343
  96.2 17.7 %collective-permute-start.19 = (bf16[1,3,192,512]{3,2,1,0:T(8,128)(2,1)S(1)}, bf16[1,3,192,512]{3,2,1,0:T(8,128)(2,1)S(1)}, u32[]{:S(2)}, u32[]{:S(2)}) collective-permute-start(bf16[1,3,192,512]{3,2,1,0:T(8,128)(2,1)S(1)} %fusion.4.rest_1_), channel_id=1, source_target_pairs={{8,16},{16,8},{9,17},{17,9},{10,18},{18,10},{11,19},{19,11},{12,20... | collective-permute-start | bytes 1769480 | tf_op jit(solution)/shard_map/ppermute | solution.py:343
  97.6 33.7 %collective-permute-start.17 = (bf16[1,3,192,512]{3,2,1,0:T(8,128)(2,1)S(1)}, bf16[1,3,192,512]{3,2,1,0:T(8,128)(2,1)S(1)}, u32[]{:S(2)}, u32[]{:S(2)}) collective-permute-start(bf16[1,3,192,512]{3,2,1,0:T(8,128)(2,1)S(1)} %pad_maximum_fusion.4.rest_2_.mine), channel_id=1, source_target_pairs={{8,0},{16,24},{9,1},{17,25},{10,2},{18,26},{11,3},{19,27},{12,4},{... | collective-permute-start | bytes 1769480 | tf_op jit(solution)/shard_map/ppermute | solution.py:343
  101.7 27.5 %collective-permute-start.21 = (bf16[1,3,192,512]{3,2,1,0:T(8,128)(2,1)S(1)}, bf16[1,3,192,512]{3,2,1,0:T(8,128)(2,1)S(1)}, u32[]{:S(2)}, u32[]{:S(2)}) collective-permute-start(bf16[1,3,192,512]{3,2,1,0:T(8,128)(2,1)S(1)} %fusion.5.rest_1_), channel_id=1, source_target_pairs={{8,16},{16,8},{9,17},{17,9},{10,18},{18,10},{11,19},{19,11},{12,20... | collective-permute-start | bytes 1769480 | tf_op jit(solution)/shard_map/ppermute | solution.py:343
  105.1 23.3 %collective-permute-start.20 = (bf16[1,3,192,512]{3,2,1,0:T(8,128)(2,1)S(1)}, bf16[1,3,192,512]{3,2,1,0:T(8,128)(2,1)S(1)}, u32[]{:S(2)}, u32[]{:S(2)}) collective-permute-start(bf16[1,3,192,512]{3,2,1,0:T(8,128)(2,1)S(1)} %get-tuple-element.158), channel_id=1, source_target_pairs={{0,8},{24,16},{1,9},{25,17},{2,10},{26,18},{3,11},{27,19},{4,12},{... | collective-permute-start | bytes 1769480 | tf_op jit(solution)/shard_map/ppermute | solution.py:343
  113.9 25.0 %collective-permute-start.16 = (bf16[1,3,192,512]{3,2,1,0:T(8,128)(2,1)S(1)}, bf16[1,3,192,512]{3,2,1,0:T(8,128)(2,1)S(1)}, u32[]{:S(2)}, u32[]{:S(2)}) collective-permute-start(bf16[1,3,192,512]{3,2,1,0:T(8,128)(2,1)S(1)} %get-tuple-element.149), channel_id=1, source_target_pairs={{0,8},{24,16},{1,9},{25,17},{2,10},{26,18},{3,11},{27,19},{4,12},{... | collective-permute-start | bytes 1769480 | tf_op jit(solution)/shard_map/ppermute | solution.py:343
  119.4 22.7 %collective-permute-start.24 = (bf16[1,3,192,512]{3,2,1,0:T(8,128)(2,1)S(1)}, bf16[1,3,192,512]{3,2,1,0:T(8,128)(2,1)S(1)}, u32[]{:S(2)}, u32[]{:S(2)}) collective-permute-start(bf16[1,3,192,512]{3,2,1,0:T(8,128)(2,1)S(1)} %pad_maximum_fusion.5.rest_1_.mine), channel_id=1, source_target_pairs={{8,0},{16,24},{9,1},{17,25},{10,2},{18,26},{11,3},{19,27},{12,4},{... | collective-permute-start | bytes 1769480 | tf_op jit(solution)/shard_map/ppermute | solution.py:343
  128.6 11.3 %collective-permute-start.25 = (bf16[1,3,192,512]{3,2,1,0:T(8,128)(2,1)S(1)}, bf16[1,3,192,512]{3,2,1,0:T(8,128)(2,1)S(1)}, u32[]{:S(2)}, u32[]{:S(2)}) collective-permute-start(bf16[1,3,192,512]{3,2,1,0:T(8,128)(2,1)S(1)} %fusion.6.rest_1_), channel_id=1, source_target_pairs={{8,16},{16,8},{9,17},{17,9},{10,18},{18,10},{11,19},{19,11},{12,20... | collective-permute-start | bytes 1769480 | tf_op jit(solution)/shard_map/ppermute | solution.py:343
  130.0 19.8 %collective-permute-start.23 = (bf16[1,3,192,512]{3,2,1,0:T(8,128)(2,1)S(1)}, bf16[1,3,192,512]{3,2,1,0:T(8,128)(2,1)S(1)}, u32[]{:S(2)}, u32[]{:S(2)}) collective-permute-start(bf16[1,3,192,512]{3,2,1,0:T(8,128)(2,1)S(1)} %pad_maximum_fusion.6.rest_2_.mine), channel_id=1, source_target_pairs={{8,0},{16,24},{9,1},{17,25},{10,2},{18,26},{11,3},{19,27},{12,4},{... | collective-permute-start | bytes 1769480 | tf_op jit(solution)/shard_map/ppermute | solution.py:343
  139.2 13.7 %collective-permute-start.22 = (bf16[1,3,192,512]{3,2,1,0:T(8,128)(2,1)S(1)}, bf16[1,3,192,512]{3,2,1,0:T(8,128)(2,1)S(1)}, u32[]{:S(2)}, u32[]{:S(2)}) collective-permute-start(bf16[1,3,192,512]{3,2,1,0:T(8,128)(2,1)S(1)} %fusion.7.rest_1_), channel_id=1, source_target_pairs={{8,16},{16,8},{9,17},{17,9},{10,18},{18,10},{11,19},{19,11},{12,20... | collective-permute-start | bytes 1769480 | tf_op jit(solution)/shard_map/ppermute | solution.py:343
  140.6 18.3 %collective-permute-start.27 = (bf16[1,3,192,512]{3,2,1,0:T(8,128)(2,1)S(1)}, bf16[1,3,192,512]{3,2,1,0:T(8,128)(2,1)S(1)}, u32[]{:S(2)}, u32[]{:S(2)}) collective-permute-start(bf16[1,3,192,512]{3,2,1,0:T(8,128)(2,1)S(1)} %pad_maximum_fusion.7.rest_2_.mine), channel_id=1, source_target_pairs={{8,0},{16,24},{9,1},{17,25},{10,2},{18,26},{11,3},{19,27},{12,4},{... | collective-permute-start | bytes 1769480 | tf_op jit(solution)/shard_map/ppermute | solution.py:343
  153.6 16.3 %collective-permute-start.26 = (bf16[1,3,192,512]{3,2,1,0:T(8,128)(2,1)S(1)}, bf16[1,3,192,512]{3,2,1,0:T(8,128)(2,1)S(1)}, u32[]{:S(2)}, u32[]{:S(2)}) collective-permute-start(bf16[1,3,192,512]{3,2,1,0:T(8,128)(2,1)S(1)} %pad_maximum_fusion.8.rest_1_.mine), channel_id=1, source_target_pairs={{8,0},{16,24},{9,1},{17,25},{10,2},{18,26},{11,3},{19,27},{12,4},{... | collective-permute-start | bytes 1769480 | tf_op jit(solution)/shard_map/ppermute | solution.py:343
  172.2 2.9 %collective-permute-start.28 = (f32[2,96,1536]{2,1,0:T(8,128)S(1)}, f32[2,96,1536]{2,1,0:T(8,128)S(1)}, u32[]{:S(2)}, u32[]{:S(2)}) collective-permute-start(f32[2,96,1536]{2,1,0:T(8,128)S(1)} %get-tuple-element.189), channel_id=1, source_target_pairs={{0,1},{1,0},{2,3},{3,2},{4,5},{5,4},{6,7},{7,6},{8,9},{9,8},{10,11... | collective-permute-start | bytes 3538952 | tf_op jit(solution)/shard_map/ppermute | solution.py:372
  175.1 10.2 %copy-start.1 = (s32[4]{0:T(128)S(1)}, s32[4]{0:T(128)}, u32[]{:S(2)}) copy-start(s32[4]{0:T(128)} %param.11) | copy-start | bytes 52
  175.4 7.7 %collective-permute-start.29 = (bf16[2,24,1536]{2,1,0:T(8,128)(2,1)S(1)}, bf16[2,24,1536]{2,1,0:T(8,128)(2,1)S(1)}, u32[]{:S(2)}, u32[]{:S(2)}) collective-permute-start(bf16[2,24,1536]{2,1,0:T(8,128)(2,1)S(1)} %get-tuple-element.221), channel_id=1, source_target_pairs={{0,2},{1,3},{2,4},{3,5},{4,6},{5,7},{6,0},{7,1},{8,10},{9,11},{10,... | collective-permute-start | bytes 442376 | tf_op jit(solution)/shard_map/ppermute | solution.py:376
  175.7 8.8 %collective-permute-start.30 = (bf16[2,24,1536]{2,1,0:T(8,128)(2,1)S(1)}, bf16[2,24,1536]{2,1,0:T(8,128)(2,1)S(1)}, u32[]{:S(2)}, u32[]{:S(2)}) collective-permute-start(bf16[2,24,1536]{2,1,0:T(8,128)(2,1)S(1)} %get-tuple-element.223), channel_id=1, source_target_pairs={{0,4},{1,5},{2,6},{3,7},{4,0},{5,1},{6,2},{7,3},{8,12},{9,13},{10,... | collective-permute-start | bytes 442376 | tf_op jit(solution)/shard_map/ppermute | solution.py:376
  176.5 8.0 %collective-permute-start.31 = (bf16[2,24,1536]{2,1,0:T(8,128)(2,1)S(1)}, bf16[2,24,1536]{2,1,0:T(8,128)(2,1)S(1)}, u32[]{:S(2)}, u32[]{:S(2)}) collective-permute-start(bf16[2,24,1536]{2,1,0:T(8,128)(2,1)S(1)} %get-tuple-element.222), channel_id=1, source_target_pairs={{0,6},{1,7},{2,0},{3,1},{4,2},{5,3},{6,4},{7,5},{8,14},{9,15},{10,... | collective-permute-start | bytes 442376 | tf_op jit(solution)/shard_map/ppermute | solution.py:376

commit v4 on v3

--- a/solution.py
+++ b/solution.py
@@ -12,7 +12,7 @@
 SLOTS = EARLY + 1
 F32 = jnp.float32
 BF16 = jnp.bfloat16
-COST_SCALE = 1
+COST_FACTOR = 4.0
 VMEM_LIMIT = 20 * 1024 * 1024
 ANY = pl.BlockSpec(memory_space=pl.ANY)
 HBM = pl.BlockSpec(memory_space=pltpu.HBM)
@@ -44,19 +44,34 @@
     )
 
 
+def begin_all(copies):
+    for copy in copies:
+        copy.start()
+
+
+def wait_all(copies):
+    for copy in copies:
+        copy.wait()
+
+
+def preload_kernel(rows, head, wg, wu, wd, b0, b1, b2, table, wsem):
+    field = fill_table(rows, 0, head, table)
+    copies = [weight_copies(field, i, (wg, wu, wd), (b0, b1, b2), wsem) for i in range(len(rows))]
+    for copy in copies:
+        begin_all(copy)
+    for copy in copies:
+        wait_all(copy)
+
+
 def over_blocks(span, total, fetch, work):
     base, end = span
-    if base == 0:
-        for i in range(min(EARLY, total)):
-            begin_all(fetch(i))
-    loaded = 0 if base == 0 else base + EARLY
 
     def body(i, carry):
         @pl.when(i + EARLY < total)
         def _():
             begin_all(fetch(i + EARLY))
 
-        @pl.when(i >= loaded)
+        @pl.when(i >= base + EARLY)
         def _():
             wait_all(fetch(i))
 
@@ -64,22 +79,12 @@
         return carry
 
     lax.fori_loop(base, end, body, 0)
-    for i in range(max(end, loaded), min(end + EARLY, total)):
+    for i in range(max(end, base + EARLY), min(end + EARLY, total)):
         wait_all(fetch(i))
 
 
-def begin_all(copies):
-    for copy in copies:
-        copy.start()
-
-
-def wait_all(copies):
-    for copy in copies:
-        copy.wait()
-
-
-def partial_kernel(span, total, rows, first, deps, head, other, x, rg, wg, wu, wd, *rest):
-    b0, b1, b2, own, send, zero, table, wsem = rest[deps + (0 if first else 3) :]
+def partial_kernel(span, total, rows, deps, head, other, x, rg, wg, wu, wd, *rest):
+    b0, b1, b2, own, send, zero, table, wsem = rest[deps + 3 :]
     field = fill_table(rows, span[0], head, table)
     fetch = lambda i: weight_copies(field, i, (wg, wu, wd), (b0, b1, b2), wsem)
     zero[...] = jnp.zeros_like(zero)
@@ -117,27 +122,37 @@
 
 def cost(products, rows, depth, blocks):
     return pl.CostEstimate(
-        flops=int(2 * products * rows * depth * SUB * blocks / COST_SCALE),
-        bytes_accessed=int(6 * depth * SUB * blocks / COST_SCALE),
+        flops=int(2 * products * rows * depth * SUB * blocks * COST_FACTOR),
+        bytes_accessed=int(6 * depth * SUB * blocks * COST_FACTOR),
         transcendentals=0,
     )
+
+
+def preload(blocks, head, weights):
+    depth = weights[0].shape[1]
+    return pl.pallas_call(
+        functools.partial(preload_kernel, blocks[:EARLY]),
+        in_specs=[VMEM] + [HBM] * 3,
+        out_specs=[VMEM] * 3,
+        out_shape=slot_shapes(depth),
+        scratch_shapes=[pltpu.SMEM((EARLY * FIELDS,), jnp.int32), pltpu.SemaphoreType.DMA((SLOTS, 3))],
+        compiler_params=pltpu.CompilerParams(vmem_limit_bytes=VMEM_LIMIT),
+        cost_estimate=cost(0, 0, depth, EARLY),
+        name="preload",
+    )(near_core(head), *[in_hbm(w) for w in weights])
 
 
 def partial_products(span, units, blocks, head, x, rg, other, weights, slots, after):
     depth = weights[0].shape[1]
     rows = x.shape[0]
     shape = (units, 3, rows, SUB)
-    first = slots is None
     seen = blocks[span[0] : span[1] + EARLY]
     operands = [near_core(v) for v in (head, other, x, rg)] + [in_hbm(w) for w in weights] + list(after)
-    in_specs = [VMEM] * 4 + [HBM] * 3 + [ANY] * len(after)
-    aliases = {}
-    if not first:
-        aliases = {len(operands) + n: n for n in range(3)}
-        operands += [near_core(v) for v in slots]
-        in_specs += [VMEM] * 3
+    in_specs = [VMEM] * 4 + [HBM] * 3 + [ANY] * len(after) + [VMEM] * 3
+    aliases = {len(operands) + n: n for n in range(3)}
+    operands += [near_core(v) for v in slots]
     out = pl.pallas_call(
-        functools.partial(partial_kernel, span, len(blocks), seen, first, len(after)),
+        functools.partial(partial_kernel, span, len(blocks), seen, len(after)),
         in_specs=in_specs,
         out_specs=[VMEM] * 6,
         scratch_shapes=[pltpu.SMEM((len(seen) * FIELDS,), jnp.int32), pltpu.SemaphoreType.DMA((SLOTS, 3))],
@@ -194,7 +209,7 @@
     over_blocks(span, total, fetch, work)
     if closing:
         half = sums.shape[1] // 2
-        give[...] = sums[:, half:]
+        give[...] = sums[:, half:].astype(BF16)
         extra[...] = sums[:, :half]
     for i in range(max(end - 2, base), end):
         leave(i).wait()
@@ -219,7 +234,7 @@
     sums_shape = pltpu.VMEM((2, rows, depth), F32)
     out_shape = slot_shapes(depth) + [pltpu.HBM((experts, width, depth), BF16)]
     if closing:
-        out_shape += [pltpu.VMEM((2, rows // 2, depth), F32)] * 2
+        out_shape += [pltpu.VMEM((2, rows // 2, depth), kind) for kind in (BF16, F32)]
     else:
         out_shape += [sums_shape, pltpu.VMEM((2, 1, SUB), F32)]
     out = pl.pallas_call(
@@ -242,6 +257,30 @@
     return out[:3], (out[3], out[4]), out[5]
 
 
+def finish_kernel(own, first, second, zero, out):
+    gate, up, d_hidden = (
+        own[:, n] + first[:, n].astype(F32) + (second[:, n].astype(F32) + zero[1]) for n in range(3)
+    )
+    sigmoid = 1.0 / (1.0 + jnp.exp(-gate))
+    active = gate * sigmoid
+    out[:, 0] = (active * up).astype(BF16)
+    out[:, 1] = (d_hidden * up * sigmoid * (1.0 + gate * (1.0 - sigmoid))).astype(BF16)
+    out[:, 2] = (d_hidden * active).astype(BF16)
+
+
+def finished(*operands):
+    shape = operands[0].shape
+    return pl.pallas_call(
+        finish_kernel,
+        in_specs=[VMEM] * 4,
+        out_specs=VMEM,
+        out_shape=pltpu.VMEM(shape, BF16),
+        compiler_params=pltpu.CompilerParams(vmem_limit_bytes=VMEM_LIMIT),
+        cost_estimate=pl.CostEstimate(flops=0, bytes_accessed=1000, transcendentals=0),
+        name="finish",
+    )(*[near_core(v) for v in operands])
+
+
 def activations(gate, up, d_hidden):
     sigmoid = jax.nn.sigmoid(gate)
     active = gate * sigmoid
@@ -280,8 +319,8 @@
 STEPS = {"P": "partial", "M": "merge", "F": "finish", "Q": "post"}
 ORDER = (
     "P0", "P1", "P2", "M0", "P3", "M1", "F0", "P4", "M2", "F1", "P5", "Q0",
-    "M3", "F2", "Q1", "M4", "F3", "P6", "M5", "P7", "F4", "Q2", "M6", "F5",
-    "Q3", "M7", "F6", "Q4", "Q5", "F7", "Q6", "Q7",
+    "M3", "F2", "Q1", "M4", "F3", "P6", "M5", "P7", "F4", "Q2", "F5", "M6",
+    "Q3", "M7", "F6", "Q4", "F7", "Q5", "Q6", "Q7",
 )
 
 
@@ -335,8 +374,9 @@
     head = jnp.where(lane == 0, common, lane - (lane <= common).astype(jnp.int32))
     head = jnp.where(lane == 127, edge.astype(jnp.int32), head)[None]
 
-    own, sent, summed, mine, came = {}, {}, {}, {}, {}
-    state = slots = None
+    own, sent, first, mine, came = {}, {}, {}, {}, {}
+    state = None
+    slots = preload(blocks, head, weights)
     after = ()
 
     def send(v, pairs):
@@ -350,13 +390,12 @@
             sent[k] = send(packed, [(0, 1), (3, 2)]) if line else None
             after = (zero,)
         elif name == "merge" and line:
-            summed[k] = own[k] + (sent[k].astype(F32) + zero[0])
-            packed = summed[k].astype(BF16)
+            first[k] = sent[k]
+            packed = (own[k] + (sent[k].astype(F32) + zero[0])).astype(BF16)
             sent[k] = send(packed, [(1, 2), (2, 1)])
             after += (packed,)
         elif name == "finish" and line:
-            all_of = summed[k] + (sent[k].astype(F32) + zero[1])
-            mine[k] = activations(all_of[:, 0], all_of[:, 1], all_of[:, 2])
+            mine[k] = finished(own[k], first[k], sent[k], zero)
             came[k] = send(mine[k], [(1, 0), (2, 3)])
             after += (mine[k],)
         elif name == "finish":
@@ -369,7 +408,7 @@
             )
             after = (zero,)
     (d_down, give), keep = state, zero
-    both = keep + lax.ppermute(give, "tensor", swap)
+    both = keep + lax.ppermute(give, "tensor", swap).astype(F32)
     result = both[:, :local]
     for n in range(1, chips):
         piece = both[:, n * local : (n + 1) * local].astype(BF16)

time: 186 us -> 178 us (0.957)
  other arithmetic: 11.2 us -> 5.7 us
  starting transfers between devices: 60.9 us -> 56.1 us
  Pallas kernels: 76.7 us -> 81.3 us
  waiting for transfers between devices: 32.2 us -> 30.3 us
    pallas_call x0 -> x9, Pallas kernels: none -> 7.4 us  [the longest x1 3.94 us: preload(): pl.pallas_call(functools.partial(preload_kernel, blocks[:EARLY]), in_spec...]
    ppermute x24, starting transfers between devices: 52.3 us -> 46.9 us  [send(): return lax.ppermute(v, 'section', pairs)]
    ppermute x3, waiting for transfers between devices: 2.99 us -> 0.01 us  [on_device(): lax.ppermute(pair, 'tensor', [(i, (i - 2 * n) % parts) for i in range(par...]
    pallas_call x8, Pallas kernels: 35.4 us -> 32.6 us  [partial_products(): pl.pallas_call(functools.partial(partial_kernel, span, len(blocks), seen,...]
    add x8 -> x0, other arithmetic: 2.53 us -> none  [on_device(): all_of = summed[k] + (sent[k].astype(F32) + zero[1])]
    convert_element_type x16 -> x8, other arithmetic: 4.08 us -> 1.7 us  [on_device(): packed = (own[k] + (sent[k].astype(F32) + zero[0])).astype(BF16)]
  transfers between devices with their start and end apart: 32 -> 32, of which waited for: 9 -> 8; matrix products, arithmetic and copies ran while one was open for 6% -> 3% of each run, Pallas kernels for 37% -> 43%
where the time goes in v4:
time: 178 us
  Pallas kernels  81.3 us (46%)
  starting transfers between devices  56.1 us (32%)
  waiting for transfers between devices  30.3 us (17%)
  other arithmetic  5.7 us (3%)
  local copies, waits for them, and re-layouts  2.68 us (2%)
    ppermute x24, starting transfers between devices, send(): return lax.ppermute(v, 'section', pairs)  46.9 us
    pallas_call x8, Pallas kernels, post_products(): pl.pallas_call(functools.partial(post_kernel, span, len(blocks), seen, le...  41.3 us
    pallas_call x8, Pallas kernels, partial_products(): pl.pallas_call(functools.partial(partial_kernel, span, len(blocks), seen,...  32.6 us
    ppermute x24, waiting for transfers between devices, send(): return lax.ppermute(v, 'section', pairs)  20.4 us
    ppermute x3, waiting for transfers between devices, on_device(): lax.ppermute(piece, 'tensor', [(i, (i + 2 * n) % parts) for i in range(pa...  6.02 us
    ppermute x3, starting transfers between devices, on_device(): lax.ppermute(pair, 'tensor', [(i, (i - 2 * n) % parts) for i in range(par...  5.04 us
    ppermute x3, starting transfers between devices, on_device(): lax.ppermute(piece, 'tensor', [(i, (i + 2 * n) % parts) for i in range(pa...  3.98 us
    pallas_call x1, Pallas kernels, preload(): pl.pallas_call(functools.partial(preload_kernel, blocks[:EARLY]), in_spec...  3.94 us
  transfers between devices with their start and end apart: 32, of which 8 were waited for; matrix products, arithmetic and copies ran while one was open for 3% of the time, Pallas kernels for 43%

profile of v4, /device:TPU:0, one launch (start us, length us, event | category | flops | bytes accessed | tf_op | source)
XLA Modules:
  0.0 177.6 jit_solution(17931482067355530555)
XLA Ops:
  0.6 0.9 pad_maximum_fusion.2
  1.6 3.9 %collective-permute-start = (bf16[2,24,1536]{2,1,0:T(8,128)(2,1)S(1)}, bf16[2,24,1536]{2,1,0:T(8,128)(2,1)S(1)}, u32[]{:S(2)}, u32[]{:S(2)}) collective-permute-start(bf16[2,24,1536]{2,1,0:T(8,128)(2,1)S(1)} %get-tuple-element.210), channel_id=1, source_target_pairs={{0,6},{1,7},{2,0},{3,1},{4,2},{5,3},{6,4},{7,5},{8,14},{9,15},{10,... | collective-permute-start | bytes 442376 | tf_op jit(solution)/shard_map/ppermute | solution.py:340
  5.5 0.5 collective-permute-start.1
  6.0 0.6 collective-permute-start.2
  6.6 0.8 reshape.78
  7.6 0.8 reshape.80
  8.6 0.7 iota_reduce_fusion
  9.3 0.7 select_bitcast_fusion.1
  10.2 0.7 compare_select_fusion.1.head
  10.9 3.9 %preload.1 = (bf16[3,1536,512]{2,1,0:T(8,128)(2,1)S(1)}, bf16[3,1536,512]{2,1,0:T(8,128)(2,1)S(1)}, bf16[3,512,1536]{2,1,0:T(8,128)(2,1)S(1)}) custom-call(s32[1,128]{1,0:T(1,128)S(1)} %compare_select_fusion.1.head, bf16[4,1536,2048]{2,1,0:T(8,128)(2,1)} %wg.33, bf16[4,1536,2048]{2,1,0:T(8,128)(2,1)} %wu.33, bf16[4,2048,1536]{2,1,0:T(8,128)(2,1)} %wd.33), custom_call_target="tpu_custom_call" | custom-call | bytes 37748736 | tf_op jit(solution)/shard_map/preload/pallas_call | solution.py:133
  15.2 1.9 %collective-permute-done.3 = bf16[2,96,1536]{2,1,0:T(8,128)(2,1)S(1)} collective-permute-done((bf16[2,96,1536]{2,1,0:T(8,128)(2,1)S(1)}, bf16[2,96,1536]{2,1,0:T(8,128)(2,1)S(1)}, u32[]{:S(2)}, u32[]{:S(2)}) %collective-permute-start.3) | collective-permute-done | bytes 589856 | tf_op jit(solution)/shard_map/ppermute | solution.py:344
  17.5 2.6 %partial.8 = (bf16[3,1536,512]{2,1,0:T(8,128)(2,1)S(1)}, bf16[3,1536,512]{2,1,0:T(8,128)(2,1)S(1)}, bf16[3,512,1536]{2,1,0:T(8,128)(2,1)S(1)}, f32[1,3,192,512]{...) custom-call(s32[1,128]{1,0:T(1,128)S(1)} %compare_select_fusion.1.he, ...), custom_call_target="tpu_custom_call", output_to_operand_aliasing={{0}: (7, {}), {1}: (8, {}), {2}: (9, {})} | custom-call | flops 3623878656 | bytes 18874368 | tf_op jit(solution)/shard_map/partial/pallas_call | solution.py:154
  20.1 3.5 %collective-permute-start.5 = (bf16[1,3,192,512]{3,2,1,0:T(8,128)(2,1)S(1)}, bf16[1,3,192,512]{3,2,1,0:T(8,128)(2,1)S(1)}, u32[]{:S(2)}, u32[]{:S(2)}) collective-permute-start(bf16[1,3,192,512]{3,2,1,0:T(8,128)(2,1)S(1)} %get-tuple-element.116), channel_id=1, source_target_pairs={{0,8},{24,16},{1,9},{25,17},{2,10},{26,18},{3,11},{27,19},{4,12},{... | collective-permute-start | bytes 1769480 | tf_op jit(solution)/shard_map/ppermute | solution.py:383
  23.6 5.6 %partial.9 = (bf16[3,1536,512]{2,1,0:T(8,128)(2,1)S(1)}, bf16[3,1536,512]{2,1,0:T(8,128)(2,1)S(1)}, bf16[3,512,1536]{2,1,0:T(8,128)(2,1)S(1)}, f32[1,3,192,512]{...) custom-call(s32[1,128]{1,0:T(1,128)S(1)} %compare_select_fusion.1.he, ...), custom_call_target="tpu_custom_call", output_to_operand_aliasing={{0}: (8, {}), {1}: (9, {}), {2}: (10, {})} | custom-call | flops 10871635968 | bytes 56623104 | tf_op jit(solution)/shard_map/partial/pallas_call | solution.py:154
  29.2 5.6 %partial.10 = (bf16[3,1536,512]{2,1,0:T(8,128)(2,1)S(1)}, bf16[3,1536,512]{2,1,0:T(8,128)(2,1)S(1)}, bf16[3,512,1536]{2,1,0:T(8,128)(2,1)S(1)}, f32[1,3,192,512]...) custom-call(s32[1,128]{1,0:T(1,128)S(1)} %compare_select_fusion.1.he, ...), custom_call_target="tpu_custom_call", output_to_operand_aliasing={{0}: (8, {}), {1}: (9, {}), {2}: (10, {})} | custom-call | flops 10871635968 | bytes 56623104 | tf_op jit(solution)/shard_map/partial/pallas_call | solution.py:154
  34.8 1.3 collective-permute-start.4
  36.2 1.3 collective-permute-start.10
  37.7 0.7 collective-permute-start.7
  38.4 5.6 %partial.11 = (bf16[3,1536,512]{2,1,0:T(8,128)(2,1)S(1)}, bf16[3,1536,512]{2,1,0:T(8,128)(2,1)S(1)}, bf16[3,512,1536]{2,1,0:T(8,128)(2,1)S(1)}, f32[1,3,192,512]...) custom-call(s32[1,128]{1,0:T(1,128)S(1)} %compare_select_fusion.1.he, ...), custom_call_target="tpu_custom_call", output_to_operand_aliasing={{0}: (9, {}), {1}: (10, {}), {2}: (11, {})} | custom-call | flops 10871635968 | bytes 56623104 | tf_op jit(solution)/shard_map/partial/pallas_call | solution.py:154
  44.0 5.8 %collective-permute-done.4.first = bf16[1,3,192,512]{3,2,1,0:T(8,128)(2,1)S(1)} collective-permute-done((bf16[1,3,192,512]{3,2,1,0:T(8,128)(2,1)S(1)}, bf16[1,3,192,512]{3,2,1,0:T(8,128)(2,1)S(1)}, u32[]{:S(2)}, u32[]{:S(2)}) %collective-permute-start.4) | collective-permute-done | bytes 589856 | tf_op jit(solution)/shard_map/ppermute | solution.py:383
  50.0 0.7 collective-permute-start.6
  50.7 7.2 %collective-permute-start.11 = (bf16[1,3,192,512]{3,2,1,0:T(8,128)(2,1)S(1)}, bf16[1,3,192,512]{3,2,1,0:T(8,128)(2,1)S(1)}, u32[]{:S(2)}, u32[]{:S(2)}) collective-permute-start(bf16[1,3,192,512]{3,2,1,0:T(8,128)(2,1)S(1)} %get-tuple-element.136), channel_id=1, source_target_pairs={{0,8},{24,16},{1,9},{25,17},{2,10},{26,18},{3,11},{27,19},{4,12},{... | collective-permute-start | bytes 1769480 | tf_op jit(solution)/shard_map/ppermute | solution.py:383
  58.4 1.3 collective-permute-start.9
  59.7 5.6 %partial.12 = (bf16[3,1536,512]{2,1,0:T(8,128)(2,1)S(1)}, bf16[3,1536,512]{2,1,0:T(8,128)(2,1)S(1)}, bf16[3,512,1536]{2,1,0:T(8,128)(2,1)S(1)}, f32[1,3,192,512]...) custom-call(s32[1,128]{1,0:T(1,128)S(1)} %compare_select_fusion.1.he, ...), custom_call_target="tpu_custom_call", output_to_operand_aliasing={{0}: (10, {}), {1}: (11, {}), {2}: (12, {})} | custom-call | flops 10871635968 | bytes 56623104 | tf_op jit(solution)/shard_map/partial/pallas_call | solution.py:154
  65.5 0.7 collective-permute-start.12
  66.7 1.3 collective-permute-start.8
  68.0 6.3 %collective-permute-start.13 = (bf16[1,3,192,512]{3,2,1,0:T(8,128)(2,1)S(1)}, bf16[1,3,192,512]{3,2,1,0:T(8,128)(2,1)S(1)}, u32[]{:S(2)}, u32[]{:S(2)}) collective-permute-start(bf16[1,3,192,512]{3,2,1,0:T(8,128)(2,1)S(1)} %get-tuple-element.144), channel_id=1, source_target_pairs={{0,8},{24,16},{1,9},{25,17},{2,10},{26,18},{3,11},{27,19},{4,12},{... | collective-permute-start | bytes 1769480 | tf_op jit(solution)/shard_map/ppermute | solution.py:383
  74.3 2.6 %partial.13 = (bf16[3,1536,512]{2,1,0:T(8,128)(2,1)S(1)}, bf16[3,1536,512]{2,1,0:T(8,128)(2,1)S(1)}, bf16[3,512,1536]{2,1,0:T(8,128)(2,1)S(1)}, f32[1,3,192,512]...) custom-call(s32[1,128]{1,0:T(1,128)S(1)} %compare_select_fusion.1.he, ...), custom_call_target="tpu_custom_call", output_to_operand_aliasing={{0}: (10, {}), {1}: (11, {}), {2}: (12, {})} | custom-call | flops 3623878656 | bytes 18874368 | tf_op jit(solution)/shard_map/partial/pallas_call | solution.py:154
  76.9 1.3 collective-permute-start.15
  78.2 3.2 %post.8 = (bf16[3,1536,512]{2,1,0:T(8,128)(2,1)S(1)}, bf16[3,1536,512]{2,1,0:T(8,128)(2,1)S(1)}, bf16[3,512,1536]{2,1,0:T(8,128)(2,1)S(1)}, bf16[4,2048,1536]{2,...) custom-call(s32[1,128]{1,0:T(1,128)S(1)} %compare_select_fusion.1.he, ...), custom_call_target="tpu_custom_call", output_to_operand_aliasing={{0}: (10, {}), {1}: (11, {}), {2}: (12, {})} | custom-call | flops 4831838208 | bytes 18874368 | tf_op jit(solution)/shard_map/post/pallas_call | solution.py:240
  81.6 0.7 collective-permute-start.14
  82.4 0.4 finish.10.rest_2_.mine
  82.8 1.5 collective-permute-start.18
  84.3 3.6 %collective-permute-done.8.came = bf16[1,3,192,512]{3,2,1,0:T(8,128)(2,1)S(1)} collective-permute-done((bf16[1,3,192,512]{3,2,1,0:T(8,128)(2,1)S(1)}, bf16[1,3,192,512]{3,2,1,0:T(8,128)(2,1)S(1)}, u32[]{:S(2)}, u32[]{:S(2)}) %collective-permute-start.8) | collective-permute-done | bytes 589856 | tf_op jit(solution)/shard_map/ppermute | solution.py:383
  87.9 7.6 %post.9 = (bf16[3,1536,512]{2,1,0:T(8,128)(2,1)S(1)}, bf16[3,1536,512]{2,1,0:T(8,128)(2,1)S(1)}, bf16[3,512,1536]{2,1,0:T(8,128)(2,1)S(1)}, bf16[4,2048,1536]{2,...) custom-call(s32[1,128]{1,0:T(1,128)S(1)} %compare_select_fusion.1.he, ...), custom_call_target="tpu_custom_call", output_to_operand_aliasing={{0}: (12, {}), {1}: (13, {}), {2}: (14, {}), {3}: (16, {}),... | custom-call | flops 14495514624 | bytes 56623104 | tf_op jit(solution)/shard_map/post/pallas_call | solution.py:240
  95.7 0.7 collective-permute-start.19
  96.9 1.3 collective-permute-start.17
  98.2 2.6 %partial.14 = (bf16[3,1536,512]{2,1,0:T(8,128)(2,1)S(1)}, bf16[3,1536,512]{2,1,0:T(8,128)(2,1)S(1)}, bf16[3,512,1536]{2,1,0:T(8,128)(2,1)S(1)}, f32[1,3,192,512]...) custom-call(s32[1,128]{1,0:T(1,128)S(1)} %compare_select_fusion.1.he, ...), custom_call_target="tpu_custom_call", output_to_operand_aliasing={{0}: (10, {}), {1}: (11, {}), {2}: (12, {})} | custom-call | flops 3623878656 | bytes 18874368 | tf_op jit(solution)/shard_map/partial/pallas_call | solution.py:154
  100.8 4.6 %collective-permute-start.21 = (bf16[1,3,192,512]{3,2,1,0:T(8,128)(2,1)S(1)}, bf16[1,3,192,512]{3,2,1,0:T(8,128)(2,1)S(1)}, u32[]{:S(2)}, u32[]{:S(2)}) collective-permute-start(bf16[1,3,192,512]{3,2,1,0:T(8,128)(2,1)S(1)} %get-tuple-element.164), channel_id=1, source_target_pairs={{0,8},{24,16},{1,9},{25,17},{2,10},{26,18},{3,11},{27,19},{4,12},{... | collective-permute-start | bytes 1769480 | tf_op jit(solution)/shard_map/ppermute | solution.py:383
  105.6 0.7 collective-permute-start.20
  106.3 2.6 %partial.15 = (bf16[3,1536,512]{2,1,0:T(8,128)(2,1)S(1)}, bf16[3,1536,512]{2,1,0:T(8,128)(2,1)S(1)}, bf16[3,512,1536]{2,1,0:T(8,128)(2,1)S(1)}, f32[1,3,192,512]...) custom-call(s32[1,128]{1,0:T(1,128)S(1)} %compare_select_fusion.1.he, ...), custom_call_target="tpu_custom_call", output_to_operand_aliasing={{0}: (9, {}), {1}: (10, {}), {2}: (11, {})} | custom-call | flops 3623878656 | bytes 18874368 | tf_op jit(solution)/shard_map/partial/pallas_call | solution.py:154
  108.9 0.4 finish.12.rest_1_.mine
  109.4 1.3 collective-permute-start.23
  110.7 7.6 %post.10 = (bf16[3,1536,512]{2,1,0:T(8,128)(2,1)S(1)}, bf16[3,1536,512]{2,1,0:T(8,128)(2,1)S(1)}, bf16[3,512,1536]{2,1,0:T(8,128)(2,1)S(1)}, bf16[4,2048,1536]{2...) custom-call(s32[1,128]{1,0:T(1,128)S(1)} %compare_select_fusion.1.he, ...), custom_call_target="tpu_custom_call", output_to_operand_aliasing={{0}: (11, {}), {1}: (12, {}), {2}: (13, {}), {3}: (15, {}),... | custom-call | flops 14495514624 | bytes 56623104 | tf_op jit(solution)/shard_map/post/pallas_call | solution.py:240
  118.3 4.9 %collective-permute-start.16 = (bf16[1,3,192,512]{3,2,1,0:T(8,128)(2,1)S(1)}, bf16[1,3,192,512]{3,2,1,0:T(8,128)(2,1)S(1)}, u32[]{:S(2)}, u32[]{:S(2)}) collective-permute-start(bf16[1,3,192,512]{3,2,1,0:T(8,128)(2,1)S(1)} %get-tuple-element.155), channel_id=1, source_target_pairs={{0,8},{24,16},{1,9},{25,17},{2,10},{26,18},{3,11},{27,19},{4,12},{... | collective-permute-start | bytes 1769480 | tf_op jit(solution)/shard_map/ppermute | solution.py:383
  123.4 0.7 collective-permute-start.24
  124.6 1.3 collective-permute-start.27
  125.9 7.6 %post.11 = (bf16[3,1536,512]{2,1,0:T(8,128)(2,1)S(1)}, bf16[3,1536,512]{2,1,0:T(8,128)(2,1)S(1)}, bf16[3,512,1536]{2,1,0:T(8,128)(2,1)S(1)}, bf16[4,2048,1536]{2...) custom-call(s32[1,128]{1,0:T(1,128)S(1)} %compare_select_fusion.1.he, ...), custom_call_target="tpu_custom_call", output_to_operand_aliasing={{0}: (12, {}), {1}: (13, {}), {2}: (14, {}), {3}: (16, {}),... | custom-call | flops 14495514624 | bytes 56623104 | tf_op jit(solution)/shard_map/post/pallas_call | solution.py:240
  133.8 0.7 collective-permute-start.22
  134.9 1.3 collective-permute-start.26
  136.3 7.6 %post.12 = (bf16[3,1536,512]{2,1,0:T(8,128)(2,1)S(1)}, bf16[3,1536,512]{2,1,0:T(8,128)(2,1)S(1)}, bf16[3,512,1536]{2,1,0:T(8,128)(2,1)S(1)}, bf16[4,2048,1536]{2...) custom-call(s32[1,128]{1,0:T(1,128)S(1)} %compare_select_fusion.1.he, ...), custom_call_target="tpu_custom_call", output_to_operand_aliasing={{0}: (12, {}), {1}: (13, {}), {2}: (14, {}), {3}: (16, {}),... | custom-call | flops 14495514624 | bytes 56623104 | tf_op jit(solution)/shard_map/post/pallas_call | solution.py:240
  144.3 1.5 collective-permute-start.25
  145.8 3.1 %post.13 = (bf16[3,1536,512]{2,1,0:T(8,128)(2,1)S(1)}, bf16[3,1536,512]{2,1,0:T(8,128)(2,1)S(1)}, bf16[3,512,1536]{2,1,0:T(8,128)(2,1)S(1)}, bf16[4,2048,1536]{2...) custom-call(s32[1,128]{1,0:T(1,128)S(1)} %compare_select_fusion.1.he, ...), custom_call_target="tpu_custom_call", output_to_operand_aliasing={{0}: (11, {}), {1}: (12, {}), {2}: (13, {}), {3}: (15, {}),... | custom-call | flops 4831838208 | bytes 18874368 | tf_op jit(solution)/shard_map/post/pallas_call | solution.py:240
  148.9 4.3 %collective-permute-done.26.came = bf16[1,3,192,512]{3,2,1,0:T(8,128)(2,1)S(1)} collective-permute-done((bf16[1,3,192,512]{3,2,1,0:T(8,128)(2,1)S(1)}, bf16[1,3,192,512]{3,2,1,0:T(8,128)(2,1)S(1)}, u32[]{:S(2)}, u32[]{:S(2)}) %collective-permute-start.26) | collective-permute-done | bytes 589856 | tf_op jit(solution)/shard_map/ppermute | solution.py:383
  153.2 2.3 %post.14 = (bf16[3,1536,512]{2,1,0:T(8,128)(2,1)S(1)}, bf16[3,1536,512]{2,1,0:T(8,128)(2,1)S(1)}, bf16[3,512,1536]{2,1,0:T(8,128)(2,1)S(1)}, bf16[4,2048,1536]{2...) custom-call(s32[1,128]{1,0:T(1,128)S(1)} %compare_select_fusion.1.he, ...), custom_call_target="tpu_custom_call", output_to_operand_aliasing={{0}: (10, {}), {1}: (11, {}), {2}: (12, {}), {3}: (14, {}),... | custom-call | flops 4831838208 | bytes 18874368 | tf_op jit(solution)/shard_map/post/pallas_call | solution.py:240
  155.6 6.6 %collective-permute-done.25.came = bf16[1,3,192,512]{3,2,1,0:T(8,128)(2,1)S(1)} collective-permute-done((bf16[1,3,192,512]{3,2,1,0:T(8,128)(2,1)S(1)}, bf16[1,3,192,512]{3,2,1,0:T(8,128)(2,1)S(1)}, u32[]{:S(2)}, u32[]{:S(2)}) %collective-permute-start.25) | collective-permute-done | bytes 589856 | tf_op jit(solution)/shard_map/ppermute | solution.py:383
  162.2 2.3 %post.15 = (bf16[3,1536,512]{2,1,0:T(8,128)(2,1)S(1)}, bf16[3,1536,512]{2,1,0:T(8,128)(2,1)S(1)}, bf16[3,512,1536]{2,1,0:T(8,128)(2,1)S(1)}, bf16[4,2048,1536]{2...) custom-call(s32[1,128]{1,0:T(1,128)S(1)} %compare_select_fusion.1.he, ...), custom_call_target="tpu_custom_call", output_to_operand_aliasing={{0}: (10, {}), {1}: (11, {}), {2}: (12, {}), {3}: (14, {})} | custom-call | flops 4831838208 | bytes 18874368 | tf_op jit(solution)/shard_map/post/pallas_call | solution.py:240
  164.6 2.0 %collective-permute-done.28 = bf16[2,96,1536]{2,1,0:T(8,128)(2,1)S(1)} collective-permute-done((bf16[2,96,1536]{2,1,0:T(8,128)(2,1)S(1)}, bf16[2,96,1536]{2,1,0:T(8,128)(2,1)S(1)}, u32[]{:S(2)}, u32[]{:S(2)}) %collective-permute-start.28) | collective-permute-done | bytes 589856 | tf_op jit(solution)/shard_map/ppermute | solution.py:411
  166.8 2.4 %collective-permute-start.29 = (bf16[2,24,1536]{2,1,0:T(8,128)(2,1)S(1)}, bf16[2,24,1536]{2,1,0:T(8,128)(2,1)S(1)}, u32[]{:S(2)}, u32[]{:S(2)}) collective-permute-start(bf16[2,24,1536]{2,1,0:T(8,128)(2,1)S(1)} %get-tuple-element.203), channel_id=1, source_target_pairs={{0,2},{1,3},{2,4},{3,5},{4,6},{5,7},{6,0},{7,1},{8,10},{9,11},{10,... | collective-permute-start | bytes 442376 | tf_op jit(solution)/shard_map/ppermute | solution.py:415
  169.3 0.5 collective-permute-start.30
  169.8 1.0 collective-permute-start.31
  170.8 3.6 %collective-permute-done.29 = bf16[2,24,1536]{2,1,0:T(8,128)(2,1)S(1)} collective-permute-done((bf16[2,24,1536]{2,1,0:T(8,128)(2,1)S(1)}, bf16[2,24,1536]{2,1,0:T(8,128)(2,1)S(1)}, u32[]{:S(2)}, u32[]{:S(2)}) %collective-permute-start.29) | collective-permute-done | bytes 147488 | tf_op jit(solution)/shard_map/ppermute | solution.py:415
  174.3 2.5 %collective-permute-done.30 = bf16[2,24,1536]{2,1,0:T(8,128)(2,1)S(1)} collective-permute-done((bf16[2,24,1536]{2,1,0:T(8,128)(2,1)S(1)}, bf16[2,24,1536]{2,1,0:T(8,128)(2,1)S(1)}, u32[]{:S(2)}, u32[]{:S(2)}) %collective-permute-start.30) | collective-permute-done | bytes 147488 | tf_op jit(solution)/shard_map/ppermute | solution.py:415
  176.9 0.7 slice_bitcast_fusion.2
  (79 shorter events, 6.0 us)
Async XLA Ops:
  0.6 8.0 %copy-start = (s32[4]{0:T(128)S(1)}, s32[4]{0:T(128)}, u32[]{:S(2)}) copy-start(s32[4]{0:T(128)} %param.11) | copy-start | bytes 52
  1.6 13.4 %collective-permute-start = (bf16[2,24,1536]{2,1,0:T(8,128)(2,1)S(1)}, bf16[2,24,1536]{2,1,0:T(8,128)(2,1)S(1)}, u32[]{:S(2)}, u32[]{:S(2)}) collective-permute-start(bf16[2,24,1536]{2,1,0:T(8,128)(2,1)S(1)} %get-tuple-element.210), channel_id=1, source_target_pairs={{0,6},{1,7},{2,0},{3,1},{4,2},{5,3},{6,4},{7,5},{8,14},{9,15},{10,... | collective-permute-start | bytes 442376 | tf_op jit(solution)/shard_map/ppermute | solution.py:340
  5.5 9.5 %collective-permute-start.1 = (bf16[2,24,1536]{2,1,0:T(8,128)(2,1)S(1)}, bf16[2,24,1536]{2,1,0:T(8,128)(2,1)S(1)}, u32[]{:S(2)}, u32[]{:S(2)}) collective-permute-start(bf16[2,24,1536]{2,1,0:T(8,128)(2,1)S(1)} %get-tuple-element.210), channel_id=1, source_target_pairs={{0,4},{1,5},{2,6},{3,7},{4,0},{5,1},{6,2},{7,3},{8,12},{9,13},{10,... | collective-permute-start | bytes 442376 | tf_op jit(solution)/shard_map/ppermute | solution.py:340
  6.0 9.0 %collective-permute-start.2 = (bf16[2,24,1536]{2,1,0:T(8,128)(2,1)S(1)}, bf16[2,24,1536]{2,1,0:T(8,128)(2,1)S(1)}, u32[]{:S(2)}, u32[]{:S(2)}) collective-permute-start(bf16[2,24,1536]{2,1,0:T(8,128)(2,1)S(1)} %get-tuple-element.210), channel_id=1, source_target_pairs={{0,2},{1,3},{2,4},{3,5},{4,6},{5,7},{6,0},{7,1},{8,10},{9,11},{10,... | collective-permute-start | bytes 442376 | tf_op jit(solution)/shard_map/ppermute | solution.py:340
  10.9 4.1 %copy-start.2 = (bf16[24,1536]{1,0:T(8,128)(2,1)S(1)}, bf16[24,1536]{1,0:T(8,128)(2,1)}, u32[]{:S(2)}) copy-start(bf16[24,1536]{1,0:T(8,128)(2,1)} %param.15) | copy-start | bytes 221188
  10.9 4.1 %copy-start.3 = (bf16[24,1536]{1,0:T(8,128)(2,1)S(1)}, bf16[24,1536]{1,0:T(8,128)(2,1)}, u32[]{:S(2)}) copy-start(bf16[24,1536]{1,0:T(8,128)(2,1)} %param.8) | copy-start | bytes 221188
  15.1 2.1 %collective-permute-start.3 = (bf16[2,96,1536]{2,1,0:T(8,128)(2,1)S(1)}, bf16[2,96,1536]{2,1,0:T(8,128)(2,1)S(1)}, u32[]{:S(2)}, u32[]{:S(2)}) collective-permute-start(bf16[2,96,1536]{2,1,0:T(8,128)(2,1)S(1)} %pad_maximum_fusion), channel_id=1, source_target_pairs={{0,1},{1,0},{2,3},{3,2},{4,5},{5,4},{6,7},{7,6},{8,9},{9,8},{10,11... | collective-permute-start | bytes 1769480 | tf_op jit(solution)/shard_map/ppermute | solution.py:344
  20.1 17.4 %collective-permute-start.5 = (bf16[1,3,192,512]{3,2,1,0:T(8,128)(2,1)S(1)}, bf16[1,3,192,512]{3,2,1,0:T(8,128)(2,1)S(1)}, u32[]{:S(2)}, u32[]{:S(2)}) collective-permute-start(bf16[1,3,192,512]{3,2,1,0:T(8,128)(2,1)S(1)} %get-tuple-element.116), channel_id=1, source_target_pairs={{0,8},{24,16},{1,9},{25,17},{2,10},{26,18},{3,11},{27,19},{4,12},{... | collective-permute-start | bytes 1769480 | tf_op jit(solution)/shard_map/ppermute | solution.py:383
  34.8 15.0 %collective-permute-start.4 = (bf16[1,3,192,512]{3,2,1,0:T(8,128)(2,1)S(1)}, bf16[1,3,192,512]{3,2,1,0:T(8,128)(2,1)S(1)}, u32[]{:S(2)}, u32[]{:S(2)}) collective-permute-start(bf16[1,3,192,512]{3,2,1,0:T(8,128)(2,1)S(1)} %get-tuple-element.109), channel_id=1, source_target_pairs={{0,8},{24,16},{1,9},{25,17},{2,10},{26,18},{3,11},{27,19},{4,12},{... | collective-permute-start | bytes 1769480 | tf_op jit(solution)/shard_map/ppermute | solution.py:383
  36.2 29.1 %collective-permute-start.10 = (bf16[1,3,192,512]{3,2,1,0:T(8,128)(2,1)S(1)}, bf16[1,3,192,512]{3,2,1,0:T(8,128)(2,1)S(1)}, u32[]{:S(2)}, u32[]{:S(2)}) collective-permute-start(bf16[1,3,192,512]{3,2,1,0:T(8,128)(2,1)S(1)} %get-tuple-element.126), channel_id=1, source_target_pairs={{0,8},{24,16},{1,9},{25,17},{2,10},{26,18},{3,11},{27,19},{4,12},{... | collective-permute-start | bytes 1769480 | tf_op jit(solution)/shard_map/ppermute | solution.py:383
  37.7 20.2 %collective-permute-start.7 = (bf16[1,3,192,512]{3,2,1,0:T(8,128)(2,1)S(1)}, bf16[1,3,192,512]{3,2,1,0:T(8,128)(2,1)S(1)}, u32[]{:S(2)}, u32[]{:S(2)}) collective-permute-start(bf16[1,3,192,512]{3,2,1,0:T(8,128)(2,1)S(1)} %add_convert_fusion.7.rest_1_), channel_id=1, source_target_pairs={{8,16},{16,8},{9,17},{17,9},{10,18},{18,10},{11,19},{19,11},{12,20... | collective-permute-start | bytes 1769480 | tf_op jit(solution)/shard_map/ppermute | solution.py:383
  50.0 16.2 %collective-permute-start.6 = (bf16[1,3,192,512]{3,2,1,0:T(8,128)(2,1)S(1)}, bf16[1,3,192,512]{3,2,1,0:T(8,128)(2,1)S(1)}, u32[]{:S(2)}, u32[]{:S(2)}) collective-permute-start(bf16[1,3,192,512]{3,2,1,0:T(8,128)(2,1)S(1)} %add_convert_fusion.6.rest_1_), channel_id=1, source_target_pairs={{8,16},{16,8},{9,17},{17,9},{10,18},{18,10},{11,19},{19,11},{12,20... | collective-permute-start | bytes 1769480 | tf_op jit(solution)/shard_map/ppermute | solution.py:383
  50.7 30.7 %collective-permute-start.11 = (bf16[1,3,192,512]{3,2,1,0:T(8,128)(2,1)S(1)}, bf16[1,3,192,512]{3,2,1,0:T(8,128)(2,1)S(1)}, u32[]{:S(2)}, u32[]{:S(2)}) collective-permute-start(bf16[1,3,192,512]{3,2,1,0:T(8,128)(2,1)S(1)} %get-tuple-element.136), channel_id=1, source_target_pairs={{0,8},{24,16},{1,9},{25,17},{2,10},{26,18},{3,11},{27,19},{4,12},{... | collective-permute-start | bytes 1769480 | tf_op jit(solution)/shard_map/ppermute | solution.py:383
  58.4 18.5 %collective-permute-start.9 = (bf16[1,3,192,512]{3,2,1,0:T(8,128)(2,1)S(1)}, bf16[1,3,192,512]{3,2,1,0:T(8,128)(2,1)S(1)}, u32[]{:S(2)}, u32[]{:S(2)}) collective-permute-start(bf16[1,3,192,512]{3,2,1,0:T(8,128)(2,1)S(1)} %finish.8.rest_2_.mine), channel_id=1, source_target_pairs={{8,0},{16,24},{9,1},{17,25},{10,2},{18,26},{11,3},{19,27},{12,4},{... | collective-permute-start | bytes 1769480 | tf_op jit(solution)/shard_map/ppermute | solution.py:383
  65.5 16.8 %collective-permute-start.12 = (bf16[1,3,192,512]{3,2,1,0:T(8,128)(2,1)S(1)}, bf16[1,3,192,512]{3,2,1,0:T(8,128)(2,1)S(1)}, u32[]{:S(2)}, u32[]{:S(2)}) collective-permute-start(bf16[1,3,192,512]{3,2,1,0:T(8,128)(2,1)S(1)} %add_convert_fusion.5.rest_1_), channel_id=1, source_target_pairs={{8,16},{16,8},{9,17},{17,9},{10,18},{18,10},{11,19},{19,11},{12,20... | collective-permute-start | bytes 1769480 | tf_op jit(solution)/shard_map/ppermute | solution.py:383
  66.7 21.3 %collective-permute-start.8 = (bf16[1,3,192,512]{3,2,1,0:T(8,128)(2,1)S(1)}, bf16[1,3,192,512]{3,2,1,0:T(8,128)(2,1)S(1)}, u32[]{:S(2)}, u32[]{:S(2)}) collective-permute-start(bf16[1,3,192,512]{3,2,1,0:T(8,128)(2,1)S(1)} %finish.9.rest_2_.mine), channel_id=1, source_target_pairs={{8,0},{16,24},{9,1},{17,25},{10,2},{18,26},{11,3},{19,27},{12,4},{... | collective-permute-start | bytes 1769480 | tf_op jit(solution)/shard_map/ppermute | solution.py:383
  68.0 27.6 %collective-permute-start.13 = (bf16[1,3,192,512]{3,2,1,0:T(8,128)(2,1)S(1)}, bf16[1,3,192,512]{3,2,1,0:T(8,128)(2,1)S(1)}, u32[]{:S(2)}, u32[]{:S(2)}) collective-permute-start(bf16[1,3,192,512]{3,2,1,0:T(8,128)(2,1)S(1)} %get-tuple-element.144), channel_id=1, source_target_pairs={{0,8},{24,16},{1,9},{25,17},{2,10},{26,18},{3,11},{27,19},{4,12},{... | collective-permute-start | bytes 1769480 | tf_op jit(solution)/shard_map/ppermute | solution.py:383
  76.9 28.5 %collective-permute-start.15 = (bf16[1,3,192,512]{3,2,1,0:T(8,128)(2,1)S(1)}, bf16[1,3,192,512]{3,2,1,0:T(8,128)(2,1)S(1)}, u32[]{:S(2)}, u32[]{:S(2)}) collective-permute-start(bf16[1,3,192,512]{3,2,1,0:T(8,128)(2,1)S(1)} %get-tuple-element.150), channel_id=1, source_target_pairs={{0,8},{24,16},{1,9},{25,17},{2,10},{26,18},{3,11},{27,19},{4,12},{... | collective-permute-start | bytes 1769480 | tf_op jit(solution)/shard_map/ppermute | solution.py:383
  81.6 14.8 %collective-permute-start.14 = (bf16[1,3,192,512]{3,2,1,0:T(8,128)(2,1)S(1)}, bf16[1,3,192,512]{3,2,1,0:T(8,128)(2,1)S(1)}, u32[]{:S(2)}, u32[]{:S(2)}) collective-permute-start(bf16[1,3,192,512]{3,2,1,0:T(8,128)(2,1)S(1)} %add_convert_fusion.4.rest_1_), channel_id=1, source_target_pairs={{8,16},{16,8},{9,17},{17,9},{10,18},{18,10},{11,19},{19,11},{12,20... | collective-permute-start | bytes 1769480 | tf_op jit(solution)/shard_map/ppermute | solution.py:383
  82.8 27.9 %collective-permute-start.18 = (bf16[1,3,192,512]{3,2,1,0:T(8,128)(2,1)S(1)}, bf16[1,3,192,512]{3,2,1,0:T(8,128)(2,1)S(1)}, u32[]{:S(2)}, u32[]{:S(2)}) collective-permute-start(bf16[1,3,192,512]{3,2,1,0:T(8,128)(2,1)S(1)} %finish.10.rest_2_.mine), channel_id=1, source_target_pairs={{8,0},{16,24},{9,1},{17,25},{10,2},{18,26},{11,3},{19,27},{12,4},{... | collective-permute-start | bytes 1769480 | tf_op jit(solution)/shard_map/ppermute | solution.py:383
  95.7 13.2 %collective-permute-start.19 = (bf16[1,3,192,512]{3,2,1,0:T(8,128)(2,1)S(1)}, bf16[1,3,192,512]{3,2,1,0:T(8,128)(2,1)S(1)}, u32[]{:S(2)}, u32[]{:S(2)}) collective-permute-start(bf16[1,3,192,512]{3,2,1,0:T(8,128)(2,1)S(1)} %add_convert_fusion.3.rest_1_), channel_id=1, source_target_pairs={{8,16},{16,8},{9,17},{17,9},{10,18},{18,10},{11,19},{19,11},{12,20... | collective-permute-start | bytes 1769480 | tf_op jit(solution)/shard_map/ppermute | solution.py:383
  96.9 29.0 %collective-permute-start.17 = (bf16[1,3,192,512]{3,2,1,0:T(8,128)(2,1)S(1)}, bf16[1,3,192,512]{3,2,1,0:T(8,128)(2,1)S(1)}, u32[]{:S(2)}, u32[]{:S(2)}) collective-permute-start(bf16[1,3,192,512]{3,2,1,0:T(8,128)(2,1)S(1)} %finish.11.rest_2_.mine), channel_id=1, source_target_pairs={{8,0},{16,24},{9,1},{17,25},{10,2},{18,26},{11,3},{19,27},{12,4},{... | collective-permute-start | bytes 1769480 | tf_op jit(solution)/shard_map/ppermute | solution.py:383
  100.8 22.4 %collective-permute-start.21 = (bf16[1,3,192,512]{3,2,1,0:T(8,128)(2,1)S(1)}, bf16[1,3,192,512]{3,2,1,0:T(8,128)(2,1)S(1)}, u32[]{:S(2)}, u32[]{:S(2)}) collective-permute-start(bf16[1,3,192,512]{3,2,1,0:T(8,128)(2,1)S(1)} %get-tuple-element.164), channel_id=1, source_target_pairs={{0,8},{24,16},{1,9},{25,17},{2,10},{26,18},{3,11},{27,19},{4,12},{... | collective-permute-start | bytes 1769480 | tf_op jit(solution)/shard_map/ppermute | solution.py:383
  105.6 18.5 %collective-permute-start.20 = (bf16[1,3,192,512]{3,2,1,0:T(8,128)(2,1)S(1)}, bf16[1,3,192,512]{3,2,1,0:T(8,128)(2,1)S(1)}, u32[]{:S(2)}, u32[]{:S(2)}) collective-permute-start(bf16[1,3,192,512]{3,2,1,0:T(8,128)(2,1)S(1)} %add_convert_fusion.2.rest_1_), channel_id=1, source_target_pairs={{8,16},{16,8},{9,17},{17,9},{10,18},{18,10},{11,19},{19,11},{12,20... | collective-permute-start | bytes 1769480 | tf_op jit(solution)/shard_map/ppermute | solution.py:383
  109.4 26.9 %collective-permute-start.23 = (bf16[1,3,192,512]{3,2,1,0:T(8,128)(2,1)S(1)}, bf16[1,3,192,512]{3,2,1,0:T(8,128)(2,1)S(1)}, u32[]{:S(2)}, u32[]{:S(2)}) collective-permute-start(bf16[1,3,192,512]{3,2,1,0:T(8,128)(2,1)S(1)} %finish.12.rest_1_.mine), channel_id=1, source_target_pairs={{8,0},{16,24},{9,1},{17,25},{10,2},{18,26},{11,3},{19,27},{12,4},{... | collective-permute-start | bytes 1769480 | tf_op jit(solution)/shard_map/ppermute | solution.py:383
  118.3 15.3 %collective-permute-start.16 = (bf16[1,3,192,512]{3,2,1,0:T(8,128)(2,1)S(1)}, bf16[1,3,192,512]{3,2,1,0:T(8,128)(2,1)S(1)}, u32[]{:S(2)}, u32[]{:S(2)}) collective-permute-start(bf16[1,3,192,512]{3,2,1,0:T(8,128)(2,1)S(1)} %get-tuple-element.155), channel_id=1, source_target_pairs={{0,8},{24,16},{1,9},{25,17},{2,10},{26,18},{3,11},{27,19},{4,12},{... | collective-permute-start | bytes 1769480 | tf_op jit(solution)/shard_map/ppermute | solution.py:383
  123.4 11.1 %collective-permute-start.24 = (bf16[1,3,192,512]{3,2,1,0:T(8,128)(2,1)S(1)}, bf16[1,3,192,512]{3,2,1,0:T(8,128)(2,1)S(1)}, u32[]{:S(2)}, u32[]{:S(2)}) collective-permute-start(bf16[1,3,192,512]{3,2,1,0:T(8,128)(2,1)S(1)} %add_convert_fusion.1.rest_2_), channel_id=1, source_target_pairs={{8,16},{16,8},{9,17},{17,9},{10,18},{18,10},{11,19},{19,11},{12,20... | collective-permute-start | bytes 1769480 | tf_op jit(solution)/shard_map/ppermute | solution.py:383
  124.6 21.2 %collective-permute-start.27 = (bf16[1,3,192,512]{3,2,1,0:T(8,128)(2,1)S(1)}, bf16[1,3,192,512]{3,2,1,0:T(8,128)(2,1)S(1)}, u32[]{:S(2)}, u32[]{:S(2)}) collective-permute-start(bf16[1,3,192,512]{3,2,1,0:T(8,128)(2,1)S(1)} %finish.13.rest_1_.mine), channel_id=1, source_target_pairs={{8,0},{16,24},{9,1},{17,25},{10,2},{18,26},{11,3},{19,27},{12,4},{... | collective-permute-start | bytes 1769480 | tf_op jit(solution)/shard_map/ppermute | solution.py:383
  133.8 10.1 %collective-permute-start.22 = (bf16[1,3,192,512]{3,2,1,0:T(8,128)(2,1)S(1)}, bf16[1,3,192,512]{3,2,1,0:T(8,128)(2,1)S(1)}, u32[]{:S(2)}, u32[]{:S(2)}) collective-permute-start(bf16[1,3,192,512]{3,2,1,0:T(8,128)(2,1)S(1)} %add_convert_fusion.rest_1_), channel_id=1, source_target_pairs={{8,16},{16,8},{9,17},{17,9},{10,18},{18,10},{11,19},{19,11},{12,20... | collective-permute-start | bytes 1769480 | tf_op jit(solution)/shard_map/ppermute | solution.py:383
  134.9 18.3 %collective-permute-start.26 = (bf16[1,3,192,512]{3,2,1,0:T(8,128)(2,1)S(1)}, bf16[1,3,192,512]{3,2,1,0:T(8,128)(2,1)S(1)}, u32[]{:S(2)}, u32[]{:S(2)}) collective-permute-start(bf16[1,3,192,512]{3,2,1,0:T(8,128)(2,1)S(1)} %finish.14.rest_2_.mine), channel_id=1, source_target_pairs={{8,0},{16,24},{9,1},{17,25},{10,2},{18,26},{11,3},{19,27},{12,4},{... | collective-permute-start | bytes 1769480 | tf_op jit(solution)/shard_map/ppermute | solution.py:383
  144.3 17.9 %collective-permute-start.25 = (bf16[1,3,192,512]{3,2,1,0:T(8,128)(2,1)S(1)}, bf16[1,3,192,512]{3,2,1,0:T(8,128)(2,1)S(1)}, u32[]{:S(2)}, u32[]{:S(2)}) collective-permute-start(bf16[1,3,192,512]{3,2,1,0:T(8,128)(2,1)S(1)} %finish.15.rest_1_.mine), channel_id=1, source_target_pairs={{8,0},{16,24},{9,1},{17,25},{10,2},{18,26},{11,3},{19,27},{12,4},{... | collective-permute-start | bytes 1769480 | tf_op jit(solution)/shard_map/ppermute | solution.py:383
  164.5 2.1 %collective-permute-start.28 = (bf16[2,96,1536]{2,1,0:T(8,128)(2,1)S(1)}, bf16[2,96,1536]{2,1,0:T(8,128)(2,1)S(1)}, u32[]{:S(2)}, u32[]{:S(2)}) collective-permute-start(bf16[2,96,1536]{2,1,0:T(8,128)(2,1)S(1)} %get-tuple-element.195), channel_id=1, source_target_pairs={{0,1},{1,0},{2,3},{3,2},{4,5},{5,4},{6,7},{7,6},{8,9},{9,8},{10,11... | collective-permute-start | bytes 1769480 | tf_op jit(solution)/shard_map/ppermute | solution.py:411
  166.6 11.0 %copy-start.1 = (s32[4]{0:T(128)S(1)}, s32[4]{0:T(128)}, u32[]{:S(2)}) copy-start(s32[4]{0:T(128)} %param.11) | copy-start | bytes 52
  166.8 7.5 %collective-permute-start.29 = (bf16[2,24,1536]{2,1,0:T(8,128)(2,1)S(1)}, bf16[2,24,1536]{2,1,0:T(8,128)(2,1)S(1)}, u32[]{:S(2)}, u32[]{:S(2)}) collective-permute-start(bf16[2,24,1536]{2,1,0:T(8,128)(2,1)S(1)} %get-tuple-element.203), channel_id=1, source_target_pairs={{0,2},{1,3},{2,4},{3,5},{4,6},{5,7},{6,0},{7,1},{8,10},{9,11},{10,... | collective-permute-start | bytes 442376 | tf_op jit(solution)/shard_map/ppermute | solution.py:415
  169.3 7.6 %collective-permute-start.30 = (bf16[2,24,1536]{2,1,0:T(8,128)(2,1)S(1)}, bf16[2,24,1536]{2,1,0:T(8,128)(2,1)S(1)}, u32[]{:S(2)}, u32[]{:S(2)}) collective-permute-start(bf16[2,24,1536]{2,1,0:T(8,128)(2,1)S(1)} %get-tuple-element.205), channel_id=1, source_target_pairs={{0,4},{1,5},{2,6},{3,7},{4,0},{5,1},{6,2},{7,3},{8,12},{9,13},{10,... | collective-permute-start | bytes 442376 | tf_op jit(solution)/shard_map/ppermute | solution.py:415
  169.8 7.1 %collective-permute-start.31 = (bf16[2,24,1536]{2,1,0:T(8,128)(2,1)S(1)}, bf16[2,24,1536]{2,1,0:T(8,128)(2,1)S(1)}, u32[]{:S(2)}, u32[]{:S(2)}) collective-permute-start(bf16[2,24,1536]{2,1,0:T(8,128)(2,1)S(1)} %get-tuple-element.204), channel_id=1, source_target_pairs={{0,6},{1,7},{2,0},{3,1},{4,2},{5,3},{6,4},{7,5},{8,14},{9,15},{10,... | collective-permute-start | bytes 442376 | tf_op jit(solution)/shard_map/ppermute | solution.py:415

commit v5 on v4

--- a/solution.py
+++ b/solution.py
@@ -64,14 +64,17 @@
 
 
 def over_blocks(span, total, fetch, work):
-    base, end = span
+    base, end, ready, ahead = span
+    stop = min(end + ahead, total)
+    for i in range(base + ready, min(base + EARLY, stop)):
+        begin_all(fetch(i))
 
     def body(i, carry):
-        @pl.when(i + EARLY < total)
+        @pl.when(i + EARLY < stop)
         def _():
             begin_all(fetch(i + EARLY))
 
-        @pl.when(i >= base + EARLY)
+        @pl.when(i >= base + ready)
         def _():
             wait_all(fetch(i))
 
@@ -79,7 +82,7 @@
         return carry
 
     lax.fori_loop(base, end, body, 0)
-    for i in range(max(end, base + EARLY), min(end + EARLY, total)):
+    for i in range(max(end, base + ready), stop):
         wait_all(fetch(i))
 
 
@@ -171,7 +174,7 @@
         sums_in, rest = rest[0], rest[2:]
     b0, b1, b2, d_down, sums, extra = rest[:6]
     ddv, table, wsem, dsem = rest[-4:]
-    base, end = span
+    base, end = span[:2]
     field = fill_table(rows, base, head, table)
     edge = head[0, head.shape[1] - 1]
     fetch = lambda i: weight_copies(field, i, (wg, wu, wd), (b0, b1, b2), wsem)
@@ -297,7 +300,7 @@
 
 
 def block_table(plan, steps, experts):
-    rows, spans = [], {}
+    rows, spans, ready = [], {}, EARLY
     for name, k in steps:
         if name not in ("partial", "post"):
             continue
@@ -306,7 +309,9 @@
             ranks = [0] if group == 0 else list(range(1, experts))
             for rank in ranks:
                 rows.append((rank, unit, group, start, int(rank == ranks[0]), int(rank == ranks[-1])))
-        spans[name, k] = (base, len(rows))
+        ahead = EARLY if name == "post" and len(rows) - base > 1 else 1
+        spans[name, k] = (base, len(rows), ready, ahead)
+        ready = ahead
     return rows, spans
 
 

time: 178 us -> 180 us (1.011)
  starting transfers between devices: 56.1 us -> 58.1 us
    pallas_call x8, Pallas kernels: 32.6 us -> 30.1 us  [partial_products(): pl.pallas_call(functools.partial(partial_kernel, span, len(blocks), seen,...]
    pallas_call x8, Pallas kernels: 41.3 us -> 43.4 us  [post_products(): pl.pallas_call(functools.partial(post_kernel, span, len(blocks), seen, le...]
    ppermute x24, starting transfers between devices: 46.9 us -> 48.9 us  [send(): return lax.ppermute(v, 'section', pairs)]
where the time goes in v5:
time: 180 us; the launch traced here: 179 us
  Pallas kernels  80.9 us (45%)
  starting transfers between devices  58.1 us (32%)
  waiting for transfers between devices  30.6 us (17%)
  other arithmetic  5.7 us (3%)
  local copies, waits for them, and re-layouts  2.68 us (1%)
    ppermute x24, starting transfers between devices, send(): return lax.ppermute(v, 'section', pairs)  48.9 us
    pallas_call x8, Pallas kernels, post_products(): pl.pallas_call(functools.partial(post_kernel, span, len(blocks), seen, le...  43.4 us
    pallas_call x8, Pallas kernels, partial_products(): pl.pallas_call(functools.partial(partial_kernel, span, len(blocks), seen,...  30.1 us
    ppermute x24, waiting for transfers between devices, send(): return lax.ppermute(v, 'section', pairs)  20.7 us
    ppermute x3, waiting for transfers between devices, on_device(): lax.ppermute(piece, 'tensor', [(i, (i + 2 * n) % parts) for i in range(pa...  6.02 us
    ppermute x3, starting transfers between devices, on_device(): lax.ppermute(pair, 'tensor', [(i, (i - 2 * n) % parts) for i in range(par...  5.04 us
    ppermute x3, starting transfers between devices, on_device(): lax.ppermute(piece, 'tensor', [(i, (i + 2 * n) % parts) for i in range(pa...  3.98 us
    pallas_call x1, Pallas kernels, preload(): pl.pallas_call(functools.partial(preload_kernel, blocks[:EARLY]), in_spec...  3.94 us
  transfers between devices with their start and end apart: 32, of which 8 were waited for; matrix products, arithmetic and copies ran while one was open for 3% of the time, Pallas kernels for 43%

profile of v5, /device:TPU:0, one launch (start us, length us, event | category | flops | bytes accessed | tf_op | source)
XLA Modules:
  0.0 179.5 jit_solution(10812543260272553197)
XLA Ops:
  0.6 0.9 pad_maximum_fusion.2
  1.6 3.9 %collective-permute-start = (bf16[2,24,1536]{2,1,0:T(8,128)(2,1)S(1)}, bf16[2,24,1536]{2,1,0:T(8,128)(2,1)S(1)}, u32[]{:S(2)}, u32[]{:S(2)}) collective-permute-start(bf16[2,24,1536]{2,1,0:T(8,128)(2,1)S(1)} %get-tuple-element.210), channel_id=1, source_target_pairs={{0,6},{1,7},{2,0},{3,1},{4,2},{5,3},{6,4},{7,5},{8,14},{9,15},{10,... | collective-permute-start | bytes 442376 | tf_op jit(solution)/shard_map/ppermute | solution.py:345
  5.5 0.5 collective-permute-start.1
  6.0 0.6 collective-permute-start.2
  6.6 0.8 reshape.78
  7.6 0.8 reshape.80
  8.6 0.7 iota_reduce_fusion
  9.3 0.7 select_bitcast_fusion.1
  10.2 0.7 compare_select_fusion.1.head
  10.9 3.9 %preload.1 = (bf16[3,1536,512]{2,1,0:T(8,128)(2,1)S(1)}, bf16[3,1536,512]{2,1,0:T(8,128)(2,1)S(1)}, bf16[3,512,1536]{2,1,0:T(8,128)(2,1)S(1)}) custom-call(s32[1,128]{1,0:T(1,128)S(1)} %compare_select_fusion.1.head, bf16[4,1536,2048]{2,1,0:T(8,128)(2,1)} %wg.33, bf16[4,1536,2048]{2,1,0:T(8,128)(2,1)} %wu.33, bf16[4,2048,1536]{2,1,0:T(8,128)(2,1)} %wd.33), custom_call_target="tpu_custom_call" | custom-call | bytes 37748736 | tf_op jit(solution)/shard_map/preload/pallas_call | solution.py:136
  15.2 1.9 %collective-permute-done.3 = bf16[2,96,1536]{2,1,0:T(8,128)(2,1)S(1)} collective-permute-done((bf16[2,96,1536]{2,1,0:T(8,128)(2,1)S(1)}, bf16[2,96,1536]{2,1,0:T(8,128)(2,1)S(1)}, u32[]{:S(2)}, u32[]{:S(2)}) %collective-permute-start.3) | collective-permute-done | bytes 589856 | tf_op jit(solution)/shard_map/ppermute | solution.py:349
  17.5 1.4 partial.8
  18.9 3.5 %collective-permute-start.5 = (bf16[1,3,192,512]{3,2,1,0:T(8,128)(2,1)S(1)}, bf16[1,3,192,512]{3,2,1,0:T(8,128)(2,1)S(1)}, u32[]{:S(2)}, u32[]{:S(2)}) collective-permute-start(bf16[1,3,192,512]{3,2,1,0:T(8,128)(2,1)S(1)} %get-tuple-element.116), channel_id=1, source_target_pairs={{0,8},{24,16},{1,9},{25,17},{2,10},{26,18},{3,11},{27,19},{4,12},{... | collective-permute-start | bytes 1769480 | tf_op jit(solution)/shard_map/ppermute | solution.py:388
  22.5 5.6 %partial.9 = (bf16[3,1536,512]{2,1,0:T(8,128)(2,1)S(1)}, bf16[3,1536,512]{2,1,0:T(8,128)(2,1)S(1)}, bf16[3,512,1536]{2,1,0:T(8,128)(2,1)S(1)}, f32[1,3,192,512]{...) custom-call(s32[1,128]{1,0:T(1,128)S(1)} %compare_select_fusion.1.he, ...), custom_call_target="tpu_custom_call", output_to_operand_aliasing={{0}: (8, {}), {1}: (9, {}), {2}: (10, {})} | custom-call | flops 10871635968 | bytes 56623104 | tf_op jit(solution)/shard_map/partial/pallas_call | solution.py:157
  28.0 5.6 %partial.10 = (bf16[3,1536,512]{2,1,0:T(8,128)(2,1)S(1)}, bf16[3,1536,512]{2,1,0:T(8,128)(2,1)S(1)}, bf16[3,512,1536]{2,1,0:T(8,128)(2,1)S(1)}, f32[1,3,192,512]...) custom-call(s32[1,128]{1,0:T(1,128)S(1)} %compare_select_fusion.1.he, ...), custom_call_target="tpu_custom_call", output_to_operand_aliasing={{0}: (8, {}), {1}: (9, {}), {2}: (10, {})} | custom-call | flops 10871635968 | bytes 56623104 | tf_op jit(solution)/shard_map/partial/pallas_call | solution.py:157
  33.6 1.3 collective-permute-start.4
  35.0 1.3 collective-permute-start.10
  36.5 0.7 collective-permute-start.7
  37.2 5.6 %partial.11 = (bf16[3,1536,512]{2,1,0:T(8,128)(2,1)S(1)}, bf16[3,1536,512]{2,1,0:T(8,128)(2,1)S(1)}, bf16[3,512,1536]{2,1,0:T(8,128)(2,1)S(1)}, f32[1,3,192,512]...) custom-call(s32[1,128]{1,0:T(1,128)S(1)} %compare_select_fusion.1.he, ...), custom_call_target="tpu_custom_call", output_to_operand_aliasing={{0}: (9, {}), {1}: (10, {}), {2}: (11, {})} | custom-call | flops 10871635968 | bytes 56623104 | tf_op jit(solution)/shard_map/partial/pallas_call | solution.py:157
  42.8 5.8 %collective-permute-done.4.first = bf16[1,3,192,512]{3,2,1,0:T(8,128)(2,1)S(1)} collective-permute-done((bf16[1,3,192,512]{3,2,1,0:T(8,128)(2,1)S(1)}, bf16[1,3,192,512]{3,2,1,0:T(8,128)(2,1)S(1)}, u32[]{:S(2)}, u32[]{:S(2)}) %collective-permute-start.4) | collective-permute-done | bytes 589856 | tf_op jit(solution)/shard_map/ppermute | solution.py:388
  48.8 0.7 collective-permute-start.6
  49.5 7.2 %collective-permute-start.11 = (bf16[1,3,192,512]{3,2,1,0:T(8,128)(2,1)S(1)}, bf16[1,3,192,512]{3,2,1,0:T(8,128)(2,1)S(1)}, u32[]{:S(2)}, u32[]{:S(2)}) collective-permute-start(bf16[1,3,192,512]{3,2,1,0:T(8,128)(2,1)S(1)} %get-tuple-element.136), channel_id=1, source_target_pairs={{0,8},{24,16},{1,9},{25,17},{2,10},{26,18},{3,11},{27,19},{4,12},{... | collective-permute-start | bytes 1769480 | tf_op jit(solution)/shard_map/ppermute | solution.py:388
  57.2 1.3 collective-permute-start.9
  58.5 5.6 %partial.12 = (bf16[3,1536,512]{2,1,0:T(8,128)(2,1)S(1)}, bf16[3,1536,512]{2,1,0:T(8,128)(2,1)S(1)}, bf16[3,512,1536]{2,1,0:T(8,128)(2,1)S(1)}, f32[1,3,192,512]...) custom-call(s32[1,128]{1,0:T(1,128)S(1)} %compare_select_fusion.1.he, ...), custom_call_target="tpu_custom_call", output_to_operand_aliasing={{0}: (10, {}), {1}: (11, {}), {2}: (12, {})} | custom-call | flops 10871635968 | bytes 56623104 | tf_op jit(solution)/shard_map/partial/pallas_call | solution.py:157
  64.3 0.7 collective-permute-start.12
  65.5 1.3 collective-permute-start.8
  66.8 6.3 %collective-permute-start.13 = (bf16[1,3,192,512]{3,2,1,0:T(8,128)(2,1)S(1)}, bf16[1,3,192,512]{3,2,1,0:T(8,128)(2,1)S(1)}, u32[]{:S(2)}, u32[]{:S(2)}) collective-permute-start(bf16[1,3,192,512]{3,2,1,0:T(8,128)(2,1)S(1)} %get-tuple-element.144), channel_id=1, source_target_pairs={{0,8},{24,16},{1,9},{25,17},{2,10},{26,18},{3,11},{27,19},{4,12},{... | collective-permute-start | bytes 1769480 | tf_op jit(solution)/shard_map/ppermute | solution.py:388
  73.1 2.5 %partial.13 = (bf16[3,1536,512]{2,1,0:T(8,128)(2,1)S(1)}, bf16[3,1536,512]{2,1,0:T(8,128)(2,1)S(1)}, bf16[3,512,1536]{2,1,0:T(8,128)(2,1)S(1)}, f32[1,3,192,512]...) custom-call(s32[1,128]{1,0:T(1,128)S(1)} %compare_select_fusion.1.he, ...), custom_call_target="tpu_custom_call", output_to_operand_aliasing={{0}: (10, {}), {1}: (11, {}), {2}: (12, {})} | custom-call | flops 3623878656 | bytes 18874368 | tf_op jit(solution)/shard_map/partial/pallas_call | solution.py:157
  75.6 1.3 collective-permute-start.15
  76.9 3.2 %post.8 = (bf16[3,1536,512]{2,1,0:T(8,128)(2,1)S(1)}, bf16[3,1536,512]{2,1,0:T(8,128)(2,1)S(1)}, bf16[3,512,1536]{2,1,0:T(8,128)(2,1)S(1)}, bf16[4,2048,1536]{2,...) custom-call(s32[1,128]{1,0:T(1,128)S(1)} %compare_select_fusion.1.he, ...), custom_call_target="tpu_custom_call", output_to_operand_aliasing={{0}: (10, {}), {1}: (11, {}), {2}: (12, {})} | custom-call | flops 4831838208 | bytes 18874368 | tf_op jit(solution)/shard_map/post/pallas_call | solution.py:243
  80.3 0.7 collective-permute-start.14
  81.1 0.4 finish.10.rest_2_.mine
  81.5 1.5 collective-permute-start.18
  83.0 3.9 %collective-permute-done.8.came = bf16[1,3,192,512]{3,2,1,0:T(8,128)(2,1)S(1)} collective-permute-done((bf16[1,3,192,512]{3,2,1,0:T(8,128)(2,1)S(1)}, bf16[1,3,192,512]{3,2,1,0:T(8,128)(2,1)S(1)}, u32[]{:S(2)}, u32[]{:S(2)}) %collective-permute-start.8) | collective-permute-done | bytes 589856 | tf_op jit(solution)/shard_map/ppermute | solution.py:388
  86.8 8.7 %post.9 = (bf16[3,1536,512]{2,1,0:T(8,128)(2,1)S(1)}, bf16[3,1536,512]{2,1,0:T(8,128)(2,1)S(1)}, bf16[3,512,1536]{2,1,0:T(8,128)(2,1)S(1)}, bf16[4,2048,1536]{2,...) custom-call(s32[1,128]{1,0:T(1,128)S(1)} %compare_select_fusion.1.he, ...), custom_call_target="tpu_custom_call", output_to_operand_aliasing={{0}: (12, {}), {1}: (13, {}), {2}: (14, {}), {3}: (16, {}),... | custom-call | flops 14495514624 | bytes 56623104 | tf_op jit(solution)/shard_map/post/pallas_call | solution.py:243
  95.7 0.7 collective-permute-start.19
  96.9 1.3 collective-permute-start.17
  98.2 1.4 partial.14
  99.6 4.6 %collective-permute-start.21 = (bf16[1,3,192,512]{3,2,1,0:T(8,128)(2,1)S(1)}, bf16[1,3,192,512]{3,2,1,0:T(8,128)(2,1)S(1)}, u32[]{:S(2)}, u32[]{:S(2)}) collective-permute-start(bf16[1,3,192,512]{3,2,1,0:T(8,128)(2,1)S(1)} %get-tuple-element.164), channel_id=1, source_target_pairs={{0,8},{24,16},{1,9},{25,17},{2,10},{26,18},{3,11},{27,19},{4,12},{... | collective-permute-start | bytes 1769480 | tf_op jit(solution)/shard_map/ppermute | solution.py:388
  104.4 0.7 collective-permute-start.20
  105.1 2.6 %partial.15 = (bf16[3,1536,512]{2,1,0:T(8,128)(2,1)S(1)}, bf16[3,1536,512]{2,1,0:T(8,128)(2,1)S(1)}, bf16[3,512,1536]{2,1,0:T(8,128)(2,1)S(1)}, f32[1,3,192,512]...) custom-call(s32[1,128]{1,0:T(1,128)S(1)} %compare_select_fusion.1.he, ...), custom_call_target="tpu_custom_call", output_to_operand_aliasing={{0}: (9, {}), {1}: (10, {}), {2}: (11, {})} | custom-call | flops 3623878656 | bytes 18874368 | tf_op jit(solution)/shard_map/partial/pallas_call | solution.py:157
  107.7 0.4 finish.12.rest_1_.mine
  108.2 1.3 collective-permute-start.23
  109.5 8.6 %post.10 = (bf16[3,1536,512]{2,1,0:T(8,128)(2,1)S(1)}, bf16[3,1536,512]{2,1,0:T(8,128)(2,1)S(1)}, bf16[3,512,1536]{2,1,0:T(8,128)(2,1)S(1)}, bf16[4,2048,1536]{2...) custom-call(s32[1,128]{1,0:T(1,128)S(1)} %compare_select_fusion.1.he, ...), custom_call_target="tpu_custom_call", output_to_operand_aliasing={{0}: (11, {}), {1}: (12, {}), {2}: (13, {}), {3}: (15, {}),... | custom-call | flops 14495514624 | bytes 56623104 | tf_op jit(solution)/shard_map/post/pallas_call | solution.py:243
  118.1 7.0 %collective-permute-start.16 = (bf16[1,3,192,512]{3,2,1,0:T(8,128)(2,1)S(1)}, bf16[1,3,192,512]{3,2,1,0:T(8,128)(2,1)S(1)}, u32[]{:S(2)}, u32[]{:S(2)}) collective-permute-start(bf16[1,3,192,512]{3,2,1,0:T(8,128)(2,1)S(1)} %get-tuple-element.155), channel_id=1, source_target_pairs={{0,8},{24,16},{1,9},{25,17},{2,10},{26,18},{3,11},{27,19},{4,12},{... | collective-permute-start | bytes 1769480 | tf_op jit(solution)/shard_map/ppermute | solution.py:388
  125.3 0.7 collective-permute-start.24
  126.5 1.3 collective-permute-start.27
  127.8 7.6 %post.11 = (bf16[3,1536,512]{2,1,0:T(8,128)(2,1)S(1)}, bf16[3,1536,512]{2,1,0:T(8,128)(2,1)S(1)}, bf16[3,512,1536]{2,1,0:T(8,128)(2,1)S(1)}, bf16[4,2048,1536]{2...) custom-call(s32[1,128]{1,0:T(1,128)S(1)} %compare_select_fusion.1.he, ...), custom_call_target="tpu_custom_call", output_to_operand_aliasing={{0}: (12, {}), {1}: (13, {}), {2}: (14, {}), {3}: (16, {}),... | custom-call | flops 14495514624 | bytes 56623104 | tf_op jit(solution)/shard_map/post/pallas_call | solution.py:243
  135.7 0.7 collective-permute-start.22
  136.8 1.3 collective-permute-start.26
  138.1 7.6 %post.12 = (bf16[3,1536,512]{2,1,0:T(8,128)(2,1)S(1)}, bf16[3,1536,512]{2,1,0:T(8,128)(2,1)S(1)}, bf16[3,512,1536]{2,1,0:T(8,128)(2,1)S(1)}, bf16[4,2048,1536]{2...) custom-call(s32[1,128]{1,0:T(1,128)S(1)} %compare_select_fusion.1.he, ...), custom_call_target="tpu_custom_call", output_to_operand_aliasing={{0}: (12, {}), {1}: (13, {}), {2}: (14, {}), {3}: (16, {}),... | custom-call | flops 14495514624 | bytes 56623104 | tf_op jit(solution)/shard_map/post/pallas_call | solution.py:243
  146.2 1.5 collective-permute-start.25
  147.7 2.3 %post.13 = (bf16[3,1536,512]{2,1,0:T(8,128)(2,1)S(1)}, bf16[3,1536,512]{2,1,0:T(8,128)(2,1)S(1)}, bf16[3,512,1536]{2,1,0:T(8,128)(2,1)S(1)}, bf16[4,2048,1536]{2...) custom-call(s32[1,128]{1,0:T(1,128)S(1)} %compare_select_fusion.1.he, ...), custom_call_target="tpu_custom_call", output_to_operand_aliasing={{0}: (11, {}), {1}: (12, {}), {2}: (13, {}), {3}: (15, {}),... | custom-call | flops 4831838208 | bytes 18874368 | tf_op jit(solution)/shard_map/post/pallas_call | solution.py:243
  150.0 7.4 %collective-permute-done.26.came = bf16[1,3,192,512]{3,2,1,0:T(8,128)(2,1)S(1)} collective-permute-done((bf16[1,3,192,512]{3,2,1,0:T(8,128)(2,1)S(1)}, bf16[1,3,192,512]{3,2,1,0:T(8,128)(2,1)S(1)}, u32[]{:S(2)}, u32[]{:S(2)}) %collective-permute-start.26) | collective-permute-done | bytes 589856 | tf_op jit(solution)/shard_map/ppermute | solution.py:388
  157.5 3.1 %post.14 = (bf16[3,1536,512]{2,1,0:T(8,128)(2,1)S(1)}, bf16[3,1536,512]{2,1,0:T(8,128)(2,1)S(1)}, bf16[3,512,1536]{2,1,0:T(8,128)(2,1)S(1)}, bf16[4,2048,1536]{2...) custom-call(s32[1,128]{1,0:T(1,128)S(1)} %compare_select_fusion.1.he, ...), custom_call_target="tpu_custom_call", output_to_operand_aliasing={{0}: (10, {}), {1}: (11, {}), {2}: (12, {}), {3}: (14, {}),... | custom-call | flops 4831838208 | bytes 18874368 | tf_op jit(solution)/shard_map/post/pallas_call | solution.py:243
  160.5 3.5 %collective-permute-done.25.came = bf16[1,3,192,512]{3,2,1,0:T(8,128)(2,1)S(1)} collective-permute-done((bf16[1,3,192,512]{3,2,1,0:T(8,128)(2,1)S(1)}, bf16[1,3,192,512]{3,2,1,0:T(8,128)(2,1)S(1)}, u32[]{:S(2)}, u32[]{:S(2)}) %collective-permute-start.25) | collective-permute-done | bytes 589856 | tf_op jit(solution)/shard_map/ppermute | solution.py:388
  164.1 2.3 %post.15 = (bf16[3,1536,512]{2,1,0:T(8,128)(2,1)S(1)}, bf16[3,1536,512]{2,1,0:T(8,128)(2,1)S(1)}, bf16[3,512,1536]{2,1,0:T(8,128)(2,1)S(1)}, bf16[4,2048,1536]{2...) custom-call(s32[1,128]{1,0:T(1,128)S(1)} %compare_select_fusion.1.he, ...), custom_call_target="tpu_custom_call", output_to_operand_aliasing={{0}: (10, {}), {1}: (11, {}), {2}: (12, {}), {3}: (14, {})} | custom-call | flops 4831838208 | bytes 18874368 | tf_op jit(solution)/shard_map/post/pallas_call | solution.py:243
  166.5 2.0 %collective-permute-done.28 = bf16[2,96,1536]{2,1,0:T(8,128)(2,1)S(1)} collective-permute-done((bf16[2,96,1536]{2,1,0:T(8,128)(2,1)S(1)}, bf16[2,96,1536]{2,1,0:T(8,128)(2,1)S(1)}, u32[]{:S(2)}, u32[]{:S(2)}) %collective-permute-start.28) | collective-permute-done | bytes 589856 | tf_op jit(solution)/shard_map/ppermute | solution.py:416
  168.7 2.4 %collective-permute-start.29 = (bf16[2,24,1536]{2,1,0:T(8,128)(2,1)S(1)}, bf16[2,24,1536]{2,1,0:T(8,128)(2,1)S(1)}, u32[]{:S(2)}, u32[]{:S(2)}) collective-permute-start(bf16[2,24,1536]{2,1,0:T(8,128)(2,1)S(1)} %get-tuple-element.203), channel_id=1, source_target_pairs={{0,2},{1,3},{2,4},{3,5},{4,6},{5,7},{6,0},{7,1},{8,10},{9,11},{10,... | collective-permute-start | bytes 442376 | tf_op jit(solution)/shard_map/ppermute | solution.py:420
  171.2 0.5 collective-permute-start.30
  171.7 1.0 collective-permute-start.31
  172.7 3.6 %collective-permute-done.29 = bf16[2,24,1536]{2,1,0:T(8,128)(2,1)S(1)} collective-permute-done((bf16[2,24,1536]{2,1,0:T(8,128)(2,1)S(1)}, bf16[2,24,1536]{2,1,0:T(8,128)(2,1)S(1)}, u32[]{:S(2)}, u32[]{:S(2)}) %collective-permute-start.29) | collective-permute-done | bytes 147488 | tf_op jit(solution)/shard_map/ppermute | solution.py:420
  176.3 2.5 %collective-permute-done.30 = bf16[2,24,1536]{2,1,0:T(8,128)(2,1)S(1)} collective-permute-done((bf16[2,24,1536]{2,1,0:T(8,128)(2,1)S(1)}, bf16[2,24,1536]{2,1,0:T(8,128)(2,1)S(1)}, u32[]{:S(2)}, u32[]{:S(2)}) %collective-permute-start.30) | collective-permute-done | bytes 147488 | tf_op jit(solution)/shard_map/ppermute | solution.py:420
  178.8 0.7 slice_bitcast_fusion.2
  (79 shorter events, 6.0 us)
Async XLA Ops:
  0.6 8.0 %copy-start = (s32[4]{0:T(128)S(1)}, s32[4]{0:T(128)}, u32[]{:S(2)}) copy-start(s32[4]{0:T(128)} %param.11) | copy-start | bytes 52
  1.6 13.4 %collective-permute-start = (bf16[2,24,1536]{2,1,0:T(8,128)(2,1)S(1)}, bf16[2,24,1536]{2,1,0:T(8,128)(2,1)S(1)}, u32[]{:S(2)}, u32[]{:S(2)}) collective-permute-start(bf16[2,24,1536]{2,1,0:T(8,128)(2,1)S(1)} %get-tuple-element.210), channel_id=1, source_target_pairs={{0,6},{1,7},{2,0},{3,1},{4,2},{5,3},{6,4},{7,5},{8,14},{9,15},{10,... | collective-permute-start | bytes 442376 | tf_op jit(solution)/shard_map/ppermute | solution.py:345
  5.5 9.5 %collective-permute-start.1 = (bf16[2,24,1536]{2,1,0:T(8,128)(2,1)S(1)}, bf16[2,24,1536]{2,1,0:T(8,128)(2,1)S(1)}, u32[]{:S(2)}, u32[]{:S(2)}) collective-permute-start(bf16[2,24,1536]{2,1,0:T(8,128)(2,1)S(1)} %get-tuple-element.210), channel_id=1, source_target_pairs={{0,4},{1,5},{2,6},{3,7},{4,0},{5,1},{6,2},{7,3},{8,12},{9,13},{10,... | collective-permute-start | bytes 442376 | tf_op jit(solution)/shard_map/ppermute | solution.py:345
  6.0 9.0 %collective-permute-start.2 = (bf16[2,24,1536]{2,1,0:T(8,128)(2,1)S(1)}, bf16[2,24,1536]{2,1,0:T(8,128)(2,1)S(1)}, u32[]{:S(2)}, u32[]{:S(2)}) collective-permute-start(bf16[2,24,1536]{2,1,0:T(8,128)(2,1)S(1)} %get-tuple-element.210), channel_id=1, source_target_pairs={{0,2},{1,3},{2,4},{3,5},{4,6},{5,7},{6,0},{7,1},{8,10},{9,11},{10,... | collective-permute-start | bytes 442376 | tf_op jit(solution)/shard_map/ppermute | solution.py:345
  10.9 4.1 %copy-start.2 = (bf16[24,1536]{1,0:T(8,128)(2,1)S(1)}, bf16[24,1536]{1,0:T(8,128)(2,1)}, u32[]{:S(2)}) copy-start(bf16[24,1536]{1,0:T(8,128)(2,1)} %param.15) | copy-start | bytes 221188
  10.9 4.1 %copy-start.3 = (bf16[24,1536]{1,0:T(8,128)(2,1)S(1)}, bf16[24,1536]{1,0:T(8,128)(2,1)}, u32[]{:S(2)}) copy-start(bf16[24,1536]{1,0:T(8,128)(2,1)} %param.8) | copy-start | bytes 221188
  15.1 2.1 %collective-permute-start.3 = (bf16[2,96,1536]{2,1,0:T(8,128)(2,1)S(1)}, bf16[2,96,1536]{2,1,0:T(8,128)(2,1)S(1)}, u32[]{:S(2)}, u32[]{:S(2)}) collective-permute-start(bf16[2,96,1536]{2,1,0:T(8,128)(2,1)S(1)} %pad_maximum_fusion), channel_id=1, source_target_pairs={{0,1},{1,0},{2,3},{3,2},{4,5},{5,4},{6,7},{7,6},{8,9},{9,8},{10,11... | collective-permute-start | bytes 1769480 | tf_op jit(solution)/shard_map/ppermute | solution.py:349
  18.9 17.4 %collective-permute-start.5 = (bf16[1,3,192,512]{3,2,1,0:T(8,128)(2,1)S(1)}, bf16[1,3,192,512]{3,2,1,0:T(8,128)(2,1)S(1)}, u32[]{:S(2)}, u32[]{:S(2)}) collective-permute-start(bf16[1,3,192,512]{3,2,1,0:T(8,128)(2,1)S(1)} %get-tuple-element.116), channel_id=1, source_target_pairs={{0,8},{24,16},{1,9},{25,17},{2,10},{26,18},{3,11},{27,19},{4,12},{... | collective-permute-start | bytes 1769480 | tf_op jit(solution)/shard_map/ppermute | solution.py:388
  33.6 15.0 %collective-permute-start.4 = (bf16[1,3,192,512]{3,2,1,0:T(8,128)(2,1)S(1)}, bf16[1,3,192,512]{3,2,1,0:T(8,128)(2,1)S(1)}, u32[]{:S(2)}, u32[]{:S(2)}) collective-permute-start(bf16[1,3,192,512]{3,2,1,0:T(8,128)(2,1)S(1)} %get-tuple-element.109), channel_id=1, source_target_pairs={{0,8},{24,16},{1,9},{25,17},{2,10},{26,18},{3,11},{27,19},{4,12},{... | collective-permute-start | bytes 1769480 | tf_op jit(solution)/shard_map/ppermute | solution.py:388
  35.0 29.1 %collective-permute-start.10 = (bf16[1,3,192,512]{3,2,1,0:T(8,128)(2,1)S(1)}, bf16[1,3,192,512]{3,2,1,0:T(8,128)(2,1)S(1)}, u32[]{:S(2)}, u32[]{:S(2)}) collective-permute-start(bf16[1,3,192,512]{3,2,1,0:T(8,128)(2,1)S(1)} %get-tuple-element.126), channel_id=1, source_target_pairs={{0,8},{24,16},{1,9},{25,17},{2,10},{26,18},{3,11},{27,19},{4,12},{... | collective-permute-start | bytes 1769480 | tf_op jit(solution)/shard_map/ppermute | solution.py:388
  36.5 20.2 %collective-permute-start.7 = (bf16[1,3,192,512]{3,2,1,0:T(8,128)(2,1)S(1)}, bf16[1,3,192,512]{3,2,1,0:T(8,128)(2,1)S(1)}, u32[]{:S(2)}, u32[]{:S(2)}) collective-permute-start(bf16[1,3,192,512]{3,2,1,0:T(8,128)(2,1)S(1)} %add_convert_fusion.7.rest_1_), channel_id=1, source_target_pairs={{8,16},{16,8},{9,17},{17,9},{10,18},{18,10},{11,19},{19,11},{12,20... | collective-permute-start | bytes 1769480 | tf_op jit(solution)/shard_map/ppermute | solution.py:388
  48.8 16.2 %collective-permute-start.6 = (bf16[1,3,192,512]{3,2,1,0:T(8,128)(2,1)S(1)}, bf16[1,3,192,512]{3,2,1,0:T(8,128)(2,1)S(1)}, u32[]{:S(2)}, u32[]{:S(2)}) collective-permute-start(bf16[1,3,192,512]{3,2,1,0:T(8,128)(2,1)S(1)} %add_convert_fusion.6.rest_1_), channel_id=1, source_target_pairs={{8,16},{16,8},{9,17},{17,9},{10,18},{18,10},{11,19},{19,11},{12,20... | collective-permute-start | bytes 1769480 | tf_op jit(solution)/shard_map/ppermute | solution.py:388
  49.5 30.6 %collective-permute-start.11 = (bf16[1,3,192,512]{3,2,1,0:T(8,128)(2,1)S(1)}, bf16[1,3,192,512]{3,2,1,0:T(8,128)(2,1)S(1)}, u32[]{:S(2)}, u32[]{:S(2)}) collective-permute-start(bf16[1,3,192,512]{3,2,1,0:T(8,128)(2,1)S(1)} %get-tuple-element.136), channel_id=1, source_target_pairs={{0,8},{24,16},{1,9},{25,17},{2,10},{26,18},{3,11},{27,19},{4,12},{... | collective-permute-start | bytes 1769480 | tf_op jit(solution)/shard_map/ppermute | solution.py:388
  57.2 18.4 %collective-permute-start.9 = (bf16[1,3,192,512]{3,2,1,0:T(8,128)(2,1)S(1)}, bf16[1,3,192,512]{3,2,1,0:T(8,128)(2,1)S(1)}, u32[]{:S(2)}, u32[]{:S(2)}) collective-permute-start(bf16[1,3,192,512]{3,2,1,0:T(8,128)(2,1)S(1)} %finish.8.rest_2_.mine), channel_id=1, source_target_pairs={{8,0},{16,24},{9,1},{17,25},{10,2},{18,26},{11,3},{19,27},{12,4},{... | collective-permute-start | bytes 1769480 | tf_op jit(solution)/shard_map/ppermute | solution.py:388
  64.3 16.7 %collective-permute-start.12 = (bf16[1,3,192,512]{3,2,1,0:T(8,128)(2,1)S(1)}, bf16[1,3,192,512]{3,2,1,0:T(8,128)(2,1)S(1)}, u32[]{:S(2)}, u32[]{:S(2)}) collective-permute-start(bf16[1,3,192,512]{3,2,1,0:T(8,128)(2,1)S(1)} %add_convert_fusion.5.rest_1_), channel_id=1, source_target_pairs={{8,16},{16,8},{9,17},{17,9},{10,18},{18,10},{11,19},{19,11},{12,20... | collective-permute-start | bytes 1769480 | tf_op jit(solution)/shard_map/ppermute | solution.py:388
  65.5 21.4 %collective-permute-start.8 = (bf16[1,3,192,512]{3,2,1,0:T(8,128)(2,1)S(1)}, bf16[1,3,192,512]{3,2,1,0:T(8,128)(2,1)S(1)}, u32[]{:S(2)}, u32[]{:S(2)}) collective-permute-start(bf16[1,3,192,512]{3,2,1,0:T(8,128)(2,1)S(1)} %finish.9.rest_2_.mine), channel_id=1, source_target_pairs={{8,0},{16,24},{9,1},{17,25},{10,2},{18,26},{11,3},{19,27},{12,4},{... | collective-permute-start | bytes 1769480 | tf_op jit(solution)/shard_map/ppermute | solution.py:388
  66.8 28.8 %collective-permute-start.13 = (bf16[1,3,192,512]{3,2,1,0:T(8,128)(2,1)S(1)}, bf16[1,3,192,512]{3,2,1,0:T(8,128)(2,1)S(1)}, u32[]{:S(2)}, u32[]{:S(2)}) collective-permute-start(bf16[1,3,192,512]{3,2,1,0:T(8,128)(2,1)S(1)} %get-tuple-element.144), channel_id=1, source_target_pairs={{0,8},{24,16},{1,9},{25,17},{2,10},{26,18},{3,11},{27,19},{4,12},{... | collective-permute-start | bytes 1769480 | tf_op jit(solution)/shard_map/ppermute | solution.py:388
  75.6 28.6 %collective-permute-start.15 = (bf16[1,3,192,512]{3,2,1,0:T(8,128)(2,1)S(1)}, bf16[1,3,192,512]{3,2,1,0:T(8,128)(2,1)S(1)}, u32[]{:S(2)}, u32[]{:S(2)}) collective-permute-start(bf16[1,3,192,512]{3,2,1,0:T(8,128)(2,1)S(1)} %get-tuple-element.150), channel_id=1, source_target_pairs={{0,8},{24,16},{1,9},{25,17},{2,10},{26,18},{3,11},{27,19},{4,12},{... | collective-permute-start | bytes 1769480 | tf_op jit(solution)/shard_map/ppermute | solution.py:388
  80.3 16.1 %collective-permute-start.14 = (bf16[1,3,192,512]{3,2,1,0:T(8,128)(2,1)S(1)}, bf16[1,3,192,512]{3,2,1,0:T(8,128)(2,1)S(1)}, u32[]{:S(2)}, u32[]{:S(2)}) collective-permute-start(bf16[1,3,192,512]{3,2,1,0:T(8,128)(2,1)S(1)} %add_convert_fusion.4.rest_1_), channel_id=1, source_target_pairs={{8,16},{16,8},{9,17},{17,9},{10,18},{18,10},{11,19},{19,11},{12,20... | collective-permute-start | bytes 1769480 | tf_op jit(solution)/shard_map/ppermute | solution.py:388
  81.5 28.0 %collective-permute-start.18 = (bf16[1,3,192,512]{3,2,1,0:T(8,128)(2,1)S(1)}, bf16[1,3,192,512]{3,2,1,0:T(8,128)(2,1)S(1)}, u32[]{:S(2)}, u32[]{:S(2)}) collective-permute-start(bf16[1,3,192,512]{3,2,1,0:T(8,128)(2,1)S(1)} %finish.10.rest_2_.mine), channel_id=1, source_target_pairs={{8,0},{16,24},{9,1},{17,25},{10,2},{18,26},{11,3},{19,27},{12,4},{... | collective-permute-start | bytes 1769480 | tf_op jit(solution)/shard_map/ppermute | solution.py:388
  95.7 12.0 %collective-permute-start.19 = (bf16[1,3,192,512]{3,2,1,0:T(8,128)(2,1)S(1)}, bf16[1,3,192,512]{3,2,1,0:T(8,128)(2,1)S(1)}, u32[]{:S(2)}, u32[]{:S(2)}) collective-permute-start(bf16[1,3,192,512]{3,2,1,0:T(8,128)(2,1)S(1)} %add_convert_fusion.3.rest_1_), channel_id=1, source_target_pairs={{8,16},{16,8},{9,17},{17,9},{10,18},{18,10},{11,19},{19,11},{12,20... | collective-permute-start | bytes 1769480 | tf_op jit(solution)/shard_map/ppermute | solution.py:388
  96.9 30.9 %collective-permute-start.17 = (bf16[1,3,192,512]{3,2,1,0:T(8,128)(2,1)S(1)}, bf16[1,3,192,512]{3,2,1,0:T(8,128)(2,1)S(1)}, u32[]{:S(2)}, u32[]{:S(2)}) collective-permute-start(bf16[1,3,192,512]{3,2,1,0:T(8,128)(2,1)S(1)} %finish.11.rest_2_.mine), channel_id=1, source_target_pairs={{8,0},{16,24},{9,1},{17,25},{10,2},{18,26},{11,3},{19,27},{12,4},{... | collective-permute-start | bytes 1769480 | tf_op jit(solution)/shard_map/ppermute | solution.py:388
  99.6 25.5 %collective-permute-start.21 = (bf16[1,3,192,512]{3,2,1,0:T(8,128)(2,1)S(1)}, bf16[1,3,192,512]{3,2,1,0:T(8,128)(2,1)S(1)}, u32[]{:S(2)}, u32[]{:S(2)}) collective-permute-start(bf16[1,3,192,512]{3,2,1,0:T(8,128)(2,1)S(1)} %get-tuple-element.164), channel_id=1, source_target_pairs={{0,8},{24,16},{1,9},{25,17},{2,10},{26,18},{3,11},{27,19},{4,12},{... | collective-permute-start | bytes 1769480 | tf_op jit(solution)/shard_map/ppermute | solution.py:388
  104.4 21.6 %collective-permute-start.20 = (bf16[1,3,192,512]{3,2,1,0:T(8,128)(2,1)S(1)}, bf16[1,3,192,512]{3,2,1,0:T(8,128)(2,1)S(1)}, u32[]{:S(2)}, u32[]{:S(2)}) collective-permute-start(bf16[1,3,192,512]{3,2,1,0:T(8,128)(2,1)S(1)} %add_convert_fusion.2.rest_1_), channel_id=1, source_target_pairs={{8,16},{16,8},{9,17},{17,9},{10,18},{18,10},{11,19},{19,11},{12,20... | collective-permute-start | bytes 1769480 | tf_op jit(solution)/shard_map/ppermute | solution.py:388
  108.2 29.9 %collective-permute-start.23 = (bf16[1,3,192,512]{3,2,1,0:T(8,128)(2,1)S(1)}, bf16[1,3,192,512]{3,2,1,0:T(8,128)(2,1)S(1)}, u32[]{:S(2)}, u32[]{:S(2)}) collective-permute-start(bf16[1,3,192,512]{3,2,1,0:T(8,128)(2,1)S(1)} %finish.12.rest_1_.mine), channel_id=1, source_target_pairs={{8,0},{16,24},{9,1},{17,25},{10,2},{18,26},{11,3},{19,27},{12,4},{... | collective-permute-start | bytes 1769480 | tf_op jit(solution)/shard_map/ppermute | solution.py:388
  118.1 17.3 %collective-permute-start.16 = (bf16[1,3,192,512]{3,2,1,0:T(8,128)(2,1)S(1)}, bf16[1,3,192,512]{3,2,1,0:T(8,128)(2,1)S(1)}, u32[]{:S(2)}, u32[]{:S(2)}) collective-permute-start(bf16[1,3,192,512]{3,2,1,0:T(8,128)(2,1)S(1)} %get-tuple-element.155), channel_id=1, source_target_pairs={{0,8},{24,16},{1,9},{25,17},{2,10},{26,18},{3,11},{27,19},{4,12},{... | collective-permute-start | bytes 1769480 | tf_op jit(solution)/shard_map/ppermute | solution.py:388
  125.3 11.1 %collective-permute-start.24 = (bf16[1,3,192,512]{3,2,1,0:T(8,128)(2,1)S(1)}, bf16[1,3,192,512]{3,2,1,0:T(8,128)(2,1)S(1)}, u32[]{:S(2)}, u32[]{:S(2)}) collective-permute-start(bf16[1,3,192,512]{3,2,1,0:T(8,128)(2,1)S(1)} %add_convert_fusion.1.rest_2_), channel_id=1, source_target_pairs={{8,16},{16,8},{9,17},{17,9},{10,18},{18,10},{11,19},{19,11},{12,20... | collective-permute-start | bytes 1769480 | tf_op jit(solution)/shard_map/ppermute | solution.py:388
  126.5 21.2 %collective-permute-start.27 = (bf16[1,3,192,512]{3,2,1,0:T(8,128)(2,1)S(1)}, bf16[1,3,192,512]{3,2,1,0:T(8,128)(2,1)S(1)}, u32[]{:S(2)}, u32[]{:S(2)}) collective-permute-start(bf16[1,3,192,512]{3,2,1,0:T(8,128)(2,1)S(1)} %finish.13.rest_1_.mine), channel_id=1, source_target_pairs={{8,0},{16,24},{9,1},{17,25},{10,2},{18,26},{11,3},{19,27},{12,4},{... | collective-permute-start | bytes 1769480 | tf_op jit(solution)/shard_map/ppermute | solution.py:388
  135.7 10.1 %collective-permute-start.22 = (bf16[1,3,192,512]{3,2,1,0:T(8,128)(2,1)S(1)}, bf16[1,3,192,512]{3,2,1,0:T(8,128)(2,1)S(1)}, u32[]{:S(2)}, u32[]{:S(2)}) collective-permute-start(bf16[1,3,192,512]{3,2,1,0:T(8,128)(2,1)S(1)} %add_convert_fusion.rest_1_), channel_id=1, source_target_pairs={{8,16},{16,8},{9,17},{17,9},{10,18},{18,10},{11,19},{19,11},{12,20... | collective-permute-start | bytes 1769480 | tf_op jit(solution)/shard_map/ppermute | solution.py:388
  136.8 20.6 %collective-permute-start.26 = (bf16[1,3,192,512]{3,2,1,0:T(8,128)(2,1)S(1)}, bf16[1,3,192,512]{3,2,1,0:T(8,128)(2,1)S(1)}, u32[]{:S(2)}, u32[]{:S(2)}) collective-permute-start(bf16[1,3,192,512]{3,2,1,0:T(8,128)(2,1)S(1)} %finish.14.rest_2_.mine), channel_id=1, source_target_pairs={{8,0},{16,24},{9,1},{17,25},{10,2},{18,26},{11,3},{19,27},{12,4},{... | collective-permute-start | bytes 1769480 | tf_op jit(solution)/shard_map/ppermute | solution.py:388
  146.2 17.9 %collective-permute-start.25 = (bf16[1,3,192,512]{3,2,1,0:T(8,128)(2,1)S(1)}, bf16[1,3,192,512]{3,2,1,0:T(8,128)(2,1)S(1)}, u32[]{:S(2)}, u32[]{:S(2)}) collective-permute-start(bf16[1,3,192,512]{3,2,1,0:T(8,128)(2,1)S(1)} %finish.15.rest_1_.mine), channel_id=1, source_target_pairs={{8,0},{16,24},{9,1},{17,25},{10,2},{18,26},{11,3},{19,27},{12,4},{... | collective-permute-start | bytes 1769480 | tf_op jit(solution)/shard_map/ppermute | solution.py:388
  166.4 2.1 %collective-permute-start.28 = (bf16[2,96,1536]{2,1,0:T(8,128)(2,1)S(1)}, bf16[2,96,1536]{2,1,0:T(8,128)(2,1)S(1)}, u32[]{:S(2)}, u32[]{:S(2)}) collective-permute-start(bf16[2,96,1536]{2,1,0:T(8,128)(2,1)S(1)} %get-tuple-element.195), channel_id=1, source_target_pairs={{0,1},{1,0},{2,3},{3,2},{4,5},{5,4},{6,7},{7,6},{8,9},{9,8},{10,11... | collective-permute-start | bytes 1769480 | tf_op jit(solution)/shard_map/ppermute | solution.py:416
  168.5 11.0 %copy-start.1 = (s32[4]{0:T(128)S(1)}, s32[4]{0:T(128)}, u32[]{:S(2)}) copy-start(s32[4]{0:T(128)} %param.11) | copy-start | bytes 52
  168.7 7.5 %collective-permute-start.29 = (bf16[2,24,1536]{2,1,0:T(8,128)(2,1)S(1)}, bf16[2,24,1536]{2,1,0:T(8,128)(2,1)S(1)}, u32[]{:S(2)}, u32[]{:S(2)}) collective-permute-start(bf16[2,24,1536]{2,1,0:T(8,128)(2,1)S(1)} %get-tuple-element.203), channel_id=1, source_target_pairs={{0,2},{1,3},{2,4},{3,5},{4,6},{5,7},{6,0},{7,1},{8,10},{9,11},{10,... | collective-permute-start | bytes 442376 | tf_op jit(solution)/shard_map/ppermute | solution.py:420
  171.2 7.6 %collective-permute-start.30 = (bf16[2,24,1536]{2,1,0:T(8,128)(2,1)S(1)}, bf16[2,24,1536]{2,1,0:T(8,128)(2,1)S(1)}, u32[]{:S(2)}, u32[]{:S(2)}) collective-permute-start(bf16[2,24,1536]{2,1,0:T(8,128)(2,1)S(1)} %get-tuple-element.205), channel_id=1, source_target_pairs={{0,4},{1,5},{2,6},{3,7},{4,0},{5,1},{6,2},{7,3},{8,12},{9,13},{10,... | collective-permute-start | bytes 442376 | tf_op jit(solution)/shard_map/ppermute | solution.py:420
  171.7 7.1 %collective-permute-start.31 = (bf16[2,24,1536]{2,1,0:T(8,128)(2,1)S(1)}, bf16[2,24,1536]{2,1,0:T(8,128)(2,1)S(1)}, u32[]{:S(2)}, u32[]{:S(2)}) collective-permute-start(bf16[2,24,1536]{2,1,0:T(8,128)(2,1)S(1)} %get-tuple-element.204), channel_id=1, source_target_pairs={{0,6},{1,7},{2,0},{3,1},{4,2},{5,3},{6,4},{7,5},{8,14},{9,15},{10,... | collective-permute-start | bytes 442376 | tf_op jit(solution)/shard_map/ppermute | solution.py:420
